TPU v7x, 32 devices: a whole 2x2x4 slice. The times are simulated.
32 devices in a mesh: mem: 2 (over x), tile: 16 (over z, y, core).
Axes of the slice: x: 2, y: 2, z: 4, core: 2. Of those that a mesh axis runs over, the one named last changes fastest.
Arguments:
- fields: float32 [256, 8, 8192], P('mem', None, 'tile')
- coefficients: float32 [6, 8192], P(None, 'tile'), may hold values from 0.04 to 0.16
- neighbours: int32 [6, 8192], P(None, 'tile'), may hold values from 0 to 8191, as said below
- obs_cell: int32 [32768], P('tile'), may hold values from 0 to 511
- obs_level: int32 [32768], P('tile'), may hold values from 0 to 7
- obs_value: float32 [32768], replicated, may hold values from -6 to 6
- obs_rinv: float32 [32768], replicated, may hold values from 2 to 32
- obs_index: int32 [8, 16, 128], P('mem', 'tile'), may hold values from 0 to 6143, as said below
- obs_weight: int32 [8, 16, 128], P('mem', 'tile'), may hold values from 0 to 3
Outputs:
- analysis: bfloat16 [256, 8, 8192], P('mem', None, 'tile')
Inputs may be any that keep to these rules, and one draw needn't show every extreme that they name: `neighbours`: each neighbour lies within 32 columns of its cell in the global column order, counted around the end of the order back to its start. `obs_index`: an entry indexes the observations of three consecutive tiles laid end to end: the tile before the block's tile, the block's own tile, and the tile after it, with wrap-around over tiles. `obs_weight`: level 0 marks a padding entry that carries no weight.
All inputs are finite; a program needn't handle non-finite values.
Results may differ from a plain program's by a relative error of at most 0.012.
Values may be sent and summed in bfloat16 or wider, within the bound.
No kernel may reach another device: no remote copies, remote signals or barrier semaphores. Data moves between devices by JAX's collectives and lax.ppermute only.
A program may use at most 64 MiB of HBM per device.

v0:
```python
import functools

import jax
import jax.numpy as jnp
from jax import lax
from jax.experimental import pallas as pl
from jax.experimental.pallas import tpu as pltpu
from jax.sharding import PartitionSpec as P

HALO = 32
NS_ITERS = 8
LANES = 128
F32 = jnp.float32
BF16 = jnp.bfloat16
VMEM_LIMIT = 48 * 1024 * 1024

NN = (((1,), (0,)), ((), ()))
NT = (((1,), (1,)), ((), ()))
TN = (((0,), (0,)), ((), ()))


def dot(a, b, dims=NN):
    return lax.dot_general(a, b, dims, preferred_element_type=F32)


def split2(x):
    high = x.astype(BF16)
    return high, (x - high.astype(F32)).astype(BF16)


def split3(x):
    high = x.astype(BF16)
    rest = x - high.astype(F32)
    middle = rest.astype(BF16)
    return high, middle, (rest - middle.astype(F32)).astype(BF16)


def iota(shape, dim):
    return lax.broadcasted_iota(jnp.int32, shape, dim)


def is_odd_tile():
    return lax.axis_index("tile") % 2 == 1


def message_rows(field_rows):
    names = ("coef_high", "coef_low", "offset", "list_high", "list_low")
    return {name: field_rows + 16 * place for place, name in enumerate(names)}


def pack_kernel(
    left_ref, right_ref, coef_ref, nbr_ref, index_ref, weight_ref, a_ref, b_ref, lists_ref, offset_ref, *, tiles
):
    columns = coef_ref.shape[1]
    half = left_ref.shape[0] // 2
    rows = message_rows(half)
    odd = is_odd_tile()
    total = columns * tiles
    lane = iota((half, LANES), 1)
    left = jnp.where(lane < 64, left_ref[:half, :], pltpu.roll(left_ref[half:, :], 64, axis=1))
    right = jnp.where(lane < 64, pltpu.roll(right_ref[:half, :], 64, axis=1), right_ref[half:, :])
    a_ref[:half, :] = jnp.where(odd, right, left).astype(BF16)
    b_ref[:half, :] = jnp.where(odd, left, right).astype(BF16)

    place = lax.axis_index("tile") * columns + iota((6, columns), 1)
    offset = nbr_ref[...] - place
    offset = jnp.where(offset > HALO, offset - total, offset)
    offset = jnp.where(offset < -HALO, offset + total, offset).astype(F32)
    offset_ref[...] = jnp.zeros_like(offset_ref)
    offset_ref[:6, :] = offset
    coef_high, coef_low = split2(coef_ref[...])
    blank = jnp.zeros((16 - 6, LANES), F32)
    for name, value in (
        ("coef_high", coef_high.astype(F32)),
        ("coef_low", coef_low.astype(F32)),
        ("offset", offset),
    ):
        first = jnp.concatenate([value[:, :LANES], blank], axis=0)
        last = jnp.concatenate([value[:, columns - LANES :], blank], axis=0)
        start = rows[name]
        a_ref[start : start + 16, :] = jnp.where(odd, last, first).astype(BF16)
        b_ref[start : start + 16, :] = jnp.where(odd, first, last).astype(BF16)

    blocks = index_ref.shape[0]
    blank = jnp.zeros((16 - blocks, LANES), F32)
    index = index_ref[:, 0, :]
    list_high = jnp.concatenate([(index // 64).astype(F32), blank], axis=0).astype(BF16)
    list_low = jnp.concatenate([(index % 64).astype(F32), blank], axis=0).astype(BF16)
    weight = jnp.concatenate([weight_ref[:, 0, :].astype(F32), blank], axis=0).astype(BF16)
    for ref in (a_ref, b_ref):
        ref[rows["list_high"] : rows["list_high"] + 16, :] = list_high
        ref[rows["list_low"] : rows["list_low"] + 16, :] = list_low
    lists_ref[0:16, :] = list_high
    lists_ref[16:32, :] = list_low
    lists_ref[32:48, :] = weight


def fill_band(coefs, offsets, high_ref, low_ref, row, lane):
    spot = iota((LANES + 2 * HALO, LANES), 0)
    own = iota((LANES + 2 * HALO, LANES), 1) + HALO
    band = jnp.where(spot == own, 1.0 - jnp.sum(coefs, axis=0, keepdims=True), 0.0)
    target = iota(offsets.shape, 1) + HALO + offsets.astype(jnp.int32)
    for j in range(6):
        band = band + jnp.where(spot == target[j : j + 1, :], coefs[j : j + 1, :], 0.0)
    high, low = split2(band)
    high_ref[row : row + LANES + 2 * HALO, lane : lane + LANES] = high
    low_ref[row : row + LANES + 2 * HALO, lane : lane + LANES] = low


def forecast_kernel(
    *refs,
    groups,
):
    field_refs = refs[:groups]
    (
    a_ref,
    b_ref,
    coef_ref,
    offset_ref,
    out_ref,
    low_halo,
    high_halo,
    u_high,
    u_low,
    first_high,
    first_low,
    second_high,
    second_low,
    ) = refs[groups:]
    levels, members, columns = out_ref.shape
    half = low_halo.shape[0]
    rows = message_rows(half)
    odd = is_odd_tile()

    def side(start, count):
        a = a_ref[start : start + count, :].astype(F32)
        b = b_ref[start : start + count, :].astype(F32)
        return jnp.where(odd, b, a), jnp.where(odd, a, b)

    low, high = side(0, half)
    low_halo[...] = low
    high_halo[...] = high
    for level in range(levels):
        top = level * members
        mid = top + members // 2
        for group, ref in enumerate(field_refs):
            lane = group * LANES
            own_high, own_low = split2(ref[pl.ds(level, members, stride=levels), :])
            u_high[top : top + members, LANES + lane : 2 * LANES + lane] = own_high
            u_low[top : top + members, lane : lane + LANES] = own_low
        low = low_halo[pl.ds(level, members // 2, stride=levels), :]
        u_high[top:mid, 0:LANES] = pltpu.roll(low, 64, axis=1).astype(BF16)
        u_high[mid : top + members, 0:LANES] = low.astype(BF16)
        high = high_halo[pl.ds(level, members // 2, stride=levels), :]
        u_high[top:mid, LANES + columns :] = high.astype(BF16)
        u_high[mid : top + members, LANES + columns :] = pltpu.roll(high, 64, axis=1).astype(BF16)

    def edges(name):
        low, high = side(rows[name], 16)
        return low[:8, :], high[:8, :]

    blank = jnp.zeros((2, columns), F32)
    own_coef = jnp.concatenate([coef_ref[...], blank], axis=0)
    coef_high = edges("coef_high")
    coef_low = edges("coef_low")
    offset = edges("offset")
    pad = jnp.zeros((8, LANES), F32)
    coef = jnp.concatenate(
        [coef_high[0] + coef_low[0], own_coef, coef_high[1] + coef_low[1], pad], axis=1
    )
    reach = jnp.concatenate([offset[0], offset_ref[...], offset[1], pad], axis=1)
    wide = coef.shape[1]
    moved_coef = pltpu.roll(coef, wide - (LANES - HALO), axis=1)
    moved_reach = pltpu.roll(reach, wide - (LANES - HALO), axis=1)
    for ref in (first_high, first_low, second_high, second_low):
        ref[...] = jnp.zeros_like(ref)
    for group in range(columns // LANES + 1):
        lane = group * LANES
        fill_band(
            moved_coef[:, lane : lane + LANES],
            moved_reach[:, lane : lane + LANES],
            first_high,
            first_low,
            lane + 64,
            lane,
        )
    for group in range(columns // LANES):
        lane = group * LANES
        fill_band(
            coef[:, LANES + lane : 2 * LANES + lane],
            reach[:, LANES + lane : 2 * LANES + lane],
            second_high,
            second_low,
            lane,
            lane,
        )
    for start in range(0, columns, 256):
        f_high = first_high[start : start + 512, start : start + 384]
        f_low = first_low[start : start + 512, start : start + 384]
        s_high = second_high[start : start + 384, start : start + 256]
        s_low = second_low[start : start + 384, start : start + 256]
        both = dot(f_high, s_high) + (dot(f_high, s_low) + dot(f_low, s_high))
        both_high, both_low = split2(both)
        own_from = max(start, LANES)
        own_to = min(start + 512, LANES + columns)
        window = u_high[:, start : start + 512]
        result = dot(window, both_high) + (
            dot(window, both_low)
            + dot(
                u_low[:, own_from - LANES : own_to - LANES],
                both_high[own_from - start : own_to - start, :],
            )
        )
        for level in range(levels):
            out_ref[level, :, start : start + 256] = result[
                level * members : (level + 1) * members, :
            ].astype(BF16)


def gather_lists(own_ref, other_refs, start, blocks):
    parts = [own_ref[start : start + 16, :].astype(F32)]
    parts += [ref[...].astype(F32) for ref in other_refs]
    return jnp.concatenate([part[b : b + 1, :] for part in parts for b in range(blocks)], axis=1)


def read_places(table_ref, slot):
    wide = slot.shape[1]
    valid = (slot >= 0) & (slot < 16 * LANES)
    slot = jnp.where(valid, slot, 0)
    one = jnp.where(iota((LANES, wide), 0) == slot % LANES, 1.0, 0.0).astype(BF16)
    found = dot(table_ref[...], one)
    pick = iota((16, wide), 0) == slot // LANES
    values = [
        jnp.sum(jnp.where(pick, found[16 * k : 16 * k + 16, :], 0.0), axis=0, keepdims=True)
        for k in range(3)
    ]
    column = (values[1] * 16.0 + values[2]).astype(jnp.int32)
    return values[0].astype(jnp.int32), jnp.where(valid, column, -1)


def make_table(cell_ref, level_ref, table):
    cell = cell_ref[...]
    table[0:16, :] = level_ref[...].astype(F32).astype(BF16)
    table[16:32, :] = (cell // 16).astype(F32).astype(BF16)
    table[32:48, :] = (cell % 16).astype(F32).astype(BF16)


def read_forecast(field, level, column, out_ref, lane):
    members = out_ref.shape[0]
    wide = level.shape[1]
    one = jnp.where(iota((field.shape[1], wide), 0) == column, 1.0, 0.0).astype(BF16)
    found = dot(field, one)
    total = jnp.zeros((members, wide), F32)
    for l in range(field.shape[0] // members):
        total = total + jnp.where(level == l, found[l * members : (l + 1) * members, :], 0.0)
    out_ref[:, lane : lane + wide] = total.astype(BF16)


def neighbour_kernel(field_ref, a_ref, b_ref, *refs, others, blocks):
    other_refs = refs[:others]
    cell_ref, level_ref, ra_ref, rb_ref, table = refs[others:]
    levels, members, columns = field_ref.shape
    half = a_ref.shape[0] - 80
    rows = message_rows(half)
    odd = is_odd_tile()
    obs = 16 * LANES
    make_table(cell_ref, level_ref, table)
    field = field_ref[...].reshape(levels * members, columns)
    for turn, (ref, out_ref) in enumerate(((a_ref, ra_ref), (b_ref, rb_ref))):
        base = 32 * turn
        high = gather_lists(ref, [r.at[base : base + 16, :] for r in other_refs], rows["list_high"], blocks)
        low = gather_lists(ref, [r.at[base + 16 : base + 32, :] for r in other_refs], rows["list_low"], blocks)
        index = (high * 64.0 + low).astype(jnp.int32)
        skip = jnp.where(odd, 0, 2 * obs) if turn == 0 else jnp.where(odd, 2 * obs, 0)
        level, column = read_places(table, index - skip)
        for lane in range(0, index.shape[1], 256):
            read_forecast(
                field, level[:, lane : lane + 256], column[:, lane : lane + 256], out_ref, lane
            )


def own_kernel(field_ref, lists_ref, *refs, others, blocks, tiles):
    other_refs = refs[:others]
    cell_ref, level_ref, value_ref, rinv_ref, r_ref, weight_ref, target_ref, table = refs[others:]
    levels, members, columns = field_ref.shape
    obs = 16 * LANES
    make_table(cell_ref, level_ref, table)
    field = field_ref[...].reshape(levels * members, columns)

    def gathered(place):
        return gather_lists(
            lists_ref,
            [r.at[64 + 16 * place : 80 + 16 * place, :] for r in other_refs],
            16 * place,
            blocks,
        )

    index = (gathered(0) * 64.0 + gathered(1)).astype(jnp.int32)
    weight = gathered(2)
    wide = index.shape[1]
    level, column = read_places(table, index - obs)
    for lane in range(0, wide, 256):
        read_forecast(field, level[:, lane : lane + 256], column[:, lane : lane + 256], r_ref, lane)

    tile = lax.axis_index("tile")
    starts = [((tile + tiles + shift) % tiles) * 16 for shift in (-1, 0, 1)]
    one = jnp.where(iota((LANES, wide), 0) == index % LANES, 1.0, 0.0).astype(BF16)
    pick = iota((48, wide), 0) == index // LANES

    def looked_up(ref):
        window = jnp.concatenate([ref[pl.ds(pl.multiple_of(s, 16), 16), :] for s in starts], axis=0)
        high, middle, low = [dot(piece, one) for piece in split3(window)]
        return jnp.sum(jnp.where(pick, (high + middle) + low, 0.0), axis=0, keepdims=True)

    weight_ref[...] = jnp.broadcast_to(looked_up(rinv_ref) * (weight / 3.0), weight_ref.shape)
    target_ref[...] = jnp.broadcast_to(looked_up(value_ref), target_ref.shape)


def doubled(high, low):
    top = jnp.concatenate([high, low], axis=1)
    bottom = jnp.concatenate([high, jnp.zeros_like(low)], axis=1)
    return jnp.concatenate([top, bottom], axis=0)


def product(left, right):
    both = dot(left, right)
    wide = both.shape[1] // 2
    return both[:, :wide] + both[:, wide:]


def joined(pair):
    return jnp.concatenate(pair, axis=1)


def weights_kernel(*refs, others):
    r_refs = refs[: others + 1]
    weight_ref, target_ref, out_ref, pert, weighted, gram_right, hat, inner, outer = refs[others + 1 :]
    members, wide = r_refs[0].shape
    blocks = wide // LANES
    share = blocks // (others + 1)
    ensemble = members * (others + 1)
    free = ensemble - 1.0

    parts = [r_refs[0][...].astype(F32)]
    for k in range(others):
        other = r_refs[k + 1][...].astype(F32)
        turn = ((k + 1) * share * LANES) % wide
        parts.append(jnp.concatenate([other[:, wide - turn :], other[:, : wide - turn]], axis=1))
    total = sum(jnp.sum(part, axis=0, keepdims=True) for part in parts)
    mean = total * (1.0 / ensemble)
    weight = weight_ref[0:1, :]
    for k, part in enumerate(parts):
        rounded = (part - mean).astype(BF16)
        pert[k * members : (k + 1) * members, :] = rounded
        weighted[k * members : (k + 1) * members, :] = (rounded.astype(F32) * weight).astype(BF16)
    departure = target_ref[0:1, :] - mean

    eye = iota((LANES, LANES), 0) == iota((LANES, LANES), 1)

    def spread(value):
        return jnp.where(eye, value, 0.0)

    scales, xs, zs = [], [], []
    for b in range(blocks):
        lanes = slice(b * LANES, (b + 1) * LANES)
        gram = dot(weighted[:, lanes], pert[:, lanes], TN)
        trace = jnp.sum(jnp.sum(spread(gram), axis=0, keepdims=True), axis=1, keepdims=True)
        scale = jnp.broadcast_to(1.0 / (free + trace), (1, LANES))
        gram = gram * scale
        x = free * scale
        right = doubled(*split2(gram))
        gram_right[b] = right
        m = 1.5 - 0.5 * x
        factor = spread(1.5 - 0.5 * x) - 0.5 * gram
        v = m * x
        inner_next = product(
            joined(split2(factor)), doubled(*split2(factor - spread(0.5 * x)))
        ) - spread(0.5 * v)
        inner[b] = inner_next
        x = m * v
        hat[b] = spread(x) + product(joined(split2(inner_next)), right)
        outer[b] = spread(jnp.full((1, LANES), -0.5, F32))
        scales.append(scale)
        xs.append(x)
        zs.append(m)

    def step(_, carry):
        xs, zs = carry
        next_xs, next_zs = [], []
        for b in range(blocks):
            x, z = xs[b], zs[b]
            m = 1.5 - 0.5 * x
            v = m * x
            factor = spread(jnp.full((1, LANES), 1.5, F32)) - 0.5 * hat[b]
            f_high, f_low = split2(factor)
            left = joined((f_high, f_low))
            inside = inner[b]
            i_high, i_low = split2(inside)
            o_high, o_low = split2(outer[b])
            right_high = joined((i_high, o_high))
            both = dot(left, jnp.concatenate([right_high, right_high], axis=0)) + dot(
                f_high, joined((i_low, o_low))
            )
            half = both[:, :LANES] - (0.5 * x) * inside
            outer[b] = both[:, LANES:] - (0.5 * z) * inside
            new = product(left, doubled(*split2(half))) - (0.5 * v) * inside
            inner[b] = new
            x = m * v
            hat[b] = spread(x) + product(joined(split2(new)), gram_right[b])
            next_xs.append(x)
            next_zs.append(m * z)
        return tuple(next_xs), tuple(next_zs)

    xs, zs = lax.fori_loop(1, NS_ITERS - 1, step, (tuple(xs), tuple(zs)))

    own = iota((members, ensemble), 0) == iota((members, ensemble), 1)
    for b in range(blocks):
        lanes = slice(b * LANES, (b + 1) * LANES)
        x, z, scale = xs[b], zs[b], scales[b]
        factor = spread(jnp.full((1, LANES), 1.5, F32)) - 0.5 * hat[b]
        last = product(joined(split2(factor)), doubled(*split2(outer[b]))) - (0.5 * z) * inner[b]
        z = (1.5 - 0.5 * x) * z
        last_high, last_low = split2(last)
        last_right = doubled(last_high, last_low)
        row = jnp.broadcast_to(departure[:, lanes], (8, LANES))
        for _ in range(2):
            moved = product(joined(split2(row)), last_right)
            row = z * row + product(joined(split2(moved)), gram_right[b])
        row = row * scale
        root = jnp.sqrt(free * scale)
        mine = pert[:members, lanes]
        core = dot(joined((mine, mine)), jnp.concatenate([last_high, last_low], axis=0))
        core = core * (root * scale)
        all_rows = joined(split2(jnp.concatenate([core, row, row], axis=0)))
        block = weighted[:, lanes]
        found = dot(all_rows, joined((block, block)), NT)
        diagonal = jnp.where(own, (root * z)[:, 0:1], 0.0)
        out_ref[b] = (found[:members, :] + found[members : members + 1, :] + diagonal).astype(BF16)


def update_kernel(*refs, others):
    field_refs = refs[: others + 1]
    weight_ref, out_ref, stage = refs[others + 1 :]
    levels, members, columns = field_refs[0].shape
    blocks = weight_ref.shape[0]
    width = columns // blocks
    per = LANES // width
    ensemble = members * (others + 1)
    first = lax.axis_index("mem") * (blocks // (others + 1))
    lane = iota((members, LANES), 1)
    for group in range(columns // LANES):
        lanes = slice(group * LANES, (group + 1) * LANES)
        left = jnp.concatenate(
            [weight_ref[(group * per + k + blocks - first) % blocks] for k in range(per)], axis=0
        )
        for level in range(levels):
            parts = [ref[level, :, lanes].astype(F32) for ref in field_refs]
            total = sum(jnp.sum(part, axis=0, keepdims=True) for part in parts)
            mean = total * (1.0 / ensemble)
            moved = jnp.concatenate([(part - mean).astype(BF16) for part in parts], axis=0)
            found = dot(left, moved)
            result = found[:members, :]
            for k in range(1, per):
                result = jnp.where(lane < k * width, result, found[k * members : (k + 1) * members, :])
            stage[group, pl.ds(level, members, stride=levels), :] = result + mean
        out_ref[:, :, lanes] = stage[group].reshape(members, levels, LANES).astype(BF16)


def vmem():
    return pl.BlockSpec(memory_space=pltpu.VMEM)


def group_spec(rows, group):
    return pl.BlockSpec((rows, LANES), lambda i: (0, group))


def call(kernel, outs, inputs, scratch=(), in_specs=None, flops=0):
    return pl.pallas_call(
        kernel,
        grid=(1,),
        out_shape=outs,
        in_specs=in_specs or [vmem()] * len(inputs),
        out_specs=[vmem()] * len(outs),
        scratch_shapes=list(scratch),
        compiler_params=pltpu.CompilerParams(vmem_limit_bytes=VMEM_LIMIT),
        cost_estimate=pl.CostEstimate(flops=flops, bytes_accessed=4 << 20, transcendentals=0),
    )(*inputs)


def shards(
    fields,
    coefficients,
    neighbours,
    obs_cell,
    obs_level,
    obs_value,
    obs_rinv,
    obs_index,
    obs_weight,
):
    tiles = lax.axis_size("tile")
    sharers = lax.axis_size("mem")
    others = sharers - 1
    members, levels, columns = fields.shape
    blocks = obs_index.shape[0]
    entries = blocks * sharers * LANES
    half = members * levels // 2
    message = jax.ShapeDtypeStruct((half + 80, LANES), BF16)
    even_pairs = []
    odd_pairs = []
    for i in range(0, tiles, 2):
        even_pairs += [(i, i + 1), (i + 1, i)]
        low, high = i + 1, (i + 2) % tiles
        odd_pairs += [(low, high), (high, low)]
    turns = [[((i + r) % sharers, i) for i in range(sharers)] for r in range(1, sharers)]

    flat = fields.reshape(members * levels, columns)
    groups = columns // LANES
    a, b, lists, offset = call(
        functools.partial(pack_kernel, tiles=tiles),
        [
            message,
            message,
            jax.ShapeDtypeStruct((48, LANES), BF16),
            jax.ShapeDtypeStruct((8, columns), F32),
        ],
        [flat, flat, coefficients, neighbours, obs_index, obs_weight],
        in_specs=[group_spec(members * levels, 0), group_spec(members * levels, groups - 1)]
        + [vmem()] * 4,
    )
    from_a = lax.ppermute(a, "tile", odd_pairs)
    from_b = lax.ppermute(b, "tile", even_pairs)
    passed = jnp.concatenate([from_a[half + 48 :], from_b[half + 48 :], lists], axis=0)
    passed = [lax.ppermute(passed, "mem", turn) for turn in turns]

    wide = columns + 2 * LANES
    mid = columns + LANES
    (forecast,) = call(
        functools.partial(forecast_kernel, groups=groups),
        [jax.ShapeDtypeStruct((levels, members, columns), BF16)],
        [flat] * groups + [from_a, from_b, coefficients, offset],
        [
            pltpu.VMEM((half, LANES), F32),
            pltpu.VMEM((half, LANES), F32),
            pltpu.VMEM((members * levels, wide), BF16),
            pltpu.VMEM((members * levels, columns), BF16),
            pltpu.VMEM((wide + LANES, mid), BF16),
            pltpu.VMEM((wide + LANES, mid), BF16),
            pltpu.VMEM((mid + LANES, columns), BF16),
            pltpu.VMEM((mid + LANES, columns), BF16),
        ],
        in_specs=[group_spec(members * levels, group) for group in range(groups)] + [vmem()] * 4,
        flops=4 << 30,
    )
    cell = obs_cell.reshape(16, LANES)
    level = obs_level.reshape(16, LANES)
    reading = jax.ShapeDtypeStruct((members, entries), BF16)
    table = pltpu.VMEM((48, LANES), BF16)
    to_a, to_b = call(
        functools.partial(neighbour_kernel, others=others, blocks=blocks),
        [reading, reading],
        [forecast, from_a, from_b, *passed, cell, level],
        [table],
        flops=2 << 30,
    )
    back_a = lax.ppermute(to_a, "tile", odd_pairs)
    back_b = lax.ppermute(to_b, "tile", even_pairs)
    vector = jax.ShapeDtypeStruct((8, entries), F32)
    own, weight, target = call(
        functools.partial(own_kernel, others=others, blocks=blocks, tiles=tiles),
        [reading, vector, vector],
        [
            forecast,
            lists,
            *passed,
            cell,
            level,
            obs_value.reshape(-1, LANES),
            obs_rinv.reshape(-1, LANES),
        ],
        [table],
        flops=2 << 30,
    )
    readings = own + back_a + back_b
    readings = [readings] + [lax.ppermute(readings, "mem", turn) for turn in turns]
    forecasts = [forecast] + [lax.ppermute(forecast, "mem", turn) for turn in turns]
    ensemble = members * sharers
    total = blocks * sharers
    square = pltpu.VMEM((total, LANES, LANES), F32)
    (weights,) = call(
        functools.partial(weights_kernel, others=others),
        [jax.ShapeDtypeStruct((total, members, ensemble), BF16)],
        [*readings, weight, target],
        [
            pltpu.VMEM((ensemble, entries), BF16),
            pltpu.VMEM((ensemble, entries), BF16),
            pltpu.VMEM((total, 2 * LANES, 2 * LANES), BF16),
            square,
            square,
            square,
        ],
        flops=8 << 30,
    )
    (analysis,) = call(
        functools.partial(update_kernel, others=others),
        [jax.ShapeDtypeStruct((members, levels, columns), BF16)],
        [*forecasts, weights],
        [pltpu.VMEM((columns // LANES, members * levels, LANES), F32)],
        flops=1 << 30,
    )
    return analysis


def solution(mesh):
    in_specs = (
        P("mem", None, "tile"),
        P(None, "tile"),
        P(None, "tile"),
        P("tile"),
        P("tile"),
        P(),
        P(),
        P("mem", "tile", None),
        P("mem", "tile", None),
    )
    out_specs = P("mem", None, "tile")
    return jax.shard_map(shards, mesh=mesh, in_specs=in_specs, out_specs=out_specs, check_vma=False)
```

profile of v0, /device:TPU:0, one launch (start us, length us, event | category | flops | bytes accessed | tf_op | source)
XLA Modules:
  0.0 62.5 jit_solution(4171959416494353474)
XLA Ops:
  0.0 0.0 copy-start
  0.0 1.6 %copy-done = f32[128,8,512]{2,1,0:T(8,128)S(1)} copy-done((f32[128,8,512]{2,1,0:T(8,128)S(1)}, f32[128,8,512]{2,1,0:T(8,128)}, u32[]{:S(2)}) %copy-start) | copy-done | bytes 2097176
  1.6 0.0 copy-start.1
  1.6 0.7 %copy-done.1 = s32[6,512]{1,0:T(8,128)S(1)} copy-done((s32[6,512]{1,0:T(8,128)S(1)}, s32[6,512]{1,0:T(8,128)}, u32[]{:S(2)}) %copy-start.1) | copy-done | bytes 12312
  2.3 0.0 copy-start.2
  2.3 0.7 %copy-done.2 = f32[6,512]{1,0:T(8,128)S(1)} copy-done((f32[6,512]{1,0:T(8,128)S(1)}, f32[6,512]{1,0:T(8,128)}, u32[]{:S(2)}) %copy-start.2) | copy-done | bytes 12312
  3.0 0.0 copy-start.3
  3.0 0.7 %copy-done.3 = s32[4,1,128]{2,1,0:T(1,128)S(1)} copy-done((s32[4,1,128]{2,1,0:T(1,128)S(1)}, s32[4,1,128]{2,1,0:T(1,128)}, u32[]{:S(2)}) %copy-start.3) | copy-done | bytes 2072
  3.7 0.0 copy-start.4
  3.7 0.7 %copy-done.4 = s32[4,1,128]{2,1,0:T(1,128)S(1)} copy-done((s32[4,1,128]{2,1,0:T(1,128)S(1)}, s32[4,1,128]{2,1,0:T(1,128)}, u32[]{:S(2)}) %copy-start.4) | copy-done | bytes 2072
  4.4 0.1 shard_map.91
  4.5 5.5 %collective-permute-start = (bf16[592,128]{1,0:T(8,128)(2,1)S(1)}, bf16[592,128]{1,0:T(8,128)(2,1)S(1)}, u32[]{:S(2)}, u32[]{:S(2)}) collective-permute-start(bf16[592,128]{1,0:T(8,128)(2,1)S(1)} %get-tuple-element.14), channel_id=1, source_target_pairs={{1,2},{2,1},{3,4},{4,3},{5,6},{6,5},{7,8},{8,7},{9,10},{10,9},{11,... | collective-permute-start | bytes 454664 | tf_op jit(solution)/shard_map/ppermute | solution.py:531
  10.1 0.0 collective-permute-start.1
  10.1 2.9 %collective-permute-done.refs_4_.a_ref = bf16[592,128]{1,0:T(8,128)(2,1)S(1)} collective-permute-done((bf16[592,128]{1,0:T(8,128)(2,1)S(1)}, bf16[592,128]{1,0:T(8,128)(2,1)S(1)}, u32[]{:S(2)}, u32[]{:S(2)}) %collective-permute-start) | collective-permute-done | bytes 151584 | tf_op jit(solution)/shard_map/ppermute | solution.py:531
  12.9 0.0 collective-permute-done.1.refs_5_.b_ref
  12.9 2.0 %collective-permute-start.3 = (bf16[112,128]{1,0:T(8,128)(2,1)S(1)}, bf16[112,128]{1,0:T(8,128)(2,1)S(1)}, u32[]{:S(2)}, u32[]{:S(2)}) collective-permute-start(bf16[112,128]{1,0:T(8,128)(2,1)S(1)} %pad_maximum_fusion), channel_id=1, source_target_pairs={{16,0},{0,16},{17,1},{1,17},{18,2},{2,18},{19,3},{3,19},{20,4},{4,... | collective-permute-start | bytes 86024 | tf_op jit(solution)/shard_map/ppermute | solution.py:534
  14.9 0.0 copy-start.7
  14.9 0.0 copy-start.8
  14.9 4.5 %shard_map.92.field_ref.refs_0_ = bf16[8,128,512]{2,1,0:T(8,128)(2,1)S(1)} custom-call(f32[1024,512]{1,0:T(8,128)S(1)} %bitcast.7, f32[1024,512]{1,0:T(8,128)S(1)} %bitcast.8, f32[1024,512]{1,0:T(8,128)S(1)} %bitcast.9, f32[1024,512]{1,0:T(8,128)S(1)} %bitcast.10, bf16[592,128]{1,0:T(8,128)(2,1)S(1)} %collective-permute-done.refs_4_.a_ref, ...), custom_call_target="tpu_custom_call" | custom-call | flops 4294967296 | bytes 4194304 | tf_op jit(solution)/shard_map/pallas_call | solution.py:478
  19.5 0.0 collective-permute-done.3.refs_0_
  19.5 0.0 copy-done.7
  19.5 0.0 copy-done.8
  19.5 0.0 copy-start.5
  19.5 0.0 copy-start.6
  19.5 2.9 %shard_map.94 = (bf16[128,1024]{1,0:T(8,128)(2,1)S(1)}, bf16[128,1024]{1,0:T(8,128)(2,1)S(1)}) custom-call(bf16[8,128,512]{2,1,0:T(8,128)(2,1)S(1)} %shard_map.92.field_ref.refs_0_, bf16[592,128]{1,0:T(8,128)(2,1)S(1)} %collective-permute-done.refs_4_.a_ref, bf16[592,128]{1,0:T(8,128)(2,1)S(1)} %collective-permute-done.1.refs_5_.b_ref, ...), custom_call_target="tpu_custom_call" | custom-call | flops 2147483648 | bytes 4194304 | tf_op jit(solution)/shard_map/pallas_call | solution.py:478
  22.4 3.8 %collective-permute-start.4 = (bf16[128,1024]{1,0:T(8,128)(2,1)S(1)}, bf16[128,1024]{1,0:T(8,128)(2,1)S(1)}, u32[]{:S(2)}, u32[]{:S(2)}) collective-permute-start(bf16[128,1024]{1,0:T(8,128)(2,1)S(1)} %get-tuple-element.19), channel_id=1, source_target_pairs={{1,2},{2,1},{3,4},{4,3},{5,6},{6,5},{7,8},{8,7},{9,10},{10,9},{11,... | collective-permute-start | bytes 786440 | tf_op jit(solution)/shard_map/ppermute | solution.py:566
  26.2 0.0 collective-permute-start.5
  26.2 0.0 copy-done.5
  26.2 0.0 copy-done.6
  26.2 1.8 %shard_map.93 = (bf16[128,1024]{1,0:T(8,128)(2,1)S(1)}, f32[8,1024]{1,0:T(8,128)S(1)}, f32[8,1024]{1,0:T(8,128)S(1)}) custom-call(bf16[8,128,512]{2,1,0:T(8,128)(2,1)S(1)} %shard_map.92.field_ref.refs_0_, bf16[48,128]{1,0:T(8,128)(2,1)S(1)} %get-tuple-element.17.lists_ref, bf16[112,128]{1,0:T(8,128)(2,1)S(1)} %collective-permute-done.3.refs_0_, ...), custom_call_target="tpu_custom_call" | custom-call | flops 2147483648 | bytes 4194304 | tf_op jit(solution)/shard_map/pallas_call | solution.py:478
  28.0 3.0 %collective-permute-done.4 = bf16[128,1024]{1,0:T(8,128)(2,1)S(1)} collective-permute-done((bf16[128,1024]{1,0:T(8,128)(2,1)S(1)}, bf16[128,1024]{1,0:T(8,128)(2,1)S(1)}, u32[]{:S(2)}, u32[]{:S(2)}) %collective-permute-start.4) | collective-permute-done | bytes 262176 | tf_op jit(solution)/shard_map/ppermute | solution.py:566
  31.0 0.0 collective-permute-done.5
  31.0 0.2 collective-permute-start.6
  31.2 1.9 %collective-permute-start.2 = (bf16[8,128,512]{2,1,0:T(8,128)(2,1)S(1)}, bf16[8,128,512]{2,1,0:T(8,128)(2,1)S(1)}, u32[]{:S(2)}, u32[]{:S(2)}) collective-permute-start(bf16[8,128,512]{2,1,0:T(8,128)(2,1)S(1)} %shard_map.92.field_ref.refs_0_), channel_id=1, source_target_pairs={{16,0},{0,16},{17,1},{1,17},{18,2},{2,18},{19,3},{3,19},{20,4},{4,... | collective-permute-start | bytes 3145736 | tf_op jit(solution)/shard_map/ppermute | solution.py:586
  33.1 7.2 %collective-permute-done.6.refs_1_ = bf16[128,1024]{1,0:T(8,128)(2,1)S(1)} collective-permute-done((bf16[128,1024]{1,0:T(8,128)(2,1)S(1)}, bf16[128,1024]{1,0:T(8,128)(2,1)S(1)}, u32[]{:S(2)}, u32[]{:S(2)}) %collective-permute-start.6) | collective-permute-done | bytes 262176 | tf_op jit(solution)/shard_map/ppermute | solution.py:585
  40.3 18.0 %shard_map.95.refs_2_ = bf16[8,128,256]{2,1,0:T(8,128)(2,1)S(1)} custom-call(bf16[128,1024]{1,0:T(8,128)(2,1)S(1)} %add_add_fusion.refs_0_, bf16[128,1024]{1,0:T(8,128)(2,1)S(1)} %collective-permute-done.6.refs_1_, f32[8,1024]{1,0:T(8,128)S(1)} %get-tuple-element.21.refs_2_, f32[8,1024]{1,0:T(8,128)S(1)} %get-tuple-element.22.refs_3_), custom_call_target="tpu_custom_call" | custom-call | flops 8589934592 | bytes 4194304 | tf_op jit(solution)/shard_map/pallas_call | solution.py:478
  58.3 1.6 %collective-permute-done.2.refs_1_ = bf16[8,128,512]{2,1,0:T(8,128)(2,1)S(1)} collective-permute-done((bf16[8,128,512]{2,1,0:T(8,128)(2,1)S(1)}, bf16[8,128,512]{2,1,0:T(8,128)(2,1)S(1)}, u32[]{:S(2)}, u32[]{:S(2)}) %collective-permute-start.2) | collective-permute-done | bytes 1048608 | tf_op jit(solution)/shard_map/ppermute | solution.py:586
  60.0 2.5 %shard_map.96 = bf16[128,8,512]{2,1,0:T(8,128)(2,1)} custom-call(bf16[8,128,512]{2,1,0:T(8,128)(2,1)S(1)} %shard_map.92.field_ref.refs_0_, bf16[8,128,512]{2,1,0:T(8,128)(2,1)S(1)} %collective-permute-done.2.refs_1_, bf16[8,128,256]{2,1,0:T(8,128)(2,1)S(1)} %shard_map.95.refs_2_), custom_call_target="tpu_custom_call" | custom-call | flops 1073741824 | bytes 4194304 | tf_op jit(solution)/shard_map/pallas_call | solution.py:478
  (4 shorter events, 0.1 us)
Async XLA Ops:
  0.0 1.6 %copy-start = (f32[128,8,512]{2,1,0:T(8,128)S(1)}, f32[128,8,512]{2,1,0:T(8,128)}, u32[]{:S(2)}) copy-start(f32[128,8,512]{2,1,0:T(8,128)} %param.9) | copy-start | bytes 6291460
  1.6 0.7 %copy-start.1 = (s32[6,512]{1,0:T(8,128)S(1)}, s32[6,512]{1,0:T(8,128)}, u32[]{:S(2)}) copy-start(s32[6,512]{1,0:T(8,128)} %nbr_ref.1) | copy-start | bytes 36868
  2.3 0.7 %copy-start.2 = (f32[6,512]{1,0:T(8,128)S(1)}, f32[6,512]{1,0:T(8,128)}, u32[]{:S(2)}) copy-start(f32[6,512]{1,0:T(8,128)} %refs_6_.1) | copy-start | bytes 36868
  3.0 0.7 %copy-start.3 = (s32[4,1,128]{2,1,0:T(1,128)S(1)}, s32[4,1,128]{2,1,0:T(1,128)}, u32[]{:S(2)}) copy-start(s32[4,1,128]{2,1,0:T(1,128)} %index_ref.1) | copy-start | bytes 6148
  3.7 0.7 %copy-start.4 = (s32[4,1,128]{2,1,0:T(1,128)S(1)}, s32[4,1,128]{2,1,0:T(1,128)}, u32[]{:S(2)}) copy-start(s32[4,1,128]{2,1,0:T(1,128)} %weight_ref.1) | copy-start | bytes 6148
  4.5 8.4 %collective-permute-start = (bf16[592,128]{1,0:T(8,128)(2,1)S(1)}, bf16[592,128]{1,0:T(8,128)(2,1)S(1)}, u32[]{:S(2)}, u32[]{:S(2)}) collective-permute-start(bf16[592,128]{1,0:T(8,128)(2,1)S(1)} %get-tuple-element.14), channel_id=1, source_target_pairs={{1,2},{2,1},{3,4},{4,3},{5,6},{6,5},{7,8},{8,7},{9,10},{10,9},{11,... | collective-permute-start | bytes 454664 | tf_op jit(solution)/shard_map/ppermute | solution.py:531
  10.1 2.9 %collective-permute-start.1 = (bf16[592,128]{1,0:T(8,128)(2,1)S(1)}, bf16[592,128]{1,0:T(8,128)(2,1)S(1)}, u32[]{:S(2)}, u32[]{:S(2)}) collective-permute-start(bf16[592,128]{1,0:T(8,128)(2,1)S(1)} %get-tuple-element.15), channel_id=1, source_target_pairs={{0,1},{1,0},{2,3},{3,2},{4,5},{5,4},{6,7},{7,6},{8,9},{9,8},{10,11... | collective-permute-start | bytes 454664 | tf_op jit(solution)/shard_map/ppermute | solution.py:532
  12.9 6.5 %collective-permute-start.3 = (bf16[112,128]{1,0:T(8,128)(2,1)S(1)}, bf16[112,128]{1,0:T(8,128)(2,1)S(1)}, u32[]{:S(2)}, u32[]{:S(2)}) collective-permute-start(bf16[112,128]{1,0:T(8,128)(2,1)S(1)} %pad_maximum_fusion), channel_id=1, source_target_pairs={{16,0},{0,16},{17,1},{1,17},{18,2},{2,18},{19,3},{3,19},{20,4},{4,... | collective-permute-start | bytes 86024 | tf_op jit(solution)/shard_map/ppermute | solution.py:534
  14.9 4.6 %copy-start.7 = (s32[2048]{0:T(1024)S(1)}, s32[2048]{0:T(1024)}, u32[]{:S(2)}) copy-start(s32[2048]{0:T(1024)} %param.12) | copy-start | bytes 24580
  14.9 4.6 %copy-start.8 = (s32[2048]{0:T(1024)S(1)}, s32[2048]{0:T(1024)}, u32[]{:S(2)}) copy-start(s32[2048]{0:T(1024)} %param.13) | copy-start | bytes 24580
  19.5 6.7 %copy-start.5 = (f32[32768]{0:T(1024)S(1)}, f32[32768]{0:T(1024)}, u32[]{:S(2)}) copy-start(f32[32768]{0:T(1024)} %param.14) | copy-start | bytes 393220
  19.5 6.7 %copy-start.6 = (f32[32768]{0:T(1024)S(1)}, f32[32768]{0:T(1024)}, u32[]{:S(2)}) copy-start(f32[32768]{0:T(1024)} %param.15) | copy-start | bytes 393220
  22.4 8.6 %collective-permute-start.4 = (bf16[128,1024]{1,0:T(8,128)(2,1)S(1)}, bf16[128,1024]{1,0:T(8,128)(2,1)S(1)}, u32[]{:S(2)}, u32[]{:S(2)}) collective-permute-start(bf16[128,1024]{1,0:T(8,128)(2,1)S(1)} %get-tuple-element.19), channel_id=1, source_target_pairs={{1,2},{2,1},{3,4},{4,3},{5,6},{6,5},{7,8},{8,7},{9,10},{10,9},{11,... | collective-permute-start | bytes 786440 | tf_op jit(solution)/shard_map/ppermute | solution.py:566
  26.2 4.8 %collective-permute-start.5 = (bf16[128,1024]{1,0:T(8,128)(2,1)S(1)}, bf16[128,1024]{1,0:T(8,128)(2,1)S(1)}, u32[]{:S(2)}, u32[]{:S(2)}) collective-permute-start(bf16[128,1024]{1,0:T(8,128)(2,1)S(1)} %get-tuple-element.20), channel_id=1, source_target_pairs={{0,1},{1,0},{2,3},{3,2},{4,5},{5,4},{6,7},{7,6},{8,9},{9,8},{10,11... | collective-permute-start | bytes 786440 | tf_op jit(solution)/shard_map/ppermute | solution.py:567
  31.0 9.3 %collective-permute-start.6 = (bf16[128,1024]{1,0:T(8,128)(2,1)S(1)}, bf16[128,1024]{1,0:T(8,128)(2,1)S(1)}, u32[]{:S(2)}, u32[]{:S(2)}) collective-permute-start(bf16[128,1024]{1,0:T(8,128)(2,1)S(1)} %add_add_fusion.refs_0_), channel_id=1, source_target_pairs={{16,0},{0,16},{17,1},{1,17},{18,2},{2,18},{19,3},{3,19},{20,4},{4,... | collective-permute-start | bytes 786440 | tf_op jit(solution)/shard_map/ppermute | solution.py:585
  31.2 28.8 %collective-permute-start.2 = (bf16[8,128,512]{2,1,0:T(8,128)(2,1)S(1)}, bf16[8,128,512]{2,1,0:T(8,128)(2,1)S(1)}, u32[]{:S(2)}, u32[]{:S(2)}) collective-permute-start(bf16[8,128,512]{2,1,0:T(8,128)(2,1)S(1)} %shard_map.92.field_ref.refs_0_), channel_id=1, source_target_pairs={{16,0},{0,16},{17,1},{1,17},{18,2},{2,18},{19,3},{3,19},{20,4},{4,... | collective-permute-start | bytes 3145736 | tf_op jit(solution)/shard_map/ppermute | solution.py:586
where the time goes:
time: 62.9 us; the launch traced here: 62.5 us
  Pallas kernels  29.9 us (48%)
  waiting for transfers between devices  14.7 us (23%)
  starting transfers between devices  13.4 us (21%)
  local copies, waits for them, and re-layouts  4.41 us (7%)
    pallas_call x6, Pallas kernels, call(): pl.pallas_call(kernel, grid=(1,), out_shape=outs, in_specs=in_specs or [v...  29.9 us
    ppermute x1, waiting for transfers between devices, shards(): lax.ppermute(readings, 'mem', turn)  7.22 us
    ppermute x1, starting transfers between devices, shards(): from_a = lax.ppermute(a, 'tile', odd_pairs)  5.51 us
    unnamed x18, local copies, waits for them, and re-layouts  4.41 us
    ppermute x1, starting transfers between devices, shards(): back_a = lax.ppermute(to_a, 'tile', odd_pairs)  3.78 us
    ppermute x1, waiting for transfers between devices, shards(): back_a = lax.ppermute(to_a, 'tile', odd_pairs)  2.99 us
    ppermute x1, waiting for transfers between devices, shards(): from_a = lax.ppermute(a, 'tile', odd_pairs)  2.87 us
    ppermute x1, starting transfers between devices, shards(): passed = [lax.ppermute(passed, 'mem', turn) for turn in turns]  2 us
  transfers between devices with their start and end apart: 7, of which 4 were waited for; matrix products, arithmetic and copies ran while one was open for 0% of the time, Pallas kernels for 39%

commit v1 on v0

v1 whole, which is shorter than its diff:
```python
import functools

import jax
import jax.numpy as jnp
from jax import lax
from jax.experimental import pallas as pl
from jax.experimental.pallas import tpu as pltpu
from jax.sharding import PartitionSpec as P

HALO = 32
NS_ITERS = 8
LANES = 128
F32 = jnp.float32
BF16 = jnp.bfloat16
VMEM_LIMIT = 48 * 1024 * 1024

NN = (((1,), (0,)), ((), ()))
NT = (((1,), (1,)), ((), ()))
TN = (((0,), (0,)), ((), ()))


def dot(a, b, dims=NN):
    return lax.dot_general(a, b, dims, preferred_element_type=F32)


def split2(x):
    high = x.astype(BF16)
    return high, (x - high.astype(F32)).astype(BF16)


def split3(x):
    high = x.astype(BF16)
    rest = x - high.astype(F32)
    middle = rest.astype(BF16)
    return high, middle, (rest - middle.astype(F32)).astype(BF16)


def iota(shape, dim):
    return lax.broadcasted_iota(jnp.int32, shape, dim)


def is_odd_tile():
    return lax.axis_index("tile") % 2 == 1


def message_rows(field_rows):
    names = ("coef_high", "coef_low", "offset", "list_high", "list_low")
    return {name: field_rows + 16 * place for place, name in enumerate(names)}


def pack_kernel(
    field_hbm,
    coef_hbm,
    nbr_hbm,
    index_hbm,
    weight_hbm,
    a_ref,
    b_ref,
    lists_ref,
    offset_ref,
    left_ref,
    right_ref,
    coef_ref,
    nbr_ref,
    index_ref,
    weight_ref,
    sems,
    *,
    tiles,
):
    columns = coef_ref.shape[1]
    levels = 8
    half = left_ref.shape[0] // 2
    members = half // levels
    rows = message_rows(half)
    odd = is_odd_tile()
    total = columns * tiles
    copies = [
        pltpu.make_async_copy(source, target, sems.at[k])
        for k, (source, target) in enumerate(
            (
                (field_hbm.at[:, 0:LANES], left_ref),
                (field_hbm.at[:, columns - LANES : columns], right_ref),
                (coef_hbm, coef_ref),
                (nbr_hbm, nbr_ref),
                (index_hbm, index_ref),
                (weight_hbm, weight_ref),
            )
        )
    ]
    for copy in copies:
        copy.start()
    for copy in copies[2:]:
        copy.wait()

    place = lax.axis_index("tile") * columns + iota((6, columns), 1)
    offset = nbr_ref[...] - place
    offset = jnp.where(offset > HALO, offset - total, offset)
    offset = jnp.where(offset < -HALO, offset + total, offset).astype(F32)
    offset_ref[...] = jnp.zeros_like(offset_ref)
    offset_ref[:6, :] = offset
    coef_high, coef_low = split2(coef_ref[...])
    blank = jnp.zeros((16 - 6, LANES), F32)
    for name, value in (
        ("coef_high", coef_high.astype(F32)),
        ("coef_low", coef_low.astype(F32)),
        ("offset", offset),
    ):
        first = jnp.concatenate([value[:, :LANES], blank], axis=0)
        last = jnp.concatenate([value[:, columns - LANES :], blank], axis=0)
        start = rows[name]
        a_ref[start : start + 16, :] = jnp.where(odd, last, first).astype(BF16)
        b_ref[start : start + 16, :] = jnp.where(odd, first, last).astype(BF16)

    blocks = index_ref.shape[0]
    blank = jnp.zeros((16 - blocks, LANES), F32)
    index = index_ref[:, 0, :]
    list_high = jnp.concatenate([(index // 64).astype(F32), blank], axis=0).astype(BF16)
    list_low = jnp.concatenate([(index % 64).astype(F32), blank], axis=0).astype(BF16)
    weight = jnp.concatenate([weight_ref[:, 0, :].astype(F32), blank], axis=0).astype(BF16)
    for ref in (a_ref, b_ref):
        ref[rows["list_high"] : rows["list_high"] + 16, :] = list_high
        ref[rows["list_low"] : rows["list_low"] + 16, :] = list_low
    lists_ref[0:16, :] = list_high
    lists_ref[16:32, :] = list_low
    lists_ref[32:48, :] = weight

    for copy in copies[:2]:
        copy.wait()
    lane = iota((members, LANES), 1)
    for level in range(levels):
        top = pl.ds(level, members, stride=levels)
        low = pl.ds(level + half, members, stride=levels)
        spot = slice(level * members, (level + 1) * members)
        left = jnp.where(lane < 64, left_ref[top, :], pltpu.roll(left_ref[low, :], 64, axis=1))
        right = jnp.where(lane < 64, pltpu.roll(right_ref[top, :], 64, axis=1), right_ref[low, :])
        a_ref[spot, :] = jnp.where(odd, right, left).astype(BF16)
        b_ref[spot, :] = jnp.where(odd, left, right).astype(BF16)


def band(coefs, offsets):
    shape = (LANES + 2 * HALO, LANES)
    spot = iota(shape, 0)
    result = jnp.where(
        spot == iota(shape, 1) + HALO, 1.0 - jnp.sum(coefs, axis=0, keepdims=True), 0.0
    )
    target = iota(offsets.shape, 1) + HALO + offsets.astype(jnp.int32)
    for j in range(6):
        result = result + jnp.where(spot == target[j : j + 1, :], coefs[j : j + 1, :], 0.0)
    return result


def dot3(left, right):
    return dot(left[0], right[0]) + (dot(left[0], right[1]) + dot(left[1], right[0]))


def padded(value, count):
    return jnp.concatenate([value, jnp.zeros((count, value.shape[1]), value.dtype)], axis=0)


def middle_kernel(*refs, groups):
    field_refs = refs[:groups]
    (
        coef_ref,
        offset_ref,
        out_ref,
        edge_high,
        edge_low,
        part_ref,
        second_ref,
        u_high,
        u_low,
        first_high,
        first_low,
        second_high,
        second_low,
    ) = refs[groups:]
    levels, members, middle = out_ref.shape
    columns = groups * LANES
    coef = padded(coef_ref[...], 2)
    reach = offset_ref[...]
    moved_coef = pltpu.roll(coef, HALO, axis=1)
    moved_reach = pltpu.roll(reach, HALO, axis=1)

    def lanes(value, group):
        return value[:, group * LANES : (group + 1) * LANES]

    firsts = {
        g: split2(band(lanes(moved_coef, g), lanes(moved_reach, g))) for g in range(1, groups)
    }
    seconds = [split2(band(lanes(coef, g), lanes(reach, g))) for g in range(groups)]
    for ref in (first_high, first_low, second_high, second_low):
        ref[...] = jnp.zeros_like(ref)
    for g in range(1, groups):
        row, lane = g * LANES - 64, (g - 1) * LANES
        count = min(LANES + 2 * HALO, columns - row)
        first_high[row : row + count, lane : lane + LANES] = firsts[g][0][:count, :]
        first_low[row : row + count, lane : lane + LANES] = firsts[g][1][:count, :]
    for g in range(1, groups - 1):
        row, lane = (g - 1) * LANES, (g - 1) * LANES
        second_high[row : row + LANES + 2 * HALO, lane : lane + LANES] = seconds[g][0]
        second_low[row : row + LANES + 2 * HALO, lane : lane + LANES] = seconds[g][1]
    both = split2(
        dot3((first_high[...], first_low[...]), (second_high[...], second_low[...]))
    )

    for k, g in enumerate((0, groups - 1)):
        second = [padded(value, 64) for value in seconds[g]]
        for j in range(2):
            second_ref[2 * k + j] = second[j]
        if k == 0:
            part = dot3([value[:128, :] for value in firsts[1]], [value[128:, :] for value in second])
            part_ref[k] = jnp.concatenate([jnp.zeros_like(part), part], axis=0)
        else:
            part_ref[k] = padded(dot3(firsts[g], [value[:128, :] for value in second]), 64)

    lane = iota((members, LANES), 1)
    for level in range(levels):
        spot = slice(level * members, (level + 1) * members)
        for group, ref in enumerate(field_refs):
            own = ref[pl.ds(level, members, stride=levels), :]
            high, low = split2(own)
            u_high[spot, group * LANES : (group + 1) * LANES] = high
            u_low[spot, group * LANES : (group + 1) * LANES] = low
        for pieces, ref in ((u_high, edge_high), (u_low, edge_low)):
            turned = [
                pltpu.roll(pieces[spot, g * LANES : (g + 1) * LANES].astype(F32), 64, axis=1)
                for g in (0, 1, groups - 2, groups - 1)
            ]
            zero = jnp.zeros_like(turned[0])
            ref[0, spot, 0:LANES] = jnp.where(lane < 64, zero, turned[0]).astype(BF16)
            ref[0, spot, LANES:] = jnp.where(lane < 64, turned[0], turned[1]).astype(BF16)
            ref[1, spot, 0:LANES] = jnp.where(lane < 64, turned[2], turned[3]).astype(BF16)
            ref[1, spot, LANES:] = jnp.where(lane < 64, turned[3], zero).astype(BF16)
    result = dot3((u_high[...], u_low[...]), both)
    for level in range(levels):
        out_ref[level] = result[level * members : (level + 1) * members, :].astype(BF16)


def edge_kernel(
    a_ref, b_ref, coef_ref, offset_ref, edge_high, edge_low, part_ref, second_ref, out_ref, u_high
):
    levels, members, _ = out_ref.shape
    columns = coef_ref.shape[1]
    half = members // 2
    rows = message_rows(levels * half)
    odd = is_odd_tile()

    def side(k, start, count):
        a = a_ref[start : start + count, :].astype(F32)
        b = b_ref[start : start + count, :].astype(F32)
        return jnp.where(odd, b, a) if k == 0 else jnp.where(odd, a, b)

    own_coef = padded(coef_ref[...], 2)
    lane8 = iota((8, LANES), 1)
    lane = iota((half, LANES), 1)
    operators = []
    for k in range(2):
        near = side(k, rows["coef_high"], 16)[:8] + side(k, rows["coef_low"], 16)[:8]
        reach = side(k, rows["offset"], 16)[:8]
        if k == 0:
            own = (own_coef[:, :LANES], offset_ref[:, :LANES])
            both = [
                jnp.where(
                    lane8 < HALO, pltpu.roll(x, HALO, axis=1), pltpu.roll(y, HALO, axis=1)
                )
                for x, y in zip((near, reach), own)
            ]
            first = split2(band(*both))
            second = [second_ref[j, :128, :] for j in range(2)]
            fresh = padded(dot3(first, second), 64)
        else:
            own = (own_coef[:, columns - LANES :], offset_ref[:, columns - LANES :])
            both = [
                jnp.where(
                    lane8 < HALO, pltpu.roll(y, HALO, axis=1), pltpu.roll(x, HALO, axis=1)
                )
                for x, y in zip((near, reach), own)
            ]
            first = [value[:128, :] for value in split2(band(*both))]
            second = [second_ref[2 + j, 128:, :] for j in range(2)]
            fresh = dot3(first, second)
            fresh = jnp.concatenate([jnp.zeros_like(fresh), fresh], axis=0)
        operators.append(split2(part_ref[k] + fresh))
    for k in range(2):
        for level in range(levels):
            top = level * members
            halo = side(k, level * half, half)
            other = pltpu.roll(halo, 64, axis=1)
            pair = (halo, other) if k == 0 else (other, halo)
            for j in range(2):
                spot = slice(top + j * half, top + (j + 1) * half)
                if k == 0:
                    own = edge_high[k, spot, 0:LANES].astype(F32)
                    u_high[k, spot, 0:LANES] = jnp.where(lane < 64, pair[j], own).astype(BF16)
                    u_high[k, spot, LANES:] = edge_high[k, spot, LANES:]
                else:
                    own = edge_high[k, spot, LANES:].astype(F32)
                    u_high[k, spot, LANES:] = jnp.where(lane < 64, own, pair[j]).astype(BF16)
                    u_high[k, spot, 0:LANES] = edge_high[k, spot, 0:LANES]
        result = dot3((u_high[k], edge_low[k]), operators[k])
        for level in range(levels):
            out_ref[level, :, k * LANES : (k + 1) * LANES] = result[
                level * members : (level + 1) * members, :
            ].astype(BF16)


def gather_lists(own_ref, other_refs, start, blocks):
    parts = [own_ref[start : start + 16, :].astype(F32)]
    parts += [ref[...].astype(F32) for ref in other_refs]
    return jnp.concatenate([part[b : b + 1, :] for part in parts for b in range(blocks)], axis=1)


def read_places(table_ref, slot):
    wide = slot.shape[1]
    valid = (slot >= 0) & (slot < 16 * LANES)
    slot = jnp.where(valid, slot, 0)
    one = jnp.where(iota((LANES, wide), 0) == slot % LANES, 1.0, 0.0).astype(BF16)
    found = dot(table_ref[...], one)
    pick = iota((16, wide), 0) == slot // LANES
    values = [
        jnp.sum(jnp.where(pick, found[16 * k : 16 * k + 16, :], 0.0), axis=0, keepdims=True)
        for k in range(3)
    ]
    column = (values[1] * 16.0 + values[2]).astype(jnp.int32)
    return values[0].astype(jnp.int32), jnp.where(valid, column, -1)


def make_table(cell_ref, level_ref, table):
    cell = cell_ref[...]
    table[0:16, :] = level_ref[...].astype(F32).astype(BF16)
    table[16:32, :] = (cell // 16).astype(F32).astype(BF16)
    table[32:48, :] = (cell % 16).astype(F32).astype(BF16)


def read_forecast(fields, level, column, out_ref, lane):
    members = out_ref.shape[0]
    wide = level.shape[1]
    middle, edge = fields
    inner = middle.shape[1]
    inside = (column >= LANES) & (column < LANES + inner)
    spot = jnp.where(inside, column - LANES, -1)
    one = jnp.where(iota((inner, wide), 0) == spot, 1.0, 0.0).astype(BF16)
    found = dot(middle, one)
    spot = jnp.where(column < LANES, column, column - inner)
    spot = jnp.where(inside, -1, spot)
    one = jnp.where(iota((2 * LANES, wide), 0) == spot, 1.0, 0.0).astype(BF16)
    found = found + dot(edge, one)
    total = jnp.zeros((members, wide), F32)
    for l in range(middle.shape[0] // members):
        total = total + jnp.where(level == l, found[l * members : (l + 1) * members, :], 0.0)
    out_ref[:, lane : lane + wide] = total.astype(BF16)


def neighbour_kernel(middle_ref, edge_ref, a_ref, b_ref, *refs, others, blocks):
    other_refs = refs[:others]
    cell_ref, level_ref, ra_ref, rb_ref, table = refs[others:]
    half = a_ref.shape[0] - 80
    rows = message_rows(half)
    odd = is_odd_tile()
    obs = 16 * LANES
    make_table(cell_ref, level_ref, table)
    fields = [ref[...].reshape(-1, ref.shape[2]) for ref in (middle_ref, edge_ref)]
    for turn, (ref, out_ref) in enumerate(((a_ref, ra_ref), (b_ref, rb_ref))):
        base = 32 * turn
        high = gather_lists(ref, [r.at[base : base + 16, :] for r in other_refs], rows["list_high"], blocks)
        low = gather_lists(ref, [r.at[base + 16 : base + 32, :] for r in other_refs], rows["list_low"], blocks)
        index = (high * 64.0 + low).astype(jnp.int32)
        skip = jnp.where(odd, 0, 2 * obs) if turn == 0 else jnp.where(odd, 2 * obs, 0)
        level, column = read_places(table, index - skip)
        for lane in range(0, index.shape[1], 256):
            read_forecast(
                fields, level[:, lane : lane + 256], column[:, lane : lane + 256], out_ref, lane
            )


def own_kernel(middle_ref, edge_ref, lists_ref, *refs, others, blocks, tiles):
    other_refs = refs[:others]
    cell_ref, level_ref, value_ref, rinv_ref, r_ref, weight_ref, target_ref, table = refs[others:]
    obs = 16 * LANES
    make_table(cell_ref, level_ref, table)
    fields = [ref[...].reshape(-1, ref.shape[2]) for ref in (middle_ref, edge_ref)]

    def gathered(place):
        return gather_lists(
            lists_ref,
            [r.at[64 + 16 * place : 80 + 16 * place, :] for r in other_refs],
            16 * place,
            blocks,
        )

    index = (gathered(0) * 64.0 + gathered(1)).astype(jnp.int32)
    weight = gathered(2)
    wide = index.shape[1]
    level, column = read_places(table, index - obs)
    for lane in range(0, wide, 256):
        read_forecast(fields, level[:, lane : lane + 256], column[:, lane : lane + 256], r_ref, lane)

    tile = lax.axis_index("tile")
    starts = [((tile + tiles + shift) % tiles) * 16 for shift in (-1, 0, 1)]
    one = jnp.where(iota((LANES, wide), 0) == index % LANES, 1.0, 0.0).astype(BF16)
    pick = iota((48, wide), 0) == index // LANES

    def looked_up(ref):
        window = jnp.concatenate([ref[pl.ds(pl.multiple_of(s, 16), 16), :] for s in starts], axis=0)
        high, middle, low = [dot(piece, one) for piece in split3(window)]
        return jnp.sum(jnp.where(pick, (high + middle) + low, 0.0), axis=0, keepdims=True)

    weight_ref[...] = jnp.broadcast_to(looked_up(rinv_ref) * (weight / 3.0), weight_ref.shape)
    target_ref[...] = jnp.broadcast_to(looked_up(value_ref), target_ref.shape)


def doubled(high, low):
    top = jnp.concatenate([high, low], axis=1)
    bottom = jnp.concatenate([high, jnp.zeros_like(low)], axis=1)
    return jnp.concatenate([top, bottom], axis=0)


def product(left, right):
    both = dot(left, right)
    wide = both.shape[1] // 2
    return both[:, :wide] + both[:, wide:]


def joined(pair):
    return jnp.concatenate(pair, axis=1)


def weights_kernel(*refs, others):
    r_refs = refs[: others + 1]
    weight_ref, target_ref, out_ref, pert, weighted, turned, gram_right, hat, inner, outer = refs[others + 1 :]
    members, wide = r_refs[0].shape
    blocks = wide // LANES
    share = blocks // (others + 1)
    ensemble = members * (others + 1)
    free = ensemble - 1.0

    parts = [r_refs[0][...].astype(F32)]
    for k in range(others):
        other = r_refs[k + 1][...].astype(F32)
        turn = ((k + 1) * share * LANES) % wide
        parts.append(jnp.concatenate([other[:, wide - turn :], other[:, : wide - turn]], axis=1))
    total = sum(jnp.sum(part, axis=0, keepdims=True) for part in parts)
    mean = total * (1.0 / ensemble)
    weight = weight_ref[0:1, :]
    for k, part in enumerate(parts):
        rounded = (part - mean).astype(BF16)
        pert[k * members : (k + 1) * members, :] = rounded
        weighted[k * members : (k + 1) * members, :] = (rounded.astype(F32) * weight).astype(BF16)
    departure = target_ref[0:1, :] - mean

    eye = iota((LANES, LANES), 0) == iota((LANES, LANES), 1)

    def spread(value):
        return jnp.where(eye, value, 0.0)

    scales, xs, zs, grams, lefts, inners = [], [], [], [], [], []
    for b in range(blocks):
        lanes = slice(b * LANES, (b + 1) * LANES)
        turned[b] = weighted[:, lanes].T
    for b in range(blocks):
        lanes = slice(b * LANES, (b + 1) * LANES)
        grams.append(dot(turned[b], pert[:, lanes]))
    for b in range(blocks):
        trace = jnp.sum(jnp.sum(spread(grams[b]), axis=0, keepdims=True), axis=1, keepdims=True)
        scales.append(jnp.broadcast_to(1.0 / (free + trace), (1, LANES)))
    for b in range(blocks):
        gram = grams[b] * scales[b]
        x = free * scales[b]
        gram_right[b] = doubled(*split2(gram))
        m = 1.5 - 0.5 * x
        factor = spread(m) - 0.5 * gram
        v = m * x
        inners.append(
            product(joined(split2(factor)), doubled(*split2(factor - spread(0.5 * x))))
            - spread(0.5 * v)
        )
        xs.append(m * v)
        zs.append(m)
    for b in range(blocks):
        inner[b] = inners[b]
        hat[b] = spread(xs[b]) + product(joined(split2(inners[b])), gram_right[b])
        outer[b] = spread(jnp.full((1, LANES), -0.5, F32))

    def step(_, carry):
        xs, zs = carry
        next_xs, next_zs = [], []
        for base in range(0, blocks, 8):
            group = range(base, min(base + 8, blocks))
            lefts, halves = {}, {}
            for b in group:
                x, z = xs[b], zs[b]
                factor = spread(jnp.full((1, LANES), 1.5, F32)) - 0.5 * hat[b]
                f_high, f_low = split2(factor)
                lefts[b] = joined((f_high, f_low))
                inside = inner[b]
                i_high, i_low = split2(inside)
                o_high, o_low = split2(outer[b])
                right_high = joined((i_high, o_high))
                both = dot(lefts[b], jnp.concatenate([right_high, right_high], axis=0)) + dot(
                    f_high, joined((i_low, o_low))
                )
                halves[b] = both[:, :LANES] - (0.5 * x) * inside
                outer[b] = both[:, LANES:] - (0.5 * z) * inside
            for b in group:
                x, z = xs[b], zs[b]
                m = 1.5 - 0.5 * x
                v = m * x
                inner[b] = product(lefts[b], doubled(*split2(halves[b]))) - (0.5 * v) * inner[b]
            for b in group:
                x, z = xs[b], zs[b]
                m = 1.5 - 0.5 * x
                x = m * m * x
                hat[b] = spread(x) + product(joined(split2(inner[b])), gram_right[b])
                next_xs.append(x)
                next_zs.append(m * z)
        return tuple(next_xs), tuple(next_zs)

    xs, zs = lax.fori_loop(1, NS_ITERS - 1, step, (tuple(xs), tuple(zs)))
    zs = list(zs)

    own = iota((members, ensemble), 0) == iota((members, ensemble), 1)
    lasts, rights, rows, cores = [], [], [], []
    for b in range(blocks):
        x, z = xs[b], zs[b]
        factor = spread(jnp.full((1, LANES), 1.5, F32)) - 0.5 * hat[b]
        last = product(joined(split2(factor)), doubled(*split2(outer[b]))) - (0.5 * z) * inner[b]
        zs[b] = (1.5 - 0.5 * x) * z
        lasts.append(split2(last))
    for b in range(blocks):
        rights.append(doubled(*lasts[b]))
        rows.append(jnp.broadcast_to(departure[:, b * LANES : (b + 1) * LANES], (8, LANES)))
    for _ in range(2):
        moved = [product(joined(split2(rows[b])), rights[b]) for b in range(blocks)]
        moved = [product(joined(split2(moved[b])), gram_right[b]) for b in range(blocks)]
        rows = [zs[b] * rows[b] + moved[b] for b in range(blocks)]
    for b in range(blocks):
        mine = pert[:members, b * LANES : (b + 1) * LANES]
        cores.append(dot(joined((mine, mine)), jnp.concatenate(lasts[b], axis=0)))
    for b in range(blocks):
        root = jnp.sqrt(free * scales[b])
        core = cores[b] * (root * scales[b])
        row = rows[b] * scales[b]
        all_rows = joined(split2(jnp.concatenate([core, row, row], axis=0)))
        found = dot(all_rows, jnp.concatenate([turned[b], turned[b]], axis=0))
        diagonal = jnp.where(own, (root * zs[b])[:, 0:1], 0.0)
        out_ref[b] = (found[:members, :] + found[members : members + 1, :] + diagonal).astype(BF16)


def update_kernel(*refs, others):
    middle_refs = refs[: others + 1]
    edge_refs = refs[others + 1 : 2 * others + 2]
    weight_ref, out_ref, stage = refs[2 * others + 2 :]
    members, levels, columns = out_ref.shape
    groups = columns // LANES
    blocks = weight_ref.shape[0]
    width = columns // blocks
    per = LANES // width
    ensemble = members * (others + 1)
    first = lax.axis_index("mem") * (blocks // (others + 1))
    lane = iota((members, LANES), 1)
    for group in range(groups):
        if group in (0, groups - 1):
            field_refs, start = edge_refs, 0 if group == 0 else LANES
        else:
            field_refs, start = middle_refs, (group - 1) * LANES
        lanes = slice(start, start + LANES)
        left = jnp.concatenate(
            [weight_ref[(group * per + k + blocks - first) % blocks] for k in range(per)], axis=0
        )
        for level in range(levels):
            parts = [ref[level, :, lanes].astype(F32) for ref in field_refs]
            total = sum(jnp.sum(part, axis=0, keepdims=True) for part in parts)
            mean = total * (1.0 / ensemble)
            moved = jnp.concatenate([(part - mean).astype(BF16) for part in parts], axis=0)
            found = dot(left, moved)
            result = found[:members, :]
            for k in range(1, per):
                result = jnp.where(lane < k * width, result, found[k * members : (k + 1) * members, :])
            stage[group, pl.ds(level, members, stride=levels), :] = result + mean
        out_ref[:, :, group * LANES : (group + 1) * LANES] = stage[group].reshape(members, levels, LANES).astype(BF16)


def vmem():
    return pl.BlockSpec(memory_space=pltpu.VMEM)


def group_spec(rows, group):
    return pl.BlockSpec((rows, LANES), lambda i: (0, group))


def call(kernel, outs, inputs, scratch=(), in_specs=None, flops=0):
    return pl.pallas_call(
        kernel,
        grid=(1,),
        out_shape=outs,
        in_specs=in_specs or [vmem()] * len(inputs),
        out_specs=[vmem()] * len(outs),
        scratch_shapes=list(scratch),
        compiler_params=pltpu.CompilerParams(vmem_limit_bytes=VMEM_LIMIT),
        cost_estimate=pl.CostEstimate(flops=flops, bytes_accessed=1 << 10, transcendentals=0),
    )(*inputs)


def shards(
    fields,
    coefficients,
    neighbours,
    obs_cell,
    obs_level,
    obs_value,
    obs_rinv,
    obs_index,
    obs_weight,
):
    tiles = lax.axis_size("tile")
    sharers = lax.axis_size("mem")
    others = sharers - 1
    members, levels, columns = fields.shape
    blocks = obs_index.shape[0]
    entries = blocks * sharers * LANES
    half = members * levels // 2
    message = jax.ShapeDtypeStruct((half + 80, LANES), BF16)
    even_pairs = []
    odd_pairs = []
    for i in range(0, tiles, 2):
        even_pairs += [(i, i + 1), (i + 1, i)]
        low, high = i + 1, (i + 2) % tiles
        odd_pairs += [(low, high), (high, low)]
    turns = [[((i + r) % sharers, i) for i in range(sharers)] for r in range(1, sharers)]

    flat = fields.reshape(members * levels, columns)
    groups = columns // LANES
    hbm = pl.BlockSpec(memory_space=pltpu.HBM)
    a, b, lists, offset = call(
        functools.partial(pack_kernel, tiles=tiles),
        [
            message,
            message,
            jax.ShapeDtypeStruct((48, LANES), BF16),
            jax.ShapeDtypeStruct((8, columns), F32),
        ],
        [flat, coefficients, neighbours, obs_index, obs_weight],
        [
            pltpu.VMEM((members * levels, LANES), F32),
            pltpu.VMEM((members * levels, LANES), F32),
            pltpu.VMEM((6, columns), F32),
            pltpu.VMEM((6, columns), jnp.int32),
            pltpu.VMEM(obs_index.shape, jnp.int32),
            pltpu.VMEM(obs_index.shape, jnp.int32),
            pltpu.SemaphoreType.DMA((6,)),
        ],
        in_specs=[hbm] * 5,
    )
    from_b = lax.ppermute(b, "tile", even_pairs)
    from_a = lax.ppermute(a, "tile", odd_pairs)
    flat_rows = members * levels
    middle = columns - 2 * LANES
    forecast, edge_high, edge_low, part, second = call(
        functools.partial(middle_kernel, groups=groups),
        [
            jax.ShapeDtypeStruct((levels, members, middle), BF16),
            jax.ShapeDtypeStruct((2, flat_rows, 2 * LANES), BF16),
            jax.ShapeDtypeStruct((2, flat_rows, 2 * LANES), BF16),
            jax.ShapeDtypeStruct((2, 2 * LANES, LANES), F32),
            jax.ShapeDtypeStruct((4, 2 * LANES, LANES), BF16),
        ],
        [flat] * groups + [coefficients, offset],
        [
            pltpu.VMEM((flat_rows, columns), BF16),
            pltpu.VMEM((flat_rows, columns), BF16),
            pltpu.VMEM((columns, columns - LANES), BF16),
            pltpu.VMEM((columns, columns - LANES), BF16),
            pltpu.VMEM((columns - LANES, middle), BF16),
            pltpu.VMEM((columns - LANES, middle), BF16),
        ],
        in_specs=[group_spec(flat_rows, group) for group in range(groups)] + [vmem()] * 2,
    )
    forecasts = [forecast] + [lax.ppermute(forecast, "mem", turn) for turn in turns]
    passed = jnp.concatenate([from_a[half + 48 :], from_b[half + 48 :], lists], axis=0)
    passed = [lax.ppermute(passed, "mem", turn) for turn in turns]
    (edge,) = call(
        edge_kernel,
        [jax.ShapeDtypeStruct((levels, members, 2 * LANES), BF16)],
        [from_a, from_b, coefficients, offset, edge_high, edge_low, part, second],
        [pltpu.VMEM((2, flat_rows, 2 * LANES), BF16)],
    )
    cell = obs_cell.reshape(16, LANES)
    level = obs_level.reshape(16, LANES)
    reading = jax.ShapeDtypeStruct((members, entries), BF16)
    table = pltpu.VMEM((48, LANES), BF16)
    to_a, to_b = call(
        functools.partial(neighbour_kernel, others=others, blocks=blocks),
        [reading, reading],
        [forecast, edge, from_a, from_b, *passed, cell, level],
        [table],
    )
    back_a = lax.ppermute(to_a, "tile", odd_pairs)
    back_b = lax.ppermute(to_b, "tile", even_pairs)
    vector = jax.ShapeDtypeStruct((8, entries), F32)
    own, weight, target = call(
        functools.partial(own_kernel, others=others, blocks=blocks, tiles=tiles),
        [reading, vector, vector],
        [
            forecast,
            edge,
            lists,
            *passed,
            cell,
            level,
            obs_value.reshape(-1, LANES),
            obs_rinv.reshape(-1, LANES),
        ],
        [table],
    )
    readings = own + back_a + back_b
    readings = [readings] + [lax.ppermute(readings, "mem", turn) for turn in turns]
    edges = [edge] + [lax.ppermute(edge, "mem", turn) for turn in turns]
    ensemble = members * sharers
    total = blocks * sharers
    square = pltpu.VMEM((total, LANES, LANES), F32)
    (weights,) = call(
        functools.partial(weights_kernel, others=others),
        [jax.ShapeDtypeStruct((total, members, ensemble), BF16)],
        [*readings, weight, target],
        [
            pltpu.VMEM((ensemble, entries), BF16),
            pltpu.VMEM((ensemble, entries), BF16),
            pltpu.VMEM((total, LANES, ensemble), BF16),
            pltpu.VMEM((total, 2 * LANES, 2 * LANES), BF16),
            square,
            square,
            square,
        ],
    )
    (analysis,) = call(
        functools.partial(update_kernel, others=others),
        [jax.ShapeDtypeStruct((members, levels, columns), BF16)],
        [*forecasts, *edges, weights],
        [pltpu.VMEM((columns // LANES, members * levels, LANES), F32)],
    )
    return analysis


def solution(mesh):
    in_specs = (
        P("mem", None, "tile"),
        P(None, "tile"),
        P(None, "tile"),
        P("tile"),
        P("tile"),
        P(),
        P(),
        P("mem", "tile", None),
        P("mem", "tile", None),
    )
    out_specs = P("mem", None, "tile")
    return jax.shard_map(shards, mesh=mesh, in_specs=in_specs, out_specs=out_specs, check_vma=False)
```

time: 62.9 us -> 68.4 us (1.087)
  waiting for transfers between devices: 14.7 us -> 30.1 us
  Pallas kernels: 29.9 us -> 19.9 us
    ppermute x1, waiting for transfers between devices: 7.22 us -> 26.2 us  [shards(): lax.ppermute(readings, 'mem', turn)]
    pallas_call x6 -> x7, Pallas kernels: 29.9 us -> 19.9 us  [call(): pl.pallas_call(kernel, grid=(1,), out_shape=outs, in_specs=in_specs or [v...]
    ppermute x1, waiting for transfers between devices: 2.99 us -> 0.98 us  [shards(): back_a = lax.ppermute(to_a, 'tile', odd_pairs)]
    ppermute x1, waiting for transfers between devices: 1.63 us -> 0.01 us  [shards(): lax.ppermute(forecast, 'mem', turn)]
    ppermute x0 -> x1, starting transfers between devices: none -> 1.49 us  [shards(): edges = [edge] + [lax.ppermute(edge, 'mem', turn) for turn in turns]]
    ppermute x1, starting transfers between devices: 1.93 us -> 0.53 us  [shards(): lax.ppermute(forecast, 'mem', turn)]
  transfers between devices with their start and end apart: 7 -> 8, of which waited for: 4 -> 3; matrix products, arithmetic and copies ran while one was open for 0% -> 0% of each run, Pallas kernels for 39% -> 21%
where the time goes in v1:
time: 68.4 us; the launch traced here: 68 us
  waiting for transfers between devices  30.1 us (44%)
  Pallas kernels  19.9 us (29%)
  starting transfers between devices  13.5 us (20%)
  local copies, waits for them, and re-layouts  4.41 us (6%)
    ppermute x1, waiting for transfers between devices, shards(): lax.ppermute(readings, 'mem', turn)  26.2 us
    pallas_call x7, Pallas kernels, call(): pl.pallas_call(kernel, grid=(1,), out_shape=outs, in_specs=in_specs or [v...  19.9 us
    ppermute x1, starting transfers between devices, shards(): from_a = lax.ppermute(a, 'tile', odd_pairs)  5.51 us
    unnamed x18, local copies, waits for them, and re-layouts  4.41 us
    ppermute x1, starting transfers between devices, shards(): back_a = lax.ppermute(to_a, 'tile', odd_pairs)  3.78 us
    ppermute x1, waiting for transfers between devices, shards(): from_a = lax.ppermute(a, 'tile', odd_pairs)  2.87 us
    ppermute x1, starting transfers between devices, shards(): passed = [lax.ppermute(passed, 'mem', turn) for turn in turns]  2 us
    ppermute x1, starting transfers between devices, shards(): edges = [edge] + [lax.ppermute(edge, 'mem', turn) for turn in turns]  1.49 us
  transfers between devices with their start and end apart: 8, of which 3 were waited for; matrix products, arithmetic and copies ran while one was open for 0% of the time, Pallas kernels for 21%

profile of v1, /device:TPU:0, one launch (start us, length us, event | category | flops | bytes accessed | tf_op | source)
XLA Modules:
  0.0 68.0 jit_solution(15676092495117906554)
XLA Ops:
  0.0 0.0 copy-start
  0.0 1.6 %copy-done = f32[128,8,512]{2,1,0:T(8,128)S(1)} copy-done((f32[128,8,512]{2,1,0:T(8,128)S(1)}, f32[128,8,512]{2,1,0:T(8,128)}, u32[]{:S(2)}) %copy-start) | copy-done | bytes 2097176
  1.6 0.0 copy-start.1
  1.6 0.7 %copy-done.1 = f32[6,512]{1,0:T(8,128)S(1)} copy-done((f32[6,512]{1,0:T(8,128)S(1)}, f32[6,512]{1,0:T(8,128)}, u32[]{:S(2)}) %copy-start.1) | copy-done | bytes 12312
  2.3 0.0 copy-start.6
  2.3 0.7 %copy-done.6 = s32[6,512]{1,0:T(8,128)S(1)} copy-done((s32[6,512]{1,0:T(8,128)S(1)}, s32[6,512]{1,0:T(8,128)}, u32[]{:S(2)}) %copy-start.6) | copy-done | bytes 12312
  3.0 0.0 copy-start.7
  3.0 0.7 copy-done.7
  3.7 0.0 copy-start.8
  3.7 0.7 copy-done.8
  4.4 0.4 shard_map.91
  4.8 5.5 %collective-permute-start.1 = (bf16[592,128]{1,0:T(8,128)(2,1)S(1)}, bf16[592,128]{1,0:T(8,128)(2,1)S(1)}, u32[]{:S(2)}, u32[]{:S(2)}) collective-permute-start(bf16[592,128]{1,0:T(8,128)(2,1)S(1)} %get-tuple-element.21), channel_id=1, source_target_pairs={{1,2},{2,1},{3,4},{4,3},{5,6},{6,5},{7,8},{8,7},{9,10},{10,9},{11,... | collective-permute-start | bytes 454664 | tf_op jit(solution)/shard_map/ppermute | solution.py:656
  10.3 0.0 collective-permute-start.2
  10.3 2.9 %collective-permute-done.1.a_ref = bf16[592,128]{1,0:T(8,128)(2,1)S(1)} collective-permute-done((bf16[592,128]{1,0:T(8,128)(2,1)S(1)}, bf16[592,128]{1,0:T(8,128)(2,1)S(1)}, u32[]{:S(2)}, u32[]{:S(2)}) %collective-permute-start.1) | collective-permute-done | bytes 151584 | tf_op jit(solution)/shard_map/ppermute | solution.py:656
  13.2 0.0 collective-permute-done.2.b_ref
  13.2 2.0 %collective-permute-start.4 = (bf16[112,128]{1,0:T(8,128)(2,1)S(1)}, bf16[112,128]{1,0:T(8,128)(2,1)S(1)}, u32[]{:S(2)}, u32[]{:S(2)}) collective-permute-start(bf16[112,128]{1,0:T(8,128)(2,1)S(1)} %pad_maximum_fusion), channel_id=1, source_target_pairs={{16,0},{0,16},{17,1},{1,17},{18,2},{2,18},{19,3},{3,19},{20,4},{4,... | collective-permute-start | bytes 86024 | tf_op jit(solution)/shard_map/ppermute | solution.py:681
  15.2 3.4 %shard_map.92 = (bf16[8,128,256]{2,1,0:T(8,128)(2,1)S(1)}, bf16[2,1024,256]{2,1,0:T(8,128)(2,1)S(1)}, bf16[2,1024,256]{2,1,0:T(8,128)(2,1)S(1)}, f32[2,256,128]{2,1,0:T(8,128)S(1)}, bf16[4,256,128]{2,1,0:T(8,128)(2,1)S(1)}) custom-call(f32[1024,512]{1,0:T(8,128)S(1)} %bitcast.6, f32[1024,512]{1,0:T(8,128)S(1)} %bitcast.7, f32[1024,512]{1,0:T(8,128)S(1)} %bitcast.8, ...), custom_call_target="tpu_custom_call" | custom-call | bytes 1024 | tf_op jit(solution)/shard_map/pallas_call | solution.py:593
  18.6 0.0 copy-start.4
  18.6 0.0 copy-start.5
  18.6 0.0 copy-start.2
  18.7 0.0 copy-start.3
  18.7 1.4 %shard_map.93.edge_ref.refs_2_ = bf16[8,128,256]{2,1,0:T(8,128)(2,1)S(1)} custom-call(bf16[592,128]{1,0:T(8,128)(2,1)S(1)} %collective-permute-done.1.a_ref, bf16[592,128]{1,0:T(8,128)(2,1)S(1)} %collective-permute-done.2.b_ref, f32[6,512]{1,0:T(8,128)S(1)} %copy-done.1, f32[8,512]{1,0:T(8,128)S(1)} %get-tuple-element.19.refs_5_.offset_ref, ...), custom_call_target="tpu_custom_call" | custom-call | bytes 1024 | tf_op jit(solution)/shard_map/pallas_call | solution.py:593
  20.1 0.0 collective-permute-done.4.refs_0_
  20.1 0.0 copy-done.4
  20.1 0.0 copy-done.5
  20.1 2.9 %shard_map.95 = (bf16[128,1024]{1,0:T(8,128)(2,1)S(1)}, bf16[128,1024]{1,0:T(8,128)(2,1)S(1)}) custom-call(bf16[8,128,256]{2,1,0:T(8,128)(2,1)S(1)} %get-tuple-element.20.middle_ref.refs_0_, bf16[8,128,256]{2,1,0:T(8,128)(2,1)S(1)} %shard_map.93.edge_ref.refs_2_, bf16[592,128]{1,0:T(8,128)(2,1)S(1)} %collective-permute-done.1.a_ref, ...), custom_call_target="tpu_custom_call" | custom-call | bytes 1024 | tf_op jit(solution)/shard_map/pallas_call | solution.py:593
  23.0 3.8 %collective-permute-start.5 = (bf16[128,1024]{1,0:T(8,128)(2,1)S(1)}, bf16[128,1024]{1,0:T(8,128)(2,1)S(1)}, u32[]{:S(2)}, u32[]{:S(2)}) collective-permute-start(bf16[128,1024]{1,0:T(8,128)(2,1)S(1)} %get-tuple-element.29), channel_id=1, source_target_pairs={{1,2},{2,1},{3,4},{4,3},{5,6},{6,5},{7,8},{8,7},{9,10},{10,9},{11,... | collective-permute-start | bytes 786440 | tf_op jit(solution)/shard_map/ppermute | solution.py:698
  26.7 0.0 collective-permute-start.6
  26.7 0.5 collective-permute-start
  27.3 1.5 %collective-permute-start.3 = (bf16[8,128,256]{2,1,0:T(8,128)(2,1)S(1)}, bf16[8,128,256]{2,1,0:T(8,128)(2,1)S(1)}, u32[]{:S(2)}, u32[]{:S(2)}) collective-permute-start(bf16[8,128,256]{2,1,0:T(8,128)(2,1)S(1)} %shard_map.93.edge_ref.refs_2_), channel_id=1, source_target_pairs={{16,0},{0,16},{17,1},{1,17},{18,2},{2,18},{19,3},{3,19},{20,4},{4,... | collective-permute-start | bytes 1572872 | tf_op jit(solution)/shard_map/ppermute | solution.py:718
  28.8 0.0 copy-done.2
  28.8 0.0 copy-done.3
  28.8 1.7 %shard_map.94 = (bf16[128,1024]{1,0:T(8,128)(2,1)S(1)}, f32[8,1024]{1,0:T(8,128)S(1)}, f32[8,1024]{1,0:T(8,128)S(1)}) custom-call(bf16[8,128,256]{2,1,0:T(8,128)(2,1)S(1)} %get-tuple-element.20.middle_ref.refs_0_, bf16[8,128,256]{2,1,0:T(8,128)(2,1)S(1)} %shard_map.93.edge_ref.refs_2_, bf16[48,128]{1,0:T(8,128)(2,1)S(1)} %get-tuple-element.27.lists_ref, ...), custom_call_target="tpu_custom_call" | custom-call | bytes 1024 | tf_op jit(solution)/shard_map/pallas_call | solution.py:593
  30.5 1.0 %collective-permute-done.5 = bf16[128,1024]{1,0:T(8,128)(2,1)S(1)} collective-permute-done((bf16[128,1024]{1,0:T(8,128)(2,1)S(1)}, bf16[128,1024]{1,0:T(8,128)(2,1)S(1)}, u32[]{:S(2)}, u32[]{:S(2)}) %collective-permute-start.5) | collective-permute-done | bytes 262176 | tf_op jit(solution)/shard_map/ppermute | solution.py:698
  31.5 0.0 collective-permute-done.6
  31.6 0.2 collective-permute-start.7
  31.7 26.2 %collective-permute-done.7.refs_1_ = bf16[128,1024]{1,0:T(8,128)(2,1)S(1)} collective-permute-done((bf16[128,1024]{1,0:T(8,128)(2,1)S(1)}, bf16[128,1024]{1,0:T(8,128)(2,1)S(1)}, u32[]{:S(2)}, u32[]{:S(2)}) %collective-permute-start.7) | collective-permute-done | bytes 262176 | tf_op jit(solution)/shard_map/ppermute | solution.py:717
  57.9 7.5 %shard_map.96.refs_4_ = bf16[8,128,256]{2,1,0:T(8,128)(2,1)S(1)} custom-call(bf16[128,1024]{1,0:T(8,128)(2,1)S(1)} %add_add_fusion.refs_0_, bf16[128,1024]{1,0:T(8,128)(2,1)S(1)} %collective-permute-done.7.refs_1_, f32[8,1024]{1,0:T(8,128)S(1)} %get-tuple-element.31.refs_2_, f32[8,1024]{1,0:T(8,128)S(1)} %get-tuple-element.32.refs_3_), custom_call_target="tpu_custom_call" | custom-call | bytes 1024 | tf_op jit(solution)/shard_map/pallas_call | solution.py:593
  65.4 0.0 collective-permute-done.refs_1_
  65.4 0.0 collective-permute-done.3.refs_3_
  65.4 2.6 %shard_map.97 = bf16[128,8,512]{2,1,0:T(8,128)(2,1)} custom-call(bf16[8,128,256]{2,1,0:T(8,128)(2,1)S(1)} %get-tuple-element.20.middle_ref.refs_0_, bf16[8,128,256]{2,1,0:T(8,128)(2,1)S(1)} %collective-permute-done.refs_1_, bf16[8,128,256]{2,1,0:T(8,128)(2,1)S(1)} %shard_map.93.edge_ref.refs_2_, bf16[8,128,256]{2,1,0:T(8,128)(2,1)S(1)} %collective-permute-done.3.refs_3_, ...), custom_call_target="tpu_custom_call" | custom-call | bytes 1024 | tf_op jit(solution)/shard_map/pallas_call | solution.py:593
  (4 shorter events, 0.1 us)
Async XLA Ops:
  0.0 1.6 %copy-start = (f32[128,8,512]{2,1,0:T(8,128)S(1)}, f32[128,8,512]{2,1,0:T(8,128)}, u32[]{:S(2)}) copy-start(f32[128,8,512]{2,1,0:T(8,128)} %param.9) | copy-start | bytes 6291460
  1.6 0.7 %copy-start.1 = (f32[6,512]{1,0:T(8,128)S(1)}, f32[6,512]{1,0:T(8,128)}, u32[]{:S(2)}) copy-start(f32[6,512]{1,0:T(8,128)} %coef_ref.1) | copy-start | bytes 36868
  2.3 0.7 %copy-start.6 = (s32[6,512]{1,0:T(8,128)S(1)}, s32[6,512]{1,0:T(8,128)}, u32[]{:S(2)}) copy-start(s32[6,512]{1,0:T(8,128)} %nbr_hbm.1) | copy-start | bytes 36868
  3.0 0.7 %copy-start.7 = (s32[4,1,128]{2,1,0:T(1,128)S(1)}, s32[4,1,128]{2,1,0:T(1,128)}, u32[]{:S(2)}) copy-start(s32[4,1,128]{2,1,0:T(1,128)} %index_hbm.1) | copy-start | bytes 6148
  3.7 0.7 %copy-start.8 = (s32[4,1,128]{2,1,0:T(1,128)S(1)}, s32[4,1,128]{2,1,0:T(1,128)}, u32[]{:S(2)}) copy-start(s32[4,1,128]{2,1,0:T(1,128)} %weight_hbm.1) | copy-start | bytes 6148
  4.8 8.4 %collective-permute-start.1 = (bf16[592,128]{1,0:T(8,128)(2,1)S(1)}, bf16[592,128]{1,0:T(8,128)(2,1)S(1)}, u32[]{:S(2)}, u32[]{:S(2)}) collective-permute-start(bf16[592,128]{1,0:T(8,128)(2,1)S(1)} %get-tuple-element.21), channel_id=1, source_target_pairs={{1,2},{2,1},{3,4},{4,3},{5,6},{6,5},{7,8},{8,7},{9,10},{10,9},{11,... | collective-permute-start | bytes 454664 | tf_op jit(solution)/shard_map/ppermute | solution.py:656
  10.3 2.9 %collective-permute-start.2 = (bf16[592,128]{1,0:T(8,128)(2,1)S(1)}, bf16[592,128]{1,0:T(8,128)(2,1)S(1)}, u32[]{:S(2)}, u32[]{:S(2)}) collective-permute-start(bf16[592,128]{1,0:T(8,128)(2,1)S(1)} %get-tuple-element.22), channel_id=1, source_target_pairs={{0,1},{1,0},{2,3},{3,2},{4,5},{5,4},{6,7},{7,6},{8,9},{9,8},{10,11... | collective-permute-start | bytes 454664 | tf_op jit(solution)/shard_map/ppermute | solution.py:655
  13.2 6.8 %collective-permute-start.4 = (bf16[112,128]{1,0:T(8,128)(2,1)S(1)}, bf16[112,128]{1,0:T(8,128)(2,1)S(1)}, u32[]{:S(2)}, u32[]{:S(2)}) collective-permute-start(bf16[112,128]{1,0:T(8,128)(2,1)S(1)} %pad_maximum_fusion), channel_id=1, source_target_pairs={{16,0},{0,16},{17,1},{1,17},{18,2},{2,18},{19,3},{3,19},{20,4},{4,... | collective-permute-start | bytes 86024 | tf_op jit(solution)/shard_map/ppermute | solution.py:681
  18.6 1.4 %copy-start.4 = (s32[2048]{0:T(1024)S(1)}, s32[2048]{0:T(1024)}, u32[]{:S(2)}) copy-start(s32[2048]{0:T(1024)} %param.12) | copy-start | bytes 24580
  18.6 1.4 %copy-start.5 = (s32[2048]{0:T(1024)S(1)}, s32[2048]{0:T(1024)}, u32[]{:S(2)}) copy-start(s32[2048]{0:T(1024)} %param.13) | copy-start | bytes 24580
  18.6 10.1 %copy-start.2 = (f32[32768]{0:T(1024)S(1)}, f32[32768]{0:T(1024)}, u32[]{:S(2)}) copy-start(f32[32768]{0:T(1024)} %param.14) | copy-start | bytes 393220
  18.7 10.1 %copy-start.3 = (f32[32768]{0:T(1024)S(1)}, f32[32768]{0:T(1024)}, u32[]{:S(2)}) copy-start(f32[32768]{0:T(1024)} %param.15) | copy-start | bytes 393220
  23.0 8.6 %collective-permute-start.5 = (bf16[128,1024]{1,0:T(8,128)(2,1)S(1)}, bf16[128,1024]{1,0:T(8,128)(2,1)S(1)}, u32[]{:S(2)}, u32[]{:S(2)}) collective-permute-start(bf16[128,1024]{1,0:T(8,128)(2,1)S(1)} %get-tuple-element.29), channel_id=1, source_target_pairs={{1,2},{2,1},{3,4},{4,3},{5,6},{6,5},{7,8},{8,7},{9,10},{10,9},{11,... | collective-permute-start | bytes 786440 | tf_op jit(solution)/shard_map/ppermute | solution.py:698
  26.7 4.8 %collective-permute-start.6 = (bf16[128,1024]{1,0:T(8,128)(2,1)S(1)}, bf16[128,1024]{1,0:T(8,128)(2,1)S(1)}, u32[]{:S(2)}, u32[]{:S(2)}) collective-permute-start(bf16[128,1024]{1,0:T(8,128)(2,1)S(1)} %get-tuple-element.30), channel_id=1, source_target_pairs={{0,1},{1,0},{2,3},{3,2},{4,5},{5,4},{6,7},{7,6},{8,9},{9,8},{10,11... | collective-permute-start | bytes 786440 | tf_op jit(solution)/shard_map/ppermute | solution.py:699
  26.7 38.7 %collective-permute-start = (bf16[8,128,256]{2,1,0:T(8,128)(2,1)S(1)}, bf16[8,128,256]{2,1,0:T(8,128)(2,1)S(1)}, u32[]{:S(2)}, u32[]{:S(2)}) collective-permute-start(bf16[8,128,256]{2,1,0:T(8,128)(2,1)S(1)} %get-tuple-element.20.middle_ref.refs_0_), channel_id=1, source_target_pairs={{16,0},{0,16},{17,1},{1,17},{18,2},{2,18},{19,3},{3,19},{20,4},{4,... | collective-permute-start | bytes 1572872 | tf_op jit(solution)/shard_map/ppermute | solution.py:679
  27.3 38.1 %collective-permute-start.3 = (bf16[8,128,256]{2,1,0:T(8,128)(2,1)S(1)}, bf16[8,128,256]{2,1,0:T(8,128)(2,1)S(1)}, u32[]{:S(2)}, u32[]{:S(2)}) collective-permute-start(bf16[8,128,256]{2,1,0:T(8,128)(2,1)S(1)} %shard_map.93.edge_ref.refs_2_), channel_id=1, source_target_pairs={{16,0},{0,16},{17,1},{1,17},{18,2},{2,18},{19,3},{3,19},{20,4},{4,... | collective-permute-start | bytes 1572872 | tf_op jit(solution)/shard_map/ppermute | solution.py:718
  31.6 26.4 %collective-permute-start.7 = (bf16[128,1024]{1,0:T(8,128)(2,1)S(1)}, bf16[128,1024]{1,0:T(8,128)(2,1)S(1)}, u32[]{:S(2)}, u32[]{:S(2)}) collective-permute-start(bf16[128,1024]{1,0:T(8,128)(2,1)S(1)} %add_add_fusion.refs_0_), channel_id=1, source_target_pairs={{16,0},{0,16},{17,1},{1,17},{18,2},{2,18},{19,3},{3,19},{20,4},{4,... | collective-permute-start | bytes 786440 | tf_op jit(solution)/shard_map/ppermute | solution.py:717

commit v2 on v1

--- a/solution.py
+++ b/solution.py
@@ -57,7 +57,7 @@
     a_ref,
     b_ref,
     lists_ref,
-    offset_ref,
+    small_ref,
     left_ref,
     right_ref,
     coef_ref,
@@ -79,53 +79,50 @@
         pltpu.make_async_copy(source, target, sems.at[k])
         for k, (source, target) in enumerate(
             (
-                (field_hbm.at[:, 0:LANES], left_ref),
-                (field_hbm.at[:, columns - LANES : columns], right_ref),
                 (coef_hbm, coef_ref),
                 (nbr_hbm, nbr_ref),
                 (index_hbm, index_ref),
                 (weight_hbm, weight_ref),
+                (field_hbm.at[:, 0:LANES], left_ref),
+                (field_hbm.at[:, columns - LANES : columns], right_ref),
             )
         )
     ]
     for copy in copies:
         copy.start()
-    for copy in copies[2:]:
+    for copy in copies[:4]:
         copy.wait()
 
     place = lax.axis_index("tile") * columns + iota((6, columns), 1)
     offset = nbr_ref[...] - place
     offset = jnp.where(offset > HALO, offset - total, offset)
     offset = jnp.where(offset < -HALO, offset + total, offset).astype(F32)
-    offset_ref[...] = jnp.zeros_like(offset_ref)
-    offset_ref[:6, :] = offset
+    small_ref[...] = jnp.zeros_like(small_ref)
+    small_ref[0:6, :] = coef_ref[...]
+    small_ref[8:14, :] = offset
     coef_high, coef_low = split2(coef_ref[...])
-    blank = jnp.zeros((16 - 6, LANES), F32)
     for name, value in (
         ("coef_high", coef_high.astype(F32)),
         ("coef_low", coef_low.astype(F32)),
         ("offset", offset),
     ):
-        first = jnp.concatenate([value[:, :LANES], blank], axis=0)
-        last = jnp.concatenate([value[:, columns - LANES :], blank], axis=0)
+        first = padded(value[:, :LANES], 10)
+        last = padded(value[:, columns - LANES :], 10)
         start = rows[name]
         a_ref[start : start + 16, :] = jnp.where(odd, last, first).astype(BF16)
         b_ref[start : start + 16, :] = jnp.where(odd, first, last).astype(BF16)
-
     blocks = index_ref.shape[0]
-    blank = jnp.zeros((16 - blocks, LANES), F32)
-    index = index_ref[:, 0, :]
-    list_high = jnp.concatenate([(index // 64).astype(F32), blank], axis=0).astype(BF16)
-    list_low = jnp.concatenate([(index % 64).astype(F32), blank], axis=0).astype(BF16)
-    weight = jnp.concatenate([weight_ref[:, 0, :].astype(F32), blank], axis=0).astype(BF16)
-    for ref in (a_ref, b_ref):
-        ref[rows["list_high"] : rows["list_high"] + 16, :] = list_high
-        ref[rows["list_low"] : rows["list_low"] + 16, :] = list_low
-    lists_ref[0:16, :] = list_high
-    lists_ref[16:32, :] = list_low
-    lists_ref[32:48, :] = weight
-
-    for copy in copies[:2]:
+    index = padded(index_ref[:, 0, :].astype(F32), 16 - blocks)
+    high = jnp.floor(index * (1.0 / 64.0))
+    for k, value in enumerate((high, index - 64.0 * high)):
+        value = value.astype(BF16)
+        start = rows["list_high"] + 16 * k
+        a_ref[start : start + 16, :] = value
+        b_ref[start : start + 16, :] = value
+        lists_ref[16 * k : 16 * k + 16, :] = value
+    lists_ref[32:48, :] = padded(weight_ref[:, 0, :].astype(F32), 16 - blocks).astype(BF16)
+
+    for copy in copies[4:]:
         copy.wait()
     lane = iota((members, LANES), 1)
     for level in range(levels):
@@ -161,8 +158,7 @@
 def middle_kernel(*refs, groups):
     field_refs = refs[:groups]
     (
-        coef_ref,
-        offset_ref,
+        small_ref,
         out_ref,
         edge_high,
         edge_low,
@@ -177,8 +173,8 @@
     ) = refs[groups:]
     levels, members, middle = out_ref.shape
     columns = groups * LANES
-    coef = padded(coef_ref[...], 2)
-    reach = offset_ref[...]
+    coef = padded(small_ref[0:6, :], 2)
+    reach = padded(small_ref[8:14, :], 2)
     moved_coef = pltpu.roll(coef, HALO, axis=1)
     moved_reach = pltpu.roll(reach, HALO, axis=1)
 
@@ -238,10 +234,10 @@
 
 
 def edge_kernel(
-    a_ref, b_ref, coef_ref, offset_ref, edge_high, edge_low, part_ref, second_ref, out_ref, u_high
+    a_ref, b_ref, small_ref, edge_high, edge_low, part_ref, second_ref, left_ref, right_ref, u_high
 ):
-    levels, members, _ = out_ref.shape
-    columns = coef_ref.shape[1]
+    levels, members, _ = left_ref.shape
+    columns = small_ref.shape[1]
     half = members // 2
     rows = message_rows(levels * half)
     odd = is_odd_tile()
@@ -251,7 +247,8 @@
         b = b_ref[start : start + count, :].astype(F32)
         return jnp.where(odd, b, a) if k == 0 else jnp.where(odd, a, b)
 
-    own_coef = padded(coef_ref[...], 2)
+    own_coef = padded(small_ref[0:6, :], 2)
+    own_reach = padded(small_ref[8:14, :], 2)
     lane8 = iota((8, LANES), 1)
     lane = iota((half, LANES), 1)
     operators = []
@@ -259,7 +256,7 @@
         near = side(k, rows["coef_high"], 16)[:8] + side(k, rows["coef_low"], 16)[:8]
         reach = side(k, rows["offset"], 16)[:8]
         if k == 0:
-            own = (own_coef[:, :LANES], offset_ref[:, :LANES])
+            own = (own_coef[:, :LANES], own_reach[:, :LANES])
             both = [
                 jnp.where(
                     lane8 < HALO, pltpu.roll(x, HALO, axis=1), pltpu.roll(y, HALO, axis=1)
@@ -270,7 +267,7 @@
             second = [second_ref[j, :128, :] for j in range(2)]
             fresh = padded(dot3(first, second), 64)
         else:
-            own = (own_coef[:, columns - LANES :], offset_ref[:, columns - LANES :])
+            own = (own_coef[:, columns - LANES :], own_reach[:, columns - LANES :])
             both = [
                 jnp.where(
                     lane8 < HALO, pltpu.roll(y, HALO, axis=1), pltpu.roll(x, HALO, axis=1)
@@ -299,16 +296,15 @@
                     u_high[k, spot, LANES:] = jnp.where(lane < 64, own, pair[j]).astype(BF16)
                     u_high[k, spot, 0:LANES] = edge_high[k, spot, 0:LANES]
         result = dot3((u_high[k], edge_low[k]), operators[k])
+        out_ref = (left_ref, right_ref)[k]
         for level in range(levels):
-            out_ref[level, :, k * LANES : (k + 1) * LANES] = result[
-                level * members : (level + 1) * members, :
-            ].astype(BF16)
-
-
-def gather_lists(own_ref, other_refs, start, blocks):
-    parts = [own_ref[start : start + 16, :].astype(F32)]
-    parts += [ref[...].astype(F32) for ref in other_refs]
-    return jnp.concatenate([part[b : b + 1, :] for part in parts for b in range(blocks)], axis=1)
+            out_ref[level] = result[level * members : (level + 1) * members, :].astype(BF16)
+
+
+def gather_lists(parts, blocks):
+    return jnp.concatenate(
+        [part[b : b + 1, :].astype(F32) for part in parts for b in range(blocks)], axis=1
+    )
 
 
 def read_places(table_ref, slot):
@@ -336,7 +332,7 @@
 def read_forecast(fields, level, column, out_ref, lane):
     members = out_ref.shape[0]
     wide = level.shape[1]
-    middle, edge = fields
+    middle, left, right = fields
     inner = middle.shape[1]
     inside = (column >= LANES) & (column < LANES + inner)
     spot = jnp.where(inside, column - LANES, -1)
@@ -345,14 +341,14 @@
     spot = jnp.where(column < LANES, column, column - inner)
     spot = jnp.where(inside, -1, spot)
     one = jnp.where(iota((2 * LANES, wide), 0) == spot, 1.0, 0.0).astype(BF16)
-    found = found + dot(edge, one)
+    found = found + dot(jnp.concatenate([left, right], axis=1), one)
     total = jnp.zeros((members, wide), F32)
     for l in range(middle.shape[0] // members):
         total = total + jnp.where(level == l, found[l * members : (l + 1) * members, :], 0.0)
     out_ref[:, lane : lane + wide] = total.astype(BF16)
 
 
-def neighbour_kernel(middle_ref, edge_ref, a_ref, b_ref, *refs, others, blocks):
+def neighbour_kernel(middle_ref, left_ref, right_ref, a_ref, b_ref, *refs, others, blocks):
     other_refs = refs[:others]
     cell_ref, level_ref, ra_ref, rb_ref, table = refs[others:]
     half = a_ref.shape[0] - 80
@@ -360,11 +356,13 @@
     odd = is_odd_tile()
     obs = 16 * LANES
     make_table(cell_ref, level_ref, table)
-    fields = [ref[...].reshape(-1, ref.shape[2]) for ref in (middle_ref, edge_ref)]
+    fields = [ref[...].reshape(-1, ref.shape[2]) for ref in (middle_ref, left_ref, right_ref)]
     for turn, (ref, out_ref) in enumerate(((a_ref, ra_ref), (b_ref, rb_ref))):
         base = 32 * turn
-        high = gather_lists(ref, [r.at[base : base + 16, :] for r in other_refs], rows["list_high"], blocks)
-        low = gather_lists(ref, [r.at[base + 16 : base + 32, :] for r in other_refs], rows["list_low"], blocks)
+        parts = [ref[rows["list_high"] : rows["list_high"] + 32, :]]
+        parts += [r[base : base + 32, :] for r in other_refs]
+        high = gather_lists([part[:16, :] for part in parts], blocks)
+        low = gather_lists([part[16:, :] for part in parts], blocks)
         index = (high * 64.0 + low).astype(jnp.int32)
         skip = jnp.where(odd, 0, 2 * obs) if turn == 0 else jnp.where(odd, 2 * obs, 0)
         level, column = read_places(table, index - skip)
@@ -374,23 +372,17 @@
             )
 
 
-def own_kernel(middle_ref, edge_ref, lists_ref, *refs, others, blocks, tiles):
+def own_kernel(middle_ref, left_ref, right_ref, lists_ref, *refs, others, blocks, tiles):
     other_refs = refs[:others]
     cell_ref, level_ref, value_ref, rinv_ref, r_ref, weight_ref, target_ref, table = refs[others:]
     obs = 16 * LANES
     make_table(cell_ref, level_ref, table)
-    fields = [ref[...].reshape(-1, ref.shape[2]) for ref in (middle_ref, edge_ref)]
-
-    def gathered(place):
-        return gather_lists(
-            lists_ref,
-            [r.at[64 + 16 * place : 80 + 16 * place, :] for r in other_refs],
-            16 * place,
-            blocks,
-        )
-
-    index = (gathered(0) * 64.0 + gathered(1)).astype(jnp.int32)
-    weight = gathered(2)
+    fields = [ref[...].reshape(-1, ref.shape[2]) for ref in (middle_ref, left_ref, right_ref)]
+
+    parts = [lists_ref[...]] + [r[64:112, :] for r in other_refs]
+    passed = [gather_lists([part[16 * k : 16 * k + 16, :] for part in parts], blocks) for k in range(3)]
+    index = (passed[0] * 64.0 + passed[1]).astype(jnp.int32)
+    weight = passed[2]
     wide = index.shape[1]
     level, column = read_places(table, index - obs)
     for lane in range(0, wide, 256):
@@ -408,6 +400,13 @@
 
     weight_ref[...] = jnp.broadcast_to(looked_up(rinv_ref) * (weight / 3.0), weight_ref.shape)
     target_ref[...] = jnp.broadcast_to(looked_up(value_ref), target_ref.shape)
+
+
+def merge_kernel(own_ref, a_ref, b_ref, *refs):
+    out_ref = refs[-1]
+    out_ref[...] = (
+        own_ref[...].astype(F32) + (a_ref[...].astype(F32) + b_ref[...].astype(F32))
+    ).astype(BF16)
 
 
 def doubled(high, low):
@@ -549,8 +548,9 @@
 
 def update_kernel(*refs, others):
     middle_refs = refs[: others + 1]
-    edge_refs = refs[others + 1 : 2 * others + 2]
-    weight_ref, out_ref, stage = refs[2 * others + 2 :]
+    left_refs = refs[others + 1 : 2 * others + 2]
+    right_refs = refs[2 * others + 2 : 3 * others + 3]
+    weight_ref, out_ref, stage = refs[3 * others + 3 :]
     members, levels, columns = out_ref.shape
     groups = columns // LANES
     blocks = weight_ref.shape[0]
@@ -561,7 +561,7 @@
     lane = iota((members, LANES), 1)
     for group in range(groups):
         if group in (0, groups - 1):
-            field_refs, start = edge_refs, 0 if group == 0 else LANES
+            field_refs, start = (left_refs if group == 0 else right_refs), 0
         else:
             field_refs, start = middle_refs, (group - 1) * LANES
         lanes = slice(start, start + LANES)
@@ -589,7 +589,7 @@
     return pl.BlockSpec((rows, LANES), lambda i: (0, group))
 
 
-def call(kernel, outs, inputs, scratch=(), in_specs=None, flops=0):
+def call(kernel, outs, inputs, scratch=(), in_specs=None, cost=0, limit=VMEM_LIMIT):
     return pl.pallas_call(
         kernel,
         grid=(1,),
@@ -597,8 +597,8 @@
         in_specs=in_specs or [vmem()] * len(inputs),
         out_specs=[vmem()] * len(outs),
         scratch_shapes=list(scratch),
-        compiler_params=pltpu.CompilerParams(vmem_limit_bytes=VMEM_LIMIT),
-        cost_estimate=pl.CostEstimate(flops=flops, bytes_accessed=1 << 10, transcendentals=0),
+        compiler_params=pltpu.CompilerParams(vmem_limit_bytes=limit),
+        cost_estimate=pl.CostEstimate(flops=cost << 30, bytes_accessed=1 << 10, transcendentals=0),
     )(*inputs)
 
 
@@ -632,13 +632,13 @@
     flat = fields.reshape(members * levels, columns)
     groups = columns // LANES
     hbm = pl.BlockSpec(memory_space=pltpu.HBM)
-    a, b, lists, offset = call(
+    a, b, lists, small = call(
         functools.partial(pack_kernel, tiles=tiles),
         [
             message,
             message,
             jax.ShapeDtypeStruct((48, LANES), BF16),
-            jax.ShapeDtypeStruct((8, columns), F32),
+            jax.ShapeDtypeStruct((16, columns), F32),
         ],
         [flat, coefficients, neighbours, obs_index, obs_weight],
         [
@@ -651,6 +651,7 @@
             pltpu.SemaphoreType.DMA((6,)),
         ],
         in_specs=[hbm] * 5,
+        limit=64 * 1024 * 1024,
     )
     from_b = lax.ppermute(b, "tile", even_pairs)
     from_a = lax.ppermute(a, "tile", odd_pairs)
@@ -665,7 +666,7 @@
             jax.ShapeDtypeStruct((2, 2 * LANES, LANES), F32),
             jax.ShapeDtypeStruct((4, 2 * LANES, LANES), BF16),
         ],
-        [flat] * groups + [coefficients, offset],
+        [flat] * groups + [small],
         [
             pltpu.VMEM((flat_rows, columns), BF16),
             pltpu.VMEM((flat_rows, columns), BF16),
@@ -674,16 +675,19 @@
             pltpu.VMEM((columns - LANES, middle), BF16),
             pltpu.VMEM((columns - LANES, middle), BF16),
         ],
-        in_specs=[group_spec(flat_rows, group) for group in range(groups)] + [vmem()] * 2,
-    )
-    forecasts = [forecast] + [lax.ppermute(forecast, "mem", turn) for turn in turns]
+        in_specs=[group_spec(flat_rows, group) for group in range(groups)] + [vmem()],
+        cost=4,
+    )
     passed = jnp.concatenate([from_a[half + 48 :], from_b[half + 48 :], lists], axis=0)
+    passed, sent = lax.optimization_barrier((passed, forecast))
+    forecasts = [forecast] + [lax.ppermute(sent, "mem", turn) for turn in turns]
     passed = [lax.ppermute(passed, "mem", turn) for turn in turns]
-    (edge,) = call(
+    left, right = call(
         edge_kernel,
-        [jax.ShapeDtypeStruct((levels, members, 2 * LANES), BF16)],
-        [from_a, from_b, coefficients, offset, edge_high, edge_low, part, second],
+        [jax.ShapeDtypeStruct((levels, members, LANES), BF16)] * 2,
+        [from_a, from_b, small, edge_high, edge_low, part, second],
         [pltpu.VMEM((2, flat_rows, 2 * LANES), BF16)],
+        cost=2,
     )
     cell = obs_cell.reshape(16, LANES)
     level = obs_level.reshape(16, LANES)
@@ -692,8 +696,9 @@
     to_a, to_b = call(
         functools.partial(neighbour_kernel, others=others, blocks=blocks),
         [reading, reading],
-        [forecast, edge, from_a, from_b, *passed, cell, level],
+        [forecast, left, right, from_a, from_b, *passed, cell, level],
         [table],
+        cost=3,
     )
     back_a = lax.ppermute(to_a, "tile", odd_pairs)
     back_b = lax.ppermute(to_b, "tile", even_pairs)
@@ -703,7 +708,8 @@
         [reading, vector, vector],
         [
             forecast,
-            edge,
+            left,
+            right,
             lists,
             *passed,
             cell,
@@ -712,10 +718,20 @@
             obs_rinv.reshape(-1, LANES),
         ],
         [table],
-    )
-    readings = own + back_a + back_b
+        cost=2,
+    )
+    unused = forecasts[1:]
+    (readings,) = call(
+        merge_kernel,
+        [reading],
+        [own, back_a, back_b, *unused],
+        in_specs=[vmem()] * 3 + [pl.BlockSpec(memory_space=pl.ANY)] * len(unused),
+        cost=0,
+    )
+    readings, sent_left, sent = lax.optimization_barrier((readings, left, right))
+    lefts = [left] + [lax.ppermute(sent_left, "mem", turn) for turn in turns]
+    rights = [right] + [lax.ppermute(sent, "mem", turn) for turn in turns]
     readings = [readings] + [lax.ppermute(readings, "mem", turn) for turn in turns]
-    edges = [edge] + [lax.ppermute(edge, "mem", turn) for turn in turns]
     ensemble = members * sharers
     total = blocks * sharers
     square = pltpu.VMEM((total, LANES, LANES), F32)
@@ -732,12 +748,14 @@
             square,
             square,
         ],
+        cost=8,
     )
     (analysis,) = call(
         functools.partial(update_kernel, others=others),
         [jax.ShapeDtypeStruct((members, levels, columns), BF16)],
-        [*forecasts, *edges, weights],
+        [*forecasts, *lefts, *rights, weights],
         [pltpu.VMEM((columns // LANES, members * levels, LANES), F32)],
+        cost=3,
     )
     return analysis
 

time: 68.4 us -> 51 us (0.75)
  waiting for transfers between devices: 30.1 us -> 14.6 us
  local copies, waits for them, and re-layouts: 4.41 us -> 2.38 us
  Pallas kernels: 19.9 us -> 21.7 us
  starting transfers between devices: 13.5 us -> 12 us
    ppermute x1, waiting for transfers between devices: 26.2 us -> 5.73 us  [shards(): lax.ppermute(readings, 'mem', turn)]
    ppermute x1, waiting for transfers between devices: 0.98 us -> 5.99 us  [shards(): back_a = lax.ppermute(to_a, 'tile', odd_pairs)]
    ppermute x1, starting transfers between devices: 3.78 us -> 0.8 us  [shards(): back_a = lax.ppermute(to_a, 'tile', odd_pairs)]
    ppermute x1, waiting for transfers between devices: 2.87 us -> 0.01 us  [shards(): from_a = lax.ppermute(a, 'tile', odd_pairs)]
    ppermute x2 -> x3, waiting for transfers between devices: 0.01 us -> 2.38 us  [the longest x1 2.14 us: shards(): rights = [right] + [lax.ppermute(sent, 'mem', turn) for turn in turns]]
    unnamed x18 -> x16, local copies, waits for them, and re-layouts: 4.41 us -> 2.37 us
    pallas_call x7 -> x8, Pallas kernels: 19.9 us -> 21.7 us  [call(): pl.pallas_call(kernel, grid=(1,), out_shape=outs, in_specs=in_specs or [v...]
    ppermute x1, starting transfers between devices: 0.16 us -> 1.55 us  [shards(): lax.ppermute(readings, 'mem', turn)]
  transfers between devices with their start and end apart: 8 -> 9, of which waited for: 3 -> 5; matrix products, arithmetic and copies ran while one was open for 0% -> 0% of each run, Pallas kernels for 21% -> 33%
where the time goes in v2:
time: 51 us; the launch traced here: 50.7 us
  Pallas kernels  21.7 us (43%)
  waiting for transfers between devices  14.6 us (29%)
  starting transfers between devices  12 us (24%)
  local copies, waits for them, and re-layouts  2.38 us (5%)
    pallas_call x8, Pallas kernels, call(): pl.pallas_call(kernel, grid=(1,), out_shape=outs, in_specs=in_specs or [v...  21.7 us
    ppermute x1, waiting for transfers between devices, shards(): back_a = lax.ppermute(to_a, 'tile', odd_pairs)  5.99 us
    ppermute x1, waiting for transfers between devices, shards(): lax.ppermute(readings, 'mem', turn)  5.73 us
    ppermute x1, starting transfers between devices, shards(): from_a = lax.ppermute(a, 'tile', odd_pairs)  5.51 us
    unnamed x16, local copies, waits for them, and re-layouts  2.37 us
    ppermute x1, waiting for transfers between devices, shards(): rights = [right] + [lax.ppermute(sent, 'mem', turn) for turn in turns]  2.14 us
    ppermute x1, starting transfers between devices, shards(): passed = [lax.ppermute(passed, 'mem', turn) for turn in turns]  1.56 us
    ppermute x1, starting transfers between devices, shards(): lax.ppermute(readings, 'mem', turn)  1.55 us
  transfers between devices with their start and end apart: 9, of which 5 were waited for; matrix products, arithmetic and copies ran while one was open for 0% of the time, Pallas kernels for 33%

profile of v2, /device:TPU:0, one launch (start us, length us, event | category | flops | bytes accessed | tf_op | source)
XLA Modules:
  0.0 50.7 jit_solution(3010265147454009764)
XLA Ops:
  0.0 2.2 %shard_map.91 = (bf16[592,128]{1,0:T(8,128)(2,1)}, bf16[592,128]{1,0:T(8,128)(2,1)}, bf16[48,128]{1,0:T(8,128)(2,1)}, f32[16,512]{1,0:T(8,128)}) custom-call(f32[1024,512]{1,0:T(8,128)} %bitcast.5, f32[6,512]{1,0:T(8,128)} %coef_hbm.1, s32[6,512]{1,0:T(8,128)} %nbr_hbm.1, s32[4,1,128]{2,1,0:T(1,128)} %index_hbm.1, s32[4,1,128]{2,1,0:T(1,128)} %weight_hbm.1), custom_call_target="tpu_custom_call" | custom-call | bytes 1024 | tf_op jit(solution)/shard_map/pallas_call | solution.py:593
  2.2 5.5 %collective-permute-start = (bf16[592,128]{1,0:T(8,128)(2,1)}, bf16[592,128]{1,0:T(8,128)(2,1)S(1)}, u32[]{:S(2)}, u32[]{:S(2)}) collective-permute-start(bf16[592,128]{1,0:T(8,128)(2,1)} %get-tuple-element.28), channel_id=1, source_target_pairs={{1,2},{2,1},{3,4},{4,3},{5,6},{6,5},{7,8},{8,7},{9,10},{10,9},{11,... | collective-permute-start | bytes 454664 | tf_op jit(solution)/shard_map/ppermute | solution.py:657
  7.7 0.0 collective-permute-start.1
  7.7 0.0 copy-start
  7.7 1.6 %copy-done = f32[128,8,512]{2,1,0:T(8,128)S(1)} copy-done((f32[128,8,512]{2,1,0:T(8,128)S(1)}, f32[128,8,512]{2,1,0:T(8,128)}, u32[]{:S(2)}) %copy-start) | copy-done | bytes 2097176
  9.3 0.0 copy-start.4
  9.3 0.8 %copy-done.4 = f32[16,512]{1,0:T(8,128)S(1)} copy-done((f32[16,512]{1,0:T(8,128)S(1)}, f32[16,512]{1,0:T(8,128)}, u32[]{:S(2)}) %copy-start.4) | copy-done | bytes 32792
  10.1 0.0 copy-start.1
  10.1 0.0 copy-start.5
  10.1 3.4 %shard_map.92 = (bf16[8,128,256]{2,1,0:T(8,128)(2,1)S(1)}, bf16[2,1024,256]{2,1,0:T(8,128)(2,1)S(1)}, bf16[2,1024,256]{2,1,0:T(8,128)(2,1)S(1)}, f32[2,256,128]{2,1,0:T(8,128)S(1)}, bf16[4,256,128]{2,1,0:T(8,128)(2,1)S(1)}) custom-call(f32[1024,512]{1,0:T(8,128)S(1)} %bitcast.6, f32[1024,512]{1,0:T(8,128)S(1)} %bitcast.7, f32[1024,512]{1,0:T(8,128)S(1)} %bitcast.8, ...), custom_call_target="tpu_custom_call" | custom-call | flops 4294967296 | bytes 1024 | tf_op jit(solution)/shard_map/pallas_call | solution.py:593
  13.5 0.0 collective-permute-done.a_ref
  13.5 0.0 collective-permute-done.1.b_ref
  13.5 0.0 copy-done.1
  13.5 1.6 %collective-permute-start.3 = (bf16[112,128]{1,0:T(8,128)(2,1)S(1)}, bf16[112,128]{1,0:T(8,128)(2,1)S(1)}, u32[]{:S(2)}, u32[]{:S(2)}) collective-permute-start(bf16[112,128]{1,0:T(8,128)(2,1)S(1)} %pad_maximum_fusion), channel_id=1, source_target_pairs={{16,0},{0,16},{17,1},{1,17},{18,2},{2,18},{19,3},{3,19},{20,4},{4,... | collective-permute-start | bytes 86024 | tf_op jit(solution)/shard_map/ppermute | solution.py:684
  15.1 0.5 %collective-permute-start.2 = (bf16[8,128,256]{2,1,0:T(8,128)(2,1)S(1)}, bf16[8,128,256]{2,1,0:T(8,128)(2,1)S(1)}, u32[]{:S(2)}, u32[]{:S(2)}) collective-permute-start(bf16[8,128,256]{2,1,0:T(8,128)(2,1)S(1)} %get-tuple-element.31.middle_ref.refs_0_), channel_id=1, source_target_pairs={{16,0},{0,16},{17,1},{1,17},{18,2},{2,18},{19,3},{3,19},{20,4},{4,... | collective-permute-start | bytes 1572872 | tf_op jit(solution)/shard_map/ppermute | solution.py:683
  15.6 0.0 copy-done.5
  15.6 0.0 copy-start.6
  15.6 0.0 copy-start.7
  15.6 1.4 %shard_map.93 = (bf16[8,128,128]{2,1,0:T(8,128)(2,1)S(1)}, bf16[8,128,128]{2,1,0:T(8,128)(2,1)S(1)}) custom-call(bf16[592,128]{1,0:T(8,128)(2,1)S(1)} %collective-permute-done.a_ref, bf16[592,128]{1,0:T(8,128)(2,1)S(1)} %collective-permute-done.1.b_ref, f32[16,512]{1,0:T(8,128)S(1)} %copy-done.5, bf16[2,1024,256]{2,1,0:T(8,128)(2,1)S(1)} %get-tuple-element.32.edge_high, ...), custom_call_target="tpu_custom_call" | custom-call | flops 2147483648 | bytes 1024 | tf_op jit(solution)/shard_map/pallas_call | solution.py:593
  17.0 0.5 collective-permute-done.3.refs_0_
  17.5 0.0 copy-done.6
  17.5 0.0 copy-done.7
  17.5 0.0 copy-start.2
  17.5 0.0 copy-start.3
  17.5 2.9 %shard_map.95 = (bf16[128,1024]{1,0:T(8,128)(2,1)S(1)}, bf16[128,1024]{1,0:T(8,128)(2,1)S(1)}) custom-call(bf16[8,128,256]{2,1,0:T(8,128)(2,1)S(1)} %get-tuple-element.31.middle_ref.refs_0_, bf16[8,128,128]{2,1,0:T(8,128)(2,1)S(1)} %get-tuple-element.42.left_ref.refs_2_, bf16[8,128,128]{2,1,0:T(8,128)(2,1)S(1)} %get-tuple-element.43.right_ref.refs_4_, ...), custom_call_target="tpu_custom_call" | custom-call | flops 3221225472 | bytes 1024 | tf_op jit(solution)/shard_map/pallas_call | solution.py:593
  20.3 0.8 %collective-permute-start.4 = (bf16[128,1024]{1,0:T(8,128)(2,1)S(1)}, bf16[128,1024]{1,0:T(8,128)(2,1)S(1)}, u32[]{:S(2)}, u32[]{:S(2)}) collective-permute-start(bf16[128,1024]{1,0:T(8,128)(2,1)S(1)} %get-tuple-element.40), channel_id=1, source_target_pairs={{1,2},{2,1},{3,4},{4,3},{5,6},{6,5},{7,8},{8,7},{9,10},{10,9},{11,... | collective-permute-start | bytes 786440 | tf_op jit(solution)/shard_map/ppermute | solution.py:703
  21.1 0.0 collective-permute-start.5
  21.2 0.0 copy-done.2
  21.2 0.0 copy-done.3
  21.2 1.7 %shard_map.94 = (bf16[128,1024]{1,0:T(8,128)(2,1)S(1)}, f32[8,1024]{1,0:T(8,128)S(1)}, f32[8,1024]{1,0:T(8,128)S(1)}) custom-call(bf16[8,128,256]{2,1,0:T(8,128)(2,1)S(1)} %get-tuple-element.31.middle_ref.refs_0_, bf16[8,128,128]{2,1,0:T(8,128)(2,1)S(1)} %get-tuple-element.42.left_ref.refs_2_, bf16[8,128,128]{2,1,0:T(8,128)(2,1)S(1)} %get-tuple-element.43.right_ref.refs_4_, ...), custom_call_target="tpu_custom_call" | custom-call | flops 2147483648 | bytes 1024 | tf_op jit(solution)/shard_map/pallas_call | solution.py:593
  22.9 6.0 %collective-permute-done.4.a_ref = bf16[128,1024]{1,0:T(8,128)(2,1)S(1)} collective-permute-done((bf16[128,1024]{1,0:T(8,128)(2,1)S(1)}, bf16[128,1024]{1,0:T(8,128)(2,1)S(1)}, u32[]{:S(2)}, u32[]{:S(2)}) %collective-permute-start.4) | collective-permute-done | bytes 262176 | tf_op jit(solution)/shard_map/ppermute | solution.py:703
  28.9 0.0 collective-permute-done.5.b_ref
  28.9 0.2 collective-permute-done.2.refs_0_.refs_1_
  29.1 0.1 shard_map.96.refs_0_
  29.2 1.5 %collective-permute-start.8 = (bf16[128,1024]{1,0:T(8,128)(2,1)S(1)}, bf16[128,1024]{1,0:T(8,128)(2,1)S(1)}, u32[]{:S(2)}, u32[]{:S(2)}) collective-permute-start(bf16[128,1024]{1,0:T(8,128)(2,1)S(1)} %shard_map.96.refs_0_), channel_id=1, source_target_pairs={{16,0},{0,16},{17,1},{1,17},{18,2},{2,18},{19,3},{3,19},{20,4},{4,... | collective-permute-start | bytes 786440 | tf_op jit(solution)/shard_map/ppermute | solution.py:734
  30.8 0.5 %collective-permute-start.6 = (bf16[8,128,128]{2,1,0:T(8,128)(2,1)S(1)}, bf16[8,128,128]{2,1,0:T(8,128)(2,1)S(1)}, u32[]{:S(2)}, u32[]{:S(2)}) collective-permute-start(bf16[8,128,128]{2,1,0:T(8,128)(2,1)S(1)} %get-tuple-element.42.left_ref.refs_2_), channel_id=1, source_target_pairs={{16,0},{0,16},{17,1},{1,17},{18,2},{2,18},{19,3},{3,19},{20,4},{4,... | collective-permute-start | bytes 786440 | tf_op jit(solution)/shard_map/ppermute | solution.py:732
  31.3 1.5 %collective-permute-start.7 = (bf16[8,128,128]{2,1,0:T(8,128)(2,1)S(1)}, bf16[8,128,128]{2,1,0:T(8,128)(2,1)S(1)}, u32[]{:S(2)}, u32[]{:S(2)}) collective-permute-start(bf16[8,128,128]{2,1,0:T(8,128)(2,1)S(1)} %get-tuple-element.43.right_ref.refs_4_), channel_id=1, source_target_pairs={{16,0},{0,16},{17,1},{1,17},{18,2},{2,18},{19,3},{3,19},{20,4},{4,... | collective-permute-start | bytes 786440 | tf_op jit(solution)/shard_map/ppermute | solution.py:733
  32.8 5.7 %collective-permute-done.8.refs_1_ = bf16[128,1024]{1,0:T(8,128)(2,1)S(1)} collective-permute-done((bf16[128,1024]{1,0:T(8,128)(2,1)S(1)}, bf16[128,1024]{1,0:T(8,128)(2,1)S(1)}, u32[]{:S(2)}, u32[]{:S(2)}) %collective-permute-start.8) | collective-permute-done | bytes 262176 | tf_op jit(solution)/shard_map/ppermute | solution.py:734
  38.6 7.4 %shard_map.97.refs_6_ = bf16[8,128,256]{2,1,0:T(8,128)(2,1)S(1)} custom-call(bf16[128,1024]{1,0:T(8,128)(2,1)S(1)} %shard_map.96.refs_0_, bf16[128,1024]{1,0:T(8,128)(2,1)S(1)} %collective-permute-done.8.refs_1_, f32[8,1024]{1,0:T(8,128)S(1)} %get-tuple-element.45.refs_2_, f32[8,1024]{1,0:T(8,128)S(1)} %get-tuple-element.46.refs_3_), custom_call_target="tpu_custom_call" | custom-call | flops 8589934592 | bytes 1024 | tf_op jit(solution)/shard_map/pallas_call | solution.py:593
  46.0 0.0 collective-permute-done.6.refs_3_
  46.0 2.1 %collective-permute-done.7.refs_5_ = bf16[8,128,128]{2,1,0:T(8,128)(2,1)S(1)} collective-permute-done((bf16[8,128,128]{2,1,0:T(8,128)(2,1)S(1)}, bf16[8,128,128]{2,1,0:T(8,128)(2,1)S(1)}, u32[]{:S(2)}, u32[]{:S(2)}) %collective-permute-start.7) | collective-permute-done | bytes 262176 | tf_op jit(solution)/shard_map/ppermute | solution.py:733
  48.2 2.6 %shard_map.98 = bf16[128,8,512]{2,1,0:T(8,128)(2,1)} custom-call(bf16[8,128,256]{2,1,0:T(8,128)(2,1)S(1)} %get-tuple-element.31.middle_ref.refs_0_, bf16[8,128,256]{2,1,0:T(8,128)(2,1)S(1)} %collective-permute-done.2.refs_0_.refs_1_, bf16[8,128,128]{2,1,0:T(8,128)(2,1)S(1)} %get-tuple-element.42.left_ref.refs_2_, ...), custom_call_target="tpu_custom_call" | custom-call | flops 3221225472 | bytes 1024 | tf_op jit(solution)/shard_map/pallas_call | solution.py:593
  (3 shorter events, 0.0 us)
Async XLA Ops:
  2.2 11.3 %collective-permute-start = (bf16[592,128]{1,0:T(8,128)(2,1)}, bf16[592,128]{1,0:T(8,128)(2,1)S(1)}, u32[]{:S(2)}, u32[]{:S(2)}) collective-permute-start(bf16[592,128]{1,0:T(8,128)(2,1)} %get-tuple-element.28), channel_id=1, source_target_pairs={{1,2},{2,1},{3,4},{4,3},{5,6},{6,5},{7,8},{8,7},{9,10},{10,9},{11,... | collective-permute-start | bytes 454664 | tf_op jit(solution)/shard_map/ppermute | solution.py:657
  7.7 5.8 %collective-permute-start.1 = (bf16[592,128]{1,0:T(8,128)(2,1)}, bf16[592,128]{1,0:T(8,128)(2,1)S(1)}, u32[]{:S(2)}, u32[]{:S(2)}) collective-permute-start(bf16[592,128]{1,0:T(8,128)(2,1)} %get-tuple-element.29), channel_id=1, source_target_pairs={{0,1},{1,0},{2,3},{3,2},{4,5},{5,4},{6,7},{7,6},{8,9},{9,8},{10,11... | collective-permute-start | bytes 454664 | tf_op jit(solution)/shard_map/ppermute | solution.py:656
  7.7 1.6 %copy-start = (f32[128,8,512]{2,1,0:T(8,128)S(1)}, f32[128,8,512]{2,1,0:T(8,128)}, u32[]{:S(2)}) copy-start(f32[128,8,512]{2,1,0:T(8,128)} %param.9) | copy-start | bytes 6291460
  9.3 0.8 %copy-start.4 = (f32[16,512]{1,0:T(8,128)S(1)}, f32[16,512]{1,0:T(8,128)}, u32[]{:S(2)}) copy-start(f32[16,512]{1,0:T(8,128)} %get-tuple-element.26.refs_4_.small_ref) | copy-start | bytes 98308
  10.1 3.4 %copy-start.1 = (bf16[48,128]{1,0:T(8,128)(2,1)S(1)}, bf16[48,128]{1,0:T(8,128)(2,1)}, u32[]{:S(2)}) copy-start(bf16[48,128]{1,0:T(8,128)(2,1)} %get-tuple-element.30.lists_ref) | copy-start | bytes 36868
  10.1 5.6 %copy-start.5 = (f32[16,512]{1,0:T(8,128)S(1)}, f32[16,512]{1,0:T(8,128)}, u32[]{:S(2)}) copy-start(f32[16,512]{1,0:T(8,128)} %get-tuple-element.26.refs_4_.small_ref) | copy-start | bytes 98308
  13.5 3.9 %collective-permute-start.3 = (bf16[112,128]{1,0:T(8,128)(2,1)S(1)}, bf16[112,128]{1,0:T(8,128)(2,1)S(1)}, u32[]{:S(2)}, u32[]{:S(2)}) collective-permute-start(bf16[112,128]{1,0:T(8,128)(2,1)S(1)} %pad_maximum_fusion), channel_id=1, source_target_pairs={{16,0},{0,16},{17,1},{1,17},{18,2},{2,18},{19,3},{3,19},{20,4},{4,... | collective-permute-start | bytes 86024 | tf_op jit(solution)/shard_map/ppermute | solution.py:684
  15.1 14.1 %collective-permute-start.2 = (bf16[8,128,256]{2,1,0:T(8,128)(2,1)S(1)}, bf16[8,128,256]{2,1,0:T(8,128)(2,1)S(1)}, u32[]{:S(2)}, u32[]{:S(2)}) collective-permute-start(bf16[8,128,256]{2,1,0:T(8,128)(2,1)S(1)} %get-tuple-element.31.middle_ref.refs_0_), channel_id=1, source_target_pairs={{16,0},{0,16},{17,1},{1,17},{18,2},{2,18},{19,3},{3,19},{20,4},{4,... | collective-permute-start | bytes 1572872 | tf_op jit(solution)/shard_map/ppermute | solution.py:683
  15.6 1.8 %copy-start.6 = (s32[2048]{0:T(1024)S(1)}, s32[2048]{0:T(1024)}, u32[]{:S(2)}) copy-start(s32[2048]{0:T(1024)} %param.12) | copy-start | bytes 24580
  15.6 1.8 %copy-start.7 = (s32[2048]{0:T(1024)S(1)}, s32[2048]{0:T(1024)}, u32[]{:S(2)}) copy-start(s32[2048]{0:T(1024)} %param.13) | copy-start | bytes 24580
  17.5 3.7 %copy-start.2 = (f32[32768]{0:T(1024)S(1)}, f32[32768]{0:T(1024)}, u32[]{:S(2)}) copy-start(f32[32768]{0:T(1024)} %param.14) | copy-start | bytes 393220
  17.5 3.7 %copy-start.3 = (f32[32768]{0:T(1024)S(1)}, f32[32768]{0:T(1024)}, u32[]{:S(2)}) copy-start(f32[32768]{0:T(1024)} %param.15) | copy-start | bytes 393220
  20.3 8.6 %collective-permute-start.4 = (bf16[128,1024]{1,0:T(8,128)(2,1)S(1)}, bf16[128,1024]{1,0:T(8,128)(2,1)S(1)}, u32[]{:S(2)}, u32[]{:S(2)}) collective-permute-start(bf16[128,1024]{1,0:T(8,128)(2,1)S(1)} %get-tuple-element.40), channel_id=1, source_target_pairs={{1,2},{2,1},{3,4},{4,3},{5,6},{6,5},{7,8},{8,7},{9,10},{10,9},{11,... | collective-permute-start | bytes 786440 | tf_op jit(solution)/shard_map/ppermute | solution.py:703
  21.1 7.8 %collective-permute-start.5 = (bf16[128,1024]{1,0:T(8,128)(2,1)S(1)}, bf16[128,1024]{1,0:T(8,128)(2,1)S(1)}, u32[]{:S(2)}, u32[]{:S(2)}) collective-permute-start(bf16[128,1024]{1,0:T(8,128)(2,1)S(1)} %get-tuple-element.41), channel_id=1, source_target_pairs={{0,1},{1,0},{2,3},{3,2},{4,5},{5,4},{6,7},{7,6},{8,9},{9,8},{10,11... | collective-permute-start | bytes 786440 | tf_op jit(solution)/shard_map/ppermute | solution.py:704
  29.2 9.3 %collective-permute-start.8 = (bf16[128,1024]{1,0:T(8,128)(2,1)S(1)}, bf16[128,1024]{1,0:T(8,128)(2,1)S(1)}, u32[]{:S(2)}, u32[]{:S(2)}) collective-permute-start(bf16[128,1024]{1,0:T(8,128)(2,1)S(1)} %shard_map.96.refs_0_), channel_id=1, source_target_pairs={{16,0},{0,16},{17,1},{1,17},{18,2},{2,18},{19,3},{3,19},{20,4},{4,... | collective-permute-start | bytes 786440 | tf_op jit(solution)/shard_map/ppermute | solution.py:734
  30.8 15.2 %collective-permute-start.6 = (bf16[8,128,128]{2,1,0:T(8,128)(2,1)S(1)}, bf16[8,128,128]{2,1,0:T(8,128)(2,1)S(1)}, u32[]{:S(2)}, u32[]{:S(2)}) collective-permute-start(bf16[8,128,128]{2,1,0:T(8,128)(2,1)S(1)} %get-tuple-element.42.left_ref.refs_2_), channel_id=1, source_target_pairs={{16,0},{0,16},{17,1},{1,17},{18,2},{2,18},{19,3},{3,19},{20,4},{4,... | collective-permute-start | bytes 786440 | tf_op jit(solution)/shard_map/ppermute | solution.py:732
  31.3 16.8 %collective-permute-start.7 = (bf16[8,128,128]{2,1,0:T(8,128)(2,1)S(1)}, bf16[8,128,128]{2,1,0:T(8,128)(2,1)S(1)}, u32[]{:S(2)}, u32[]{:S(2)}) collective-permute-start(bf16[8,128,128]{2,1,0:T(8,128)(2,1)S(1)} %get-tuple-element.43.right_ref.refs_4_), channel_id=1, source_target_pairs={{16,0},{0,16},{17,1},{1,17},{18,2},{2,18},{19,3},{3,19},{20,4},{4,... | collective-permute-start | bytes 786440 | tf_op jit(solution)/shard_map/ppermute | solution.py:733

commit v3 on v2

--- a/solution.py
+++ b/solution.py
@@ -157,9 +157,8 @@
 
 def middle_kernel(*refs, groups):
     field_refs = refs[:groups]
+    small_ref, middle_ref, kept_ref = refs[groups : groups + 3]
     (
-        small_ref,
-        out_ref,
         edge_high,
         edge_low,
         part_ref,
@@ -170,8 +169,10 @@
         first_low,
         second_high,
         second_low,
-    ) = refs[groups:]
-    levels, members, middle = out_ref.shape
+    ) = refs[groups + 3 :]
+    late, members, _ = kept_ref.shape
+    levels = 2 * late
+    early = (groups - 2) * levels - late
     columns = groups * LANES
     coef = padded(small_ref[0:6, :], 2)
     reach = padded(small_ref[8:14, :], 2)
@@ -229,14 +230,19 @@
             ref[1, spot, 0:LANES] = jnp.where(lane < 64, turned[2], turned[3]).astype(BF16)
             ref[1, spot, LANES:] = jnp.where(lane < 64, turned[3], zero).astype(BF16)
     result = dot3((u_high[...], u_low[...]), both)
-    for level in range(levels):
-        out_ref[level] = result[level * members : (level + 1) * members, :].astype(BF16)
+    for k in range((groups - 2) * levels):
+        level, lane = k % levels, (k // levels) * LANES
+        value = result[level * members : (level + 1) * members, lane : lane + LANES].astype(BF16)
+        if k < early:
+            middle_ref[k] = value
+        else:
+            kept_ref[k - early] = value
 
 
 def edge_kernel(
-    a_ref, b_ref, small_ref, edge_high, edge_low, part_ref, second_ref, left_ref, right_ref, u_high
+    a_ref, b_ref, small_ref, edge_high, edge_low, part_ref, second_ref, kept_ref, first_ref, next_ref, last_ref, u_high
 ):
-    levels, members, _ = left_ref.shape
+    levels, members, _ = next_ref.shape
     columns = small_ref.shape[1]
     half = members // 2
     rows = message_rows(levels * half)
@@ -296,15 +302,35 @@
                     u_high[k, spot, LANES:] = jnp.where(lane < 64, own, pair[j]).astype(BF16)
                     u_high[k, spot, 0:LANES] = edge_high[k, spot, 0:LANES]
         result = dot3((u_high[k], edge_low[k]), operators[k])
-        out_ref = (left_ref, right_ref)[k]
+        part = levels // 2
+        if k == 0:
+            first_ref[:part] = kept_ref[...]
         for level in range(levels):
-            out_ref[level] = result[level * members : (level + 1) * members, :].astype(BF16)
+            value = result[level * members : (level + 1) * members, :].astype(BF16)
+            if k == 0 and level < part:
+                first_ref[part + level] = value
+            elif k == 0:
+                next_ref[level - part] = value
+            elif level < part:
+                next_ref[part + level] = value
+            else:
+                last_ref[level - part] = value
 
 
 def gather_lists(parts, blocks):
-    return jnp.concatenate(
-        [part[b : b + 1, :].astype(F32) for part in parts for b in range(blocks)], axis=1
-    )
+    count = len(parts)
+    me = lax.axis_index("mem")
+    rows = [
+        jnp.concatenate([part[b : b + 1, :].astype(F32) for b in range(blocks)], axis=1)
+        for part in parts
+    ]
+    placed = []
+    for place in range(count):
+        value = rows[0]
+        for shift in range(1, count):
+            value = jnp.where((me + shift) % count == place, rows[shift], value)
+        placed.append(value)
+    return jnp.concatenate(placed, axis=1)
 
 
 def read_places(table_ref, slot):
@@ -329,55 +355,69 @@
     table[32:48, :] = (cell % 16).astype(F32).astype(BF16)
 
 
-def read_forecast(fields, level, column, out_ref, lane):
+def read_forecast(field, level, column, out_ref, lane):
     members = out_ref.shape[0]
     wide = level.shape[1]
-    middle, left, right = fields
-    inner = middle.shape[1]
-    inside = (column >= LANES) & (column < LANES + inner)
-    spot = jnp.where(inside, column - LANES, -1)
-    one = jnp.where(iota((inner, wide), 0) == spot, 1.0, 0.0).astype(BF16)
-    found = dot(middle, one)
-    spot = jnp.where(column < LANES, column, column - inner)
-    spot = jnp.where(inside, -1, spot)
-    one = jnp.where(iota((2 * LANES, wide), 0) == spot, 1.0, 0.0).astype(BF16)
-    found = found + dot(jnp.concatenate([left, right], axis=1), one)
+    one = jnp.where(iota((field.shape[1], wide), 0) == column, 1.0, 0.0).astype(BF16)
+    found = dot(field, one)
     total = jnp.zeros((members, wide), F32)
-    for l in range(middle.shape[0] // members):
+    for l in range(field.shape[0] // members):
         total = total + jnp.where(level == l, found[l * members : (l + 1) * members, :], 0.0)
     out_ref[:, lane : lane + wide] = total.astype(BF16)
 
 
-def neighbour_kernel(middle_ref, left_ref, right_ref, a_ref, b_ref, *refs, others, blocks):
-    other_refs = refs[:others]
-    cell_ref, level_ref, ra_ref, rb_ref, table = refs[others:]
-    half = a_ref.shape[0] - 80
+def whole(middle_ref, first_ref, next_ref, last_ref):
+    part, members, _ = last_ref.shape
+    middle = jnp.concatenate([middle_ref[...], first_ref[:part]], axis=0)
+    groups = [
+        jnp.concatenate([first_ref[part:], next_ref[:part]], axis=0),
+        *(middle[k : k + 2 * part] for k in range(0, middle.shape[0], 2 * part)),
+        jnp.concatenate([next_ref[part:], last_ref[...]], axis=0),
+    ]
+    return joined([group.reshape(-1, LANES) for group in groups])
+
+
+def neighbour_kernel(*refs, others, blocks, turn):
+    message_ref = refs[4]
+    other_refs = refs[5 : 5 + others]
+    cell_ref, level_ref = refs[5 + others : 7 + others]
+    out_ref, table = refs[-2:]
+    half = message_ref.shape[0] - 80
     rows = message_rows(half)
     odd = is_odd_tile()
     obs = 16 * LANES
     make_table(cell_ref, level_ref, table)
-    fields = [ref[...].reshape(-1, ref.shape[2]) for ref in (middle_ref, left_ref, right_ref)]
-    for turn, (ref, out_ref) in enumerate(((a_ref, ra_ref), (b_ref, rb_ref))):
-        base = 32 * turn
-        parts = [ref[rows["list_high"] : rows["list_high"] + 32, :]]
-        parts += [r[base : base + 32, :] for r in other_refs]
-        high = gather_lists([part[:16, :] for part in parts], blocks)
-        low = gather_lists([part[16:, :] for part in parts], blocks)
-        index = (high * 64.0 + low).astype(jnp.int32)
-        skip = jnp.where(odd, 0, 2 * obs) if turn == 0 else jnp.where(odd, 2 * obs, 0)
-        level, column = read_places(table, index - skip)
-        for lane in range(0, index.shape[1], 256):
-            read_forecast(
-                fields, level[:, lane : lane + 256], column[:, lane : lane + 256], out_ref, lane
-            )
-
-
-def own_kernel(middle_ref, left_ref, right_ref, lists_ref, *refs, others, blocks, tiles):
-    other_refs = refs[:others]
-    cell_ref, level_ref, value_ref, rinv_ref, r_ref, weight_ref, target_ref, table = refs[others:]
+    field = whole(*refs[:4])
+    base = 32 * turn
+    parts = [message_ref[rows["list_high"] : rows["list_high"] + 32, :]]
+    parts += [r[base : base + 32, :] for r in other_refs]
+    high = gather_lists([part[:16, :] for part in parts], blocks)
+    low = gather_lists([part[16:, :] for part in parts], blocks)
+    index = (high * 64.0 + low).astype(jnp.int32)
+    skip = jnp.where(odd, 0, 2 * obs) if turn == 0 else jnp.where(odd, 2 * obs, 0)
+    level, column = read_places(table, index - skip)
+    for lane in range(0, index.shape[1], 256):
+        read_forecast(
+            field, level[:, lane : lane + 256], column[:, lane : lane + 256], out_ref, lane
+        )
+
+
+def own_kernel(*refs, others, blocks, tiles):
+    lists_ref = refs[4]
+    other_refs = refs[5 : 5 + others]
+    (
+        cell_ref,
+        level_ref,
+        value_ref,
+        rinv_ref,
+        r_ref,
+        weight_ref,
+        target_ref,
+        table,
+    ) = refs[5 + others :]
     obs = 16 * LANES
     make_table(cell_ref, level_ref, table)
-    fields = [ref[...].reshape(-1, ref.shape[2]) for ref in (middle_ref, left_ref, right_ref)]
+    field = whole(*refs[:4])
 
     parts = [lists_ref[...]] + [r[64:112, :] for r in other_refs]
     passed = [gather_lists([part[16 * k : 16 * k + 16, :] for part in parts], blocks) for k in range(3)]
@@ -386,7 +426,7 @@
     wide = index.shape[1]
     level, column = read_places(table, index - obs)
     for lane in range(0, wide, 256):
-        read_forecast(fields, level[:, lane : lane + 256], column[:, lane : lane + 256], r_ref, lane)
+        read_forecast(field, level[:, lane : lane + 256], column[:, lane : lane + 256], r_ref, lane)
 
     tile = lax.axis_index("tile")
     starts = [((tile + tiles + shift) % tiles) * 16 for shift in (-1, 0, 1)]
@@ -427,18 +467,14 @@
 
 def weights_kernel(*refs, others):
     r_refs = refs[: others + 1]
-    weight_ref, target_ref, out_ref, pert, weighted, turned, gram_right, hat, inner, outer = refs[others + 1 :]
+    weight_ref, target_ref = refs[others + 1 : others + 3]
+    out_ref, pert, weighted, turned, gram_right, hat, inner, outer = refs[-8:]
     members, wide = r_refs[0].shape
     blocks = wide // LANES
-    share = blocks // (others + 1)
     ensemble = members * (others + 1)
     free = ensemble - 1.0
 
-    parts = [r_refs[0][...].astype(F32)]
-    for k in range(others):
-        other = r_refs[k + 1][...].astype(F32)
-        turn = ((k + 1) * share * LANES) % wide
-        parts.append(jnp.concatenate([other[:, wide - turn :], other[:, : wide - turn]], axis=1))
+    parts = [ref[...].astype(F32) for ref in r_refs]
     total = sum(jnp.sum(part, axis=0, keepdims=True) for part in parts)
     mean = total * (1.0 / ensemble)
     weight = weight_ref[0:1, :]
@@ -479,44 +515,35 @@
     for b in range(blocks):
         inner[b] = inners[b]
         hat[b] = spread(xs[b]) + product(joined(split2(inners[b])), gram_right[b])
-        outer[b] = spread(jnp.full((1, LANES), -0.5, F32))
-
-    def step(_, carry):
-        xs, zs = carry
-        next_xs, next_zs = [], []
-        for base in range(0, blocks, 8):
-            group = range(base, min(base + 8, blocks))
-            lefts, halves = {}, {}
-            for b in group:
-                x, z = xs[b], zs[b]
-                factor = spread(jnp.full((1, LANES), 1.5, F32)) - 0.5 * hat[b]
-                f_high, f_low = split2(factor)
-                lefts[b] = joined((f_high, f_low))
-                inside = inner[b]
-                i_high, i_low = split2(inside)
-                o_high, o_low = split2(outer[b])
-                right_high = joined((i_high, o_high))
-                both = dot(lefts[b], jnp.concatenate([right_high, right_high], axis=0)) + dot(
-                    f_high, joined((i_low, o_low))
-                )
-                halves[b] = both[:, :LANES] - (0.5 * x) * inside
-                outer[b] = both[:, LANES:] - (0.5 * z) * inside
-            for b in group:
-                x, z = xs[b], zs[b]
-                m = 1.5 - 0.5 * x
-                v = m * x
-                inner[b] = product(lefts[b], doubled(*split2(halves[b]))) - (0.5 * v) * inner[b]
-            for b in group:
-                x, z = xs[b], zs[b]
-                m = 1.5 - 0.5 * x
-                x = m * m * x
-                hat[b] = spread(x) + product(joined(split2(inner[b])), gram_right[b])
-                next_xs.append(x)
-                next_zs.append(m * z)
-        return tuple(next_xs), tuple(next_zs)
-
-    xs, zs = lax.fori_loop(1, NS_ITERS - 1, step, (tuple(xs), tuple(zs)))
-    zs = list(zs)
+
+    for turn in range(1, NS_ITERS - 1):
+        lefts, halves = [], []
+        for b in range(blocks):
+            x, z = xs[b], zs[b]
+            factor = spread(jnp.full((1, LANES), 1.5, F32)) - 0.5 * hat[b]
+            f_high, f_low = split2(factor)
+            lefts.append(joined((f_high, f_low)))
+            inside = inner[b]
+            if turn == 1:
+                halves.append(product(lefts[b], doubled(*split2(inside))) - (0.5 * x) * inside)
+                outer[b] = -0.5 * factor - (0.5 * z) * inside
+                continue
+            i_high, i_low = split2(inside)
+            o_high, o_low = split2(outer[b])
+            right_high = joined((i_high, o_high))
+            both = dot(lefts[b], jnp.concatenate([right_high, right_high], axis=0)) + dot(
+                f_high, joined((i_low, o_low))
+            )
+            halves.append(both[:, :LANES] - (0.5 * x) * inside)
+            outer[b] = both[:, LANES:] - (0.5 * z) * inside
+        for b in range(blocks):
+            m = 1.5 - 0.5 * xs[b]
+            inner[b] = product(lefts[b], doubled(*split2(halves[b]))) - (0.5 * m * xs[b]) * inner[b]
+        for b in range(blocks):
+            m = 1.5 - 0.5 * xs[b]
+            xs[b] = m * m * xs[b]
+            zs[b] = m * zs[b]
+            hat[b] = spread(xs[b]) + product(joined(split2(inner[b])), gram_right[b])
 
     own = iota((members, ensemble), 0) == iota((members, ensemble), 1)
     lasts, rights, rows, cores = [], [], [], []
@@ -546,39 +573,78 @@
         out_ref[b] = (found[:members, :] + found[members : members + 1, :] + diagonal).astype(BF16)
 
 
+def updated(left, parts, width):
+    members = parts[0].shape[0]
+    parts = [part.astype(F32) for part in parts]
+    total = sum(jnp.sum(part, axis=0, keepdims=True) for part in parts)
+    mean = total * (1.0 / (members * len(parts)))
+    found = dot(left, jnp.concatenate([(part - mean).astype(BF16) for part in parts], axis=0))
+    result = found[:members, :]
+    lane = iota(result.shape, 1)
+    for k in range(1, LANES // width):
+        result = jnp.where(lane < k * width, result, found[k * members : (k + 1) * members, :])
+    return result + mean
+
+
+def weights_of(weight_ref, group, columns):
+    per = weight_ref.shape[0] * LANES // columns
+    return jnp.concatenate([weight_ref[group * per + k] for k in range(per)], axis=0)
+
+
 def update_kernel(*refs, others):
-    middle_refs = refs[: others + 1]
-    left_refs = refs[others + 1 : 2 * others + 2]
-    right_refs = refs[2 * others + 2 : 3 * others + 3]
-    weight_ref, out_ref, stage = refs[3 * others + 3 :]
-    members, levels, columns = out_ref.shape
+    count = others + 1
+    middles, firsts, afters = [refs[k * count : (k + 1) * count] for k in range(3)]
+    weight_ref, out_hbm, rest_ref, stage, done, sems = refs[3 * count :]
+    members, levels, columns = out_hbm.shape
+    width = columns // weight_ref.shape[0]
+    part = levels // 2
     groups = columns // LANES
-    blocks = weight_ref.shape[0]
-    width = columns // blocks
-    per = LANES // width
-    ensemble = members * (others + 1)
-    first = lax.axis_index("mem") * (blocks // (others + 1))
-    lane = iota((members, LANES), 1)
-    for group in range(groups):
-        if group in (0, groups - 1):
-            field_refs, start = (left_refs if group == 0 else right_refs), 0
-        else:
-            field_refs, start = middle_refs, (group - 1) * LANES
-        lanes = slice(start, start + LANES)
-        left = jnp.concatenate(
-            [weight_ref[(group * per + k + blocks - first) % blocks] for k in range(per)], axis=0
+    copies = []
+    for group in (*range(1, groups - 1), 0):
+        left = weights_of(weight_ref, group, columns)
+        for level in range(levels):
+            place = (group - 1) * levels + level
+            if group == groups - 2 and level >= part:
+                parts = [ref[level - part] for ref in firsts]
+            elif group:
+                parts = [ref[place] for ref in middles]
+            elif level < part:
+                parts = [ref[part + level] for ref in firsts]
+            else:
+                parts = [ref[level - part] for ref in afters]
+            stage[group, pl.ds(level, members, stride=levels), :] = updated(left, parts, width)
+        done[group] = stage[group].reshape(members, levels, LANES).astype(BF16)
+        lanes = slice(group * LANES, (group + 1) * LANES)
+        copies.append(pltpu.make_async_copy(done.at[group], out_hbm.at[:, :, lanes], sems.at[group]))
+        copies[-1].start()
+    left = weights_of(weight_ref, groups - 1, columns)
+    for level in range(part):
+        rest_ref[pl.ds(level, members, stride=levels), :] = updated(
+            left, [ref[part + level] for ref in afters], width
         )
-        for level in range(levels):
-            parts = [ref[level, :, lanes].astype(F32) for ref in field_refs]
-            total = sum(jnp.sum(part, axis=0, keepdims=True) for part in parts)
-            mean = total * (1.0 / ensemble)
-            moved = jnp.concatenate([(part - mean).astype(BF16) for part in parts], axis=0)
-            found = dot(left, moved)
-            result = found[:members, :]
-            for k in range(1, per):
-                result = jnp.where(lane < k * width, result, found[k * members : (k + 1) * members, :])
-            stage[group, pl.ds(level, members, stride=levels), :] = result + mean
-        out_ref[:, :, group * LANES : (group + 1) * LANES] = stage[group].reshape(members, levels, LANES).astype(BF16)
+    for level in range(part, levels):
+        rest_ref[pl.ds(level, members, stride=levels), :] = jnp.zeros((members, LANES), F32)
+    for copy in copies:
+        copy.wait()
+
+
+def finish_kernel(*refs, others):
+    count = others + 1
+    lasts = refs[:count]
+    weight_ref, rest_ref, _, out_hbm, stage, done, sem = refs[count:]
+    members, levels, columns = out_hbm.shape
+    width = columns // weight_ref.shape[0]
+    part = levels // 2
+    left = weights_of(weight_ref, columns // LANES - 1, columns)
+    stage[...] = rest_ref[...]
+    for level in range(part):
+        stage[pl.ds(part + level, members, stride=levels), :] = updated(
+            left, [ref[level] for ref in lasts], width
+        )
+    done[...] = stage[...].reshape(members, levels, LANES).astype(BF16)
+    copy = pltpu.make_async_copy(done, out_hbm.at[:, :, columns - LANES : columns], sem)
+    copy.start()
+    copy.wait()
 
 
 def vmem():
@@ -589,14 +655,15 @@
     return pl.BlockSpec((rows, LANES), lambda i: (0, group))
 
 
-def call(kernel, outs, inputs, scratch=(), in_specs=None, cost=0, limit=VMEM_LIMIT):
+def call(kernel, outs, inputs, scratch=(), in_specs=None, out_specs=None, aliases=None, cost=0, limit=VMEM_LIMIT):
     return pl.pallas_call(
         kernel,
         grid=(1,),
         out_shape=outs,
         in_specs=in_specs or [vmem()] * len(inputs),
-        out_specs=[vmem()] * len(outs),
+        out_specs=out_specs or [vmem()] * len(outs),
         scratch_shapes=list(scratch),
+        input_output_aliases=aliases or {},
         compiler_params=pltpu.CompilerParams(vmem_limit_bytes=limit),
         cost_estimate=pl.CostEstimate(flops=cost << 30, bytes_accessed=1 << 10, transcendentals=0),
     )(*inputs)
@@ -656,11 +723,11 @@
     from_b = lax.ppermute(b, "tile", even_pairs)
     from_a = lax.ppermute(a, "tile", odd_pairs)
     flat_rows = members * levels
-    middle = columns - 2 * LANES
-    forecast, edge_high, edge_low, part, second = call(
+    middle, kept, edge_high, edge_low, part, second = call(
         functools.partial(middle_kernel, groups=groups),
         [
-            jax.ShapeDtypeStruct((levels, members, middle), BF16),
+            jax.ShapeDtypeStruct(((groups - 2) * levels - levels // 2, members, LANES), BF16),
+            jax.ShapeDtypeStruct((levels // 2, members, LANES), BF16),
             jax.ShapeDtypeStruct((2, flat_rows, 2 * LANES), BF16),
             jax.ShapeDtypeStruct((2, flat_rows, 2 * LANES), BF16),
             jax.ShapeDtypeStruct((2, 2 * LANES, LANES), F32),
@@ -672,34 +739,52 @@
             pltpu.VMEM((flat_rows, columns), BF16),
             pltpu.VMEM((columns, columns - LANES), BF16),
             pltpu.VMEM((columns, columns - LANES), BF16),
-            pltpu.VMEM((columns - LANES, middle), BF16),
-            pltpu.VMEM((columns - LANES, middle), BF16),
+            pltpu.VMEM((columns - LANES, columns - 2 * LANES), BF16),
+            pltpu.VMEM((columns - LANES, columns - 2 * LANES), BF16),
         ],
         in_specs=[group_spec(flat_rows, group) for group in range(groups)] + [vmem()],
         cost=4,
     )
     passed = jnp.concatenate([from_a[half + 48 :], from_b[half + 48 :], lists], axis=0)
-    passed, sent = lax.optimization_barrier((passed, forecast))
-    forecasts = [forecast] + [lax.ppermute(sent, "mem", turn) for turn in turns]
+
+    def swapped(value, sent):
+        return [value] + [lax.ppermute(sent, "mem", turn) for turn in turns]
+
+    passed, sent = lax.optimization_barrier((passed, middle))
+    middles = swapped(middle, sent)
     passed = [lax.ppermute(passed, "mem", turn) for turn in turns]
-    left, right = call(
+    first, after, last = call(
         edge_kernel,
-        [jax.ShapeDtypeStruct((levels, members, LANES), BF16)] * 2,
-        [from_a, from_b, small, edge_high, edge_low, part, second],
+        [
+            jax.ShapeDtypeStruct((levels, members, LANES), BF16),
+            jax.ShapeDtypeStruct((levels, members, LANES), BF16),
+            jax.ShapeDtypeStruct((levels // 2, members, LANES), BF16),
+        ],
+        [from_a, from_b, small, edge_high, edge_low, part, second, kept],
         [pltpu.VMEM((2, flat_rows, 2 * LANES), BF16)],
         cost=2,
     )
+    pieces = [middle, first, after, last]
     cell = obs_cell.reshape(16, LANES)
     level = obs_level.reshape(16, LANES)
     reading = jax.ShapeDtypeStruct((members, entries), BF16)
     table = pltpu.VMEM((48, LANES), BF16)
-    to_a, to_b = call(
-        functools.partial(neighbour_kernel, others=others, blocks=blocks),
-        [reading, reading],
-        [forecast, left, right, from_a, from_b, *passed, cell, level],
-        [table],
-        cost=3,
-    )
+    to_neighbour = []
+    for turn, received in enumerate((from_a, from_b)):
+        inputs = [*pieces, received, *passed, cell, level]
+        to_neighbour += call(
+            functools.partial(
+                neighbour_kernel, others=others, blocks=blocks, turn=turn
+            ),
+            [reading],
+            [*inputs, *to_neighbour],
+            [table],
+            in_specs=[vmem()] * len(inputs) + [pl.BlockSpec(memory_space=pl.ANY)] * turn,
+            cost=2,
+        )
+    to_a, to_b = to_neighbour
+    to_b, sent = lax.optimization_barrier((to_b, first))
+    firsts = swapped(first, sent)
     back_a = lax.ppermute(to_a, "tile", odd_pairs)
     back_b = lax.ppermute(to_b, "tile", even_pairs)
     vector = jax.ShapeDtypeStruct((8, entries), F32)
@@ -707,9 +792,7 @@
         functools.partial(own_kernel, others=others, blocks=blocks, tiles=tiles),
         [reading, vector, vector],
         [
-            forecast,
-            left,
-            right,
+            *pieces,
             lists,
             *passed,
             cell,
@@ -720,7 +803,7 @@
         [table],
         cost=2,
     )
-    unused = forecasts[1:]
+    unused = middles[1:]
     (readings,) = call(
         merge_kernel,
         [reading],
@@ -728,17 +811,18 @@
         in_specs=[vmem()] * 3 + [pl.BlockSpec(memory_space=pl.ANY)] * len(unused),
         cost=0,
     )
-    readings, sent_left, sent = lax.optimization_barrier((readings, left, right))
-    lefts = [left] + [lax.ppermute(sent_left, "mem", turn) for turn in turns]
-    rights = [right] + [lax.ppermute(sent, "mem", turn) for turn in turns]
-    readings = [readings] + [lax.ppermute(readings, "mem", turn) for turn in turns]
+    readings, sent, sent_last = lax.optimization_barrier((readings, after, last))
+    readings = swapped(readings, readings)
+    afters = swapped(after, sent)
+    lasts = swapped(last, sent_last)
+    unused = firsts[1:]
     ensemble = members * sharers
     total = blocks * sharers
     square = pltpu.VMEM((total, LANES, LANES), F32)
     (weights,) = call(
         functools.partial(weights_kernel, others=others),
         [jax.ShapeDtypeStruct((total, members, ensemble), BF16)],
-        [*readings, weight, target],
+        [*readings, weight, target, *unused],
         [
             pltpu.VMEM((ensemble, entries), BF16),
             pltpu.VMEM((ensemble, entries), BF16),
@@ -748,14 +832,38 @@
             square,
             square,
         ],
+        in_specs=[vmem()] * (sharers + 2) + [pl.BlockSpec(memory_space=pl.ANY)] * len(unused),
         cost=8,
     )
+    rows = members * levels
+    result = jax.ShapeDtypeStruct((members, levels, columns), BF16)
+    inputs = [*middles, *firsts, *afters, weights]
+    analysis, rest = call(
+        functools.partial(update_kernel, others=others),
+        [result, jax.ShapeDtypeStruct((rows, LANES), F32)],
+        inputs,
+        [
+            pltpu.VMEM((groups - 1, rows, LANES), F32),
+            pltpu.VMEM((groups - 1, members, levels, LANES), BF16),
+            pltpu.SemaphoreType.DMA((groups - 1,)),
+        ],
+        out_specs=[hbm, vmem()],
+        cost=2,
+    )
+    inputs = [*lasts, weights, rest, analysis]
     (analysis,) = call(
-        functools.partial(update_kernel, others=others),
-        [jax.ShapeDtypeStruct((members, levels, columns), BF16)],
-        [*forecasts, *lefts, *rights, weights],
-        [pltpu.VMEM((columns // LANES, members * levels, LANES), F32)],
-        cost=3,
+        functools.partial(finish_kernel, others=others),
+        [result],
+        inputs,
+        [
+            pltpu.VMEM((rows, LANES), F32),
+            pltpu.VMEM((members, levels, LANES), BF16),
+            pltpu.SemaphoreType.DMA,
+        ],
+        in_specs=[vmem()] * (len(inputs) - 1) + [hbm],
+        out_specs=[hbm],
+        aliases={len(inputs) - 1: 0},
+        cost=1,
     )
     return analysis
 

time: 51 us -> 48.4 us (0.949)
  waiting for transfers between devices: 14.6 us -> 10.1 us
  starting transfers between devices: 12 us -> 14.2 us
  Pallas kernels: 21.7 us -> 21.1 us
    ppermute x4 -> x5, waiting for transfers between devices: 8.12 us -> 5.44 us  [swapped(): return [value] + [lax.ppermute(sent, 'mem', turn) for turn in turns]]
    ppermute x4 -> x5, starting transfers between devices: 4.11 us -> 6.24 us  [swapped(): return [value] + [lax.ppermute(sent, 'mem', turn) for turn in turns]]
    ppermute x1, waiting for transfers between devices: 5.99 us -> 4.17 us  [shards(): back_a = lax.ppermute(to_a, 'tile', odd_pairs)]
    pallas_call x8 -> x10, Pallas kernels: 21.7 us -> 21.1 us  [call(): pl.pallas_call(kernel, grid=(1,), out_shape=outs, in_specs=in_specs or [v...]
  transfers between devices with their start and end apart: 9 -> 10, of which waited for: 5 -> 3; matrix products, arithmetic and copies ran while one was open for 0% -> 0% of each run, Pallas kernels for 33% -> 37%
where the time goes in v3:
time: 48.4 us; the launch traced here: 48.1 us
  Pallas kernels  21.1 us (44%)
  starting transfers between devices  14.2 us (29%)
  waiting for transfers between devices  10.1 us (21%)
  local copies, waits for them, and re-layouts  2.38 us (5%)
    pallas_call x10, Pallas kernels, call(): pl.pallas_call(kernel, grid=(1,), out_shape=outs, in_specs=in_specs or [v...  21.1 us
    ppermute x5, starting transfers between devices, swapped(): return [value] + [lax.ppermute(sent, 'mem', turn) for turn in turns]  6.24 us
    ppermute x1, starting transfers between devices, shards(): from_a = lax.ppermute(a, 'tile', odd_pairs)  5.51 us
    ppermute x5, waiting for transfers between devices, swapped(): return [value] + [lax.ppermute(sent, 'mem', turn) for turn in turns]  5.44 us
    ppermute x1, waiting for transfers between devices, shards(): back_a = lax.ppermute(to_a, 'tile', odd_pairs)  4.17 us
    unnamed x16, local copies, waits for them, and re-layouts  2.38 us
    ppermute x1, starting transfers between devices, shards(): passed = [lax.ppermute(passed, 'mem', turn) for turn in turns]  1.56 us
  transfers between devices with their start and end apart: 10, of which 3 were waited for; matrix products, arithmetic and copies ran while one was open for 0% of the time, Pallas kernels for 37%

profile of v3, /device:TPU:0, one launch (start us, length us, event | category | flops | bytes accessed | tf_op | source)
XLA Modules:
  0.0 48.1 jit_solution(14655503938158035532)
XLA Ops:
  0.0 2.2 %shard_map.91 = (bf16[592,128]{1,0:T(8,128)(2,1)}, bf16[592,128]{1,0:T(8,128)(2,1)}, bf16[48,128]{1,0:T(8,128)(2,1)}, f32[16,512]{1,0:T(8,128)}) custom-call(f32[1024,512]{1,0:T(8,128)} %bitcast.5, f32[6,512]{1,0:T(8,128)} %coef_hbm.1, s32[6,512]{1,0:T(8,128)} %nbr_hbm.1, s32[4,1,128]{2,1,0:T(1,128)} %index_hbm.1, s32[4,1,128]{2,1,0:T(1,128)} %weight_hbm.1), custom_call_target="tpu_custom_call" | custom-call | bytes 1024 | tf_op jit(solution)/shard_map/pallas_call | solution.py:659
  2.2 5.5 %collective-permute-start = (bf16[592,128]{1,0:T(8,128)(2,1)}, bf16[592,128]{1,0:T(8,128)(2,1)S(1)}, u32[]{:S(2)}, u32[]{:S(2)}) collective-permute-start(bf16[592,128]{1,0:T(8,128)(2,1)} %get-tuple-element.30), channel_id=1, source_target_pairs={{1,2},{2,1},{3,4},{4,3},{5,6},{6,5},{7,8},{8,7},{9,10},{10,9},{11,... | collective-permute-start | bytes 454664 | tf_op jit(solution)/shard_map/ppermute | solution.py:724
  7.7 0.0 collective-permute-start.1
  7.7 0.0 copy-start
  7.7 1.6 %copy-done = f32[128,8,512]{2,1,0:T(8,128)S(1)} copy-done((f32[128,8,512]{2,1,0:T(8,128)S(1)}, f32[128,8,512]{2,1,0:T(8,128)}, u32[]{:S(2)}) %copy-start) | copy-done | bytes 2097176
  9.3 0.0 copy-start.4
  9.3 0.8 %copy-done.4 = f32[16,512]{1,0:T(8,128)S(1)} copy-done((f32[16,512]{1,0:T(8,128)S(1)}, f32[16,512]{1,0:T(8,128)}, u32[]{:S(2)}) %copy-start.4) | copy-done | bytes 32792
  10.1 0.0 copy-start.1
  10.1 0.0 copy-start.5
  10.1 3.4 %shard_map.92 = (bf16[12,128,128]{2,1,0:T(8,128)(2,1)S(1)}, bf16[4,128,128]{2,1,0:T(8,128)(2,1)S(1)}, bf16[2,1024,256]{2,1,0:T(8,128)(2,1)S(1)}, bf16[2,1024,256...) custom-call(f32[1024,512]{1,0:T(8,128)S(1)} %bitcast.6, f32[1024,512]{1,0:T(8,128)S(1)} %bitcast.7, ...), custom_call_target="tpu_custom_call" | custom-call | flops 4294967296 | bytes 1024 | tf_op jit(solution)/shard_map/pallas_call | solution.py:659
  13.5 0.0 collective-permute-done.a_ref.refs_4_
  13.5 0.0 collective-permute-done.1.b_ref.refs_4_
  13.5 0.0 copy-done.1
  13.5 1.6 %collective-permute-start.2 = (bf16[112,128]{1,0:T(8,128)(2,1)S(1)}, bf16[112,128]{1,0:T(8,128)(2,1)S(1)}, u32[]{:S(2)}, u32[]{:S(2)}) collective-permute-start(bf16[112,128]{1,0:T(8,128)(2,1)S(1)} %pad_maximum_fusion), channel_id=1, source_target_pairs={{16,0},{0,16},{17,1},{1,17},{18,2},{2,18},{19,3},{3,19},{20,4},{4,... | collective-permute-start | bytes 86024 | tf_op jit(solution)/shard_map/ppermute | solution.py:755
  15.1 0.5 %collective-permute-start.5 = (bf16[12,128,128]{2,1,0:T(8,128)(2,1)S(1)}, bf16[12,128,128]{2,1,0:T(8,128)(2,1)S(1)}, u32[]{:S(2)}, u32[]{:S(2)}) collective-permute-start(bf16[12,128,128]{2,1,0:T(8,128)(2,1)S(1)} %get-tuple-element.46.refs_0_), channel_id=1, source_target_pairs={{16,0},{0,16},{17,1},{1,17},{18,2},{2,18},{19,3},{3,19},{20,4},{4,... | collective-permute-start | bytes 1179656 | tf_op jit(solution)/shard_map/ppermute | solution.py:751
  15.6 0.0 copy-done.5
  15.6 0.0 copy-start.6
  15.6 0.0 copy-start.7
  15.6 1.4 %shard_map.93 = (bf16[8,128,128]{2,1,0:T(8,128)(2,1)S(1)}, bf16[8,128,128]{2,1,0:T(8,128)(2,1)S(1)}, bf16[4,128,128]{2,1,0:T(8,128)(2,1)S(1)}) custom-call(bf16[592,128]{1,0:T(8,128)(2,1)S(1)} %collective-permute-done.a_ref.refs_4_, bf16[592,128]{1,0:T(8,128)(2,1)S(1)} %collective-permute-done.1.b_ref.refs_4_, f32[16,512]{1,0:T(8,128)S(1)} %copy-done.5, ...), custom_call_target="tpu_custom_call" | custom-call | flops 2147483648 | bytes 1024 | tf_op jit(solution)/shard_map/pallas_call | solution.py:659
  17.0 0.5 collective-permute-done.2.refs_5_
  17.5 0.0 copy-done.6
  17.5 0.0 copy-done.7
  17.5 1.5 %shard_map.95.refs_8_ = bf16[128,1024]{1,0:T(8,128)(2,1)S(1)} custom-call(bf16[12,128,128]{2,1,0:T(8,128)(2,1)S(1)} %get-tuple-element.46.refs_0_, bf16[8,128,128]{2,1,0:T(8,128)(2,1)S(1)} %get-tuple-element.51.refs_1_.refs_2_, bf16[8,128,128]{2,1,0:T(8,128)(2,1)S(1)} %get-tuple-element.52.refs_2_.refs_4_, ...), custom_call_target="tpu_custom_call" | custom-call | flops 2147483648 | bytes 1024 | tf_op jit(solution)/shard_map/pallas_call | solution.py:659
  19.0 0.0 copy-start.2
  19.0 0.0 copy-start.3
  19.0 1.5 %shard_map.96 = bf16[128,1024]{1,0:T(8,128)(2,1)S(1)} custom-call(bf16[12,128,128]{2,1,0:T(8,128)(2,1)S(1)} %get-tuple-element.46.refs_0_, bf16[8,128,128]{2,1,0:T(8,128)(2,1)S(1)} %get-tuple-element.51.refs_1_.refs_2_, bf16[8,128,128]{2,1,0:T(8,128)(2,1)S(1)} %get-tuple-element.52.refs_2_.refs_4_, ...), custom_call_target="tpu_custom_call" | custom-call | flops 2147483648 | bytes 1024 | tf_op jit(solution)/shard_map/pallas_call | solution.py:659
  20.5 0.1 collective-permute-start.4
  20.6 0.8 %collective-permute-start.3 = (bf16[128,1024]{1,0:T(8,128)(2,1)S(1)}, bf16[128,1024]{1,0:T(8,128)(2,1)S(1)}, u32[]{:S(2)}, u32[]{:S(2)}) collective-permute-start(bf16[128,1024]{1,0:T(8,128)(2,1)S(1)} %shard_map.95.refs_8_), channel_id=1, source_target_pairs={{1,2},{2,1},{3,4},{4,3},{5,6},{6,5},{7,8},{8,7},{9,10},{10,9},{11,... | collective-permute-start | bytes 786440 | tf_op jit(solution)/shard_map/ppermute | solution.py:788
  21.4 1.9 %collective-permute-start.8 = (bf16[8,128,128]{2,1,0:T(8,128)(2,1)S(1)}, bf16[8,128,128]{2,1,0:T(8,128)(2,1)S(1)}, u32[]{:S(2)}, u32[]{:S(2)}) collective-permute-start(bf16[8,128,128]{2,1,0:T(8,128)(2,1)S(1)} %get-tuple-element.51.refs_1_.refs_2_), channel_id=1, source_target_pairs={{16,0},{0,16},{17,1},{1,17},{18,2},{2,18},{19,3},{3,19},{20,4},{4,... | collective-permute-start | bytes 786440 | tf_op jit(solution)/shard_map/ppermute | solution.py:751
  23.3 0.0 copy-done.2
  23.3 0.0 copy-done.3
  23.3 1.8 %shard_map.94 = (bf16[128,1024]{1,0:T(8,128)(2,1)S(1)}, f32[8,1024]{1,0:T(8,128)S(1)}, f32[8,1024]{1,0:T(8,128)S(1)}) custom-call(bf16[12,128,128]{2,1,0:T(8,128)(2,1)S(1)} %get-tuple-element.46.refs_0_, bf16[8,128,128]{2,1,0:T(8,128)(2,1)S(1)} %get-tuple-element.51.refs_1_.refs_2_, bf16[8,128,128]{2,1,0:T(8,128)(2,1)S(1)} %get-tuple-element.52.refs_2_.refs_4_, ...), custom_call_target="tpu_custom_call" | custom-call | flops 2147483648 | bytes 1024 | tf_op jit(solution)/shard_map/pallas_call | solution.py:659
  25.1 0.0 collective-permute-done.4.b_ref
  25.1 4.2 %collective-permute-done.3.a_ref = bf16[128,1024]{1,0:T(8,128)(2,1)S(1)} collective-permute-done((bf16[128,1024]{1,0:T(8,128)(2,1)S(1)}, bf16[128,1024]{1,0:T(8,128)(2,1)S(1)}, u32[]{:S(2)}, u32[]{:S(2)}) %collective-permute-start.3) | collective-permute-done | bytes 262176 | tf_op jit(solution)/shard_map/ppermute | solution.py:788
  29.3 0.0 collective-permute-done.5.refs_0_.refs_1_
  29.3 0.1 shard_map.97.refs_0_
  29.4 1.8 %collective-permute-start.7 = (bf16[128,1024]{1,0:T(8,128)(2,1)S(1)}, bf16[128,1024]{1,0:T(8,128)(2,1)S(1)}, u32[]{:S(2)}, u32[]{:S(2)}) collective-permute-start(bf16[128,1024]{1,0:T(8,128)(2,1)S(1)} %shard_map.97.refs_0_), channel_id=1, source_target_pairs={{16,0},{0,16},{17,1},{1,17},{18,2},{2,18},{19,3},{3,19},{20,4},{4,... | collective-permute-start | bytes 786440 | tf_op jit(solution)/shard_map/ppermute | solution.py:751
  31.2 0.3 collective-permute-start.9
  31.5 1.7 %collective-permute-start.6 = (bf16[4,128,128]{2,1,0:T(8,128)(2,1)S(1)}, bf16[4,128,128]{2,1,0:T(8,128)(2,1)S(1)}, u32[]{:S(2)}, u32[]{:S(2)}) collective-permute-start(bf16[4,128,128]{2,1,0:T(8,128)(2,1)S(1)} %get-tuple-element.47.refs_3_.refs_0_), channel_id=1, source_target_pairs={{16,0},{0,16},{17,1},{1,17},{18,2},{2,18},{19,3},{3,19},{20,4},{4,... | collective-permute-start | bytes 393224 | tf_op jit(solution)/shard_map/ppermute | solution.py:751
  33.2 0.0 collective-permute-done.8.refs_4_.refs_3_
  33.2 5.4 %collective-permute-done.7.refs_1_ = bf16[128,1024]{1,0:T(8,128)(2,1)S(1)} collective-permute-done((bf16[128,1024]{1,0:T(8,128)(2,1)S(1)}, bf16[128,1024]{1,0:T(8,128)(2,1)S(1)}, u32[]{:S(2)}, u32[]{:S(2)}) %collective-permute-start.7) | collective-permute-done | bytes 262176 | tf_op jit(solution)/shard_map/ppermute | solution.py:751
  38.6 6.2 %shard_map.98.refs_6_.refs_2_ = bf16[8,128,256]{2,1,0:T(8,128)(2,1)S(1)} custom-call(bf16[128,1024]{1,0:T(8,128)(2,1)S(1)} %shard_map.97.refs_0_, bf16[128,1024]{1,0:T(8,128)(2,1)S(1)} %collective-permute-done.7.refs_1_, f32[8,1024]{1,0:T(8,128)S(1)} %get-tuple-element.49.refs_2_, f32[8,1024]{1,0:T(8,128)S(1)} %get-tuple-element.50.refs_3_, ...), custom_call_target="tpu_custom_call" | custom-call | flops 8589934592 | bytes 1024 | tf_op jit(solution)/shard_map/pallas_call | solution.py:659
  44.9 0.0 collective-permute-done.9.refs_5_
  44.9 2.0 %shard_map.99 = (bf16[128,8,512]{2,1,0:T(8,128)(2,1)}, f32[1024,128]{1,0:T(8,128)S(1)}) custom-call(bf16[12,128,128]{2,1,0:T(8,128)(2,1)S(1)} %get-tuple-element.46.refs_0_, bf16[12,128,128]{2,1,0:T(8,128)(2,1)S(1)} %collective-permute-done.5.refs_0_.refs_1_, bf16[8,128,128]{2,1,0:T(8,128)(2,1)S(1)} %get-tuple-element.51.refs_1_.refs_2_, ...), custom_call_target="tpu_custom_call" | custom-call | flops 2147483648 | bytes 1024 | tf_op jit(solution)/shard_map/pallas_call | solution.py:659
  46.9 0.0 collective-permute-done.6.refs_1_
  46.9 1.1 %shard_map.100 = bf16[128,8,512]{2,1,0:T(8,128)(2,1)} custom-call(bf16[4,128,128]{2,1,0:T(8,128)(2,1)S(1)} %get-tuple-element.47.refs_3_.refs_0_, bf16[4,128,128]{2,1,0:T(8,128)(2,1)S(1)} %collective-permute-done.6.refs_1_, bf16[8,128,256]{2,1,0:T(8,128)(2,1)S(1)} %shard_map.98.refs_6_.refs_2_, ...), custom_call_target="tpu_custom_call", output_to_operand_aliasing={{}: (4, {})} | custom-call | flops 1073741824 | bytes 1024 | tf_op jit(solution)/shard_map/pallas_call | solution.py:659
  (3 shorter events, 0.0 us)
Async XLA Ops:
  2.2 11.3 %collective-permute-start = (bf16[592,128]{1,0:T(8,128)(2,1)}, bf16[592,128]{1,0:T(8,128)(2,1)S(1)}, u32[]{:S(2)}, u32[]{:S(2)}) collective-permute-start(bf16[592,128]{1,0:T(8,128)(2,1)} %get-tuple-element.30), channel_id=1, source_target_pairs={{1,2},{2,1},{3,4},{4,3},{5,6},{6,5},{7,8},{8,7},{9,10},{10,9},{11,... | collective-permute-start | bytes 454664 | tf_op jit(solution)/shard_map/ppermute | solution.py:724
  7.7 5.8 %collective-permute-start.1 = (bf16[592,128]{1,0:T(8,128)(2,1)}, bf16[592,128]{1,0:T(8,128)(2,1)S(1)}, u32[]{:S(2)}, u32[]{:S(2)}) collective-permute-start(bf16[592,128]{1,0:T(8,128)(2,1)} %get-tuple-element.31), channel_id=1, source_target_pairs={{0,1},{1,0},{2,3},{3,2},{4,5},{5,4},{6,7},{7,6},{8,9},{9,8},{10,11... | collective-permute-start | bytes 454664 | tf_op jit(solution)/shard_map/ppermute | solution.py:723
  7.7 1.6 %copy-start = (f32[128,8,512]{2,1,0:T(8,128)S(1)}, f32[128,8,512]{2,1,0:T(8,128)}, u32[]{:S(2)}) copy-start(f32[128,8,512]{2,1,0:T(8,128)} %param.9) | copy-start | bytes 6291460
  9.3 0.8 %copy-start.4 = (f32[16,512]{1,0:T(8,128)S(1)}, f32[16,512]{1,0:T(8,128)}, u32[]{:S(2)}) copy-start(f32[16,512]{1,0:T(8,128)} %get-tuple-element.32.refs_4_.small_ref) | copy-start | bytes 98308
  10.1 3.4 %copy-start.1 = (bf16[48,128]{1,0:T(8,128)(2,1)S(1)}, bf16[48,128]{1,0:T(8,128)(2,1)}, u32[]{:S(2)}) copy-start(bf16[48,128]{1,0:T(8,128)(2,1)} %get-tuple-element.42.refs_4_) | copy-start | bytes 36868
  10.1 5.6 %copy-start.5 = (f32[16,512]{1,0:T(8,128)S(1)}, f32[16,512]{1,0:T(8,128)}, u32[]{:S(2)}) copy-start(f32[16,512]{1,0:T(8,128)} %get-tuple-element.32.refs_4_.small_ref) | copy-start | bytes 98308
  13.5 3.9 %collective-permute-start.2 = (bf16[112,128]{1,0:T(8,128)(2,1)S(1)}, bf16[112,128]{1,0:T(8,128)(2,1)S(1)}, u32[]{:S(2)}, u32[]{:S(2)}) collective-permute-start(bf16[112,128]{1,0:T(8,128)(2,1)S(1)} %pad_maximum_fusion), channel_id=1, source_target_pairs={{16,0},{0,16},{17,1},{1,17},{18,2},{2,18},{19,3},{3,19},{20,4},{4,... | collective-permute-start | bytes 86024 | tf_op jit(solution)/shard_map/ppermute | solution.py:755
  15.1 14.2 %collective-permute-start.5 = (bf16[12,128,128]{2,1,0:T(8,128)(2,1)S(1)}, bf16[12,128,128]{2,1,0:T(8,128)(2,1)S(1)}, u32[]{:S(2)}, u32[]{:S(2)}) collective-permute-start(bf16[12,128,128]{2,1,0:T(8,128)(2,1)S(1)} %get-tuple-element.46.refs_0_), channel_id=1, source_target_pairs={{16,0},{0,16},{17,1},{1,17},{18,2},{2,18},{19,3},{3,19},{20,4},{4,... | collective-permute-start | bytes 1179656 | tf_op jit(solution)/shard_map/ppermute | solution.py:751
  15.6 1.8 %copy-start.6 = (s32[2048]{0:T(1024)S(1)}, s32[2048]{0:T(1024)}, u32[]{:S(2)}) copy-start(s32[2048]{0:T(1024)} %param.12) | copy-start | bytes 24580
  15.6 1.8 %copy-start.7 = (s32[2048]{0:T(1024)S(1)}, s32[2048]{0:T(1024)}, u32[]{:S(2)}) copy-start(s32[2048]{0:T(1024)} %param.13) | copy-start | bytes 24580
  19.0 4.3 %copy-start.2 = (f32[32768]{0:T(1024)S(1)}, f32[32768]{0:T(1024)}, u32[]{:S(2)}) copy-start(f32[32768]{0:T(1024)} %param.14) | copy-start | bytes 393220
  19.0 4.3 %copy-start.3 = (f32[32768]{0:T(1024)S(1)}, f32[32768]{0:T(1024)}, u32[]{:S(2)}) copy-start(f32[32768]{0:T(1024)} %param.15) | copy-start | bytes 393220
  20.5 4.6 %collective-permute-start.4 = (bf16[128,1024]{1,0:T(8,128)(2,1)S(1)}, bf16[128,1024]{1,0:T(8,128)(2,1)S(1)}, u32[]{:S(2)}, u32[]{:S(2)}) collective-permute-start(bf16[128,1024]{1,0:T(8,128)(2,1)S(1)} %shard_map.96), channel_id=1, source_target_pairs={{0,1},{1,0},{2,3},{3,2},{4,5},{5,4},{6,7},{7,6},{8,9},{9,8},{10,11... | collective-permute-start | bytes 786440 | tf_op jit(solution)/shard_map/ppermute | solution.py:789
  20.6 8.7 %collective-permute-start.3 = (bf16[128,1024]{1,0:T(8,128)(2,1)S(1)}, bf16[128,1024]{1,0:T(8,128)(2,1)S(1)}, u32[]{:S(2)}, u32[]{:S(2)}) collective-permute-start(bf16[128,1024]{1,0:T(8,128)(2,1)S(1)} %shard_map.95.refs_8_), channel_id=1, source_target_pairs={{1,2},{2,1},{3,4},{4,3},{5,6},{6,5},{7,8},{8,7},{9,10},{10,9},{11,... | collective-permute-start | bytes 786440 | tf_op jit(solution)/shard_map/ppermute | solution.py:788
  21.4 11.8 %collective-permute-start.8 = (bf16[8,128,128]{2,1,0:T(8,128)(2,1)S(1)}, bf16[8,128,128]{2,1,0:T(8,128)(2,1)S(1)}, u32[]{:S(2)}, u32[]{:S(2)}) collective-permute-start(bf16[8,128,128]{2,1,0:T(8,128)(2,1)S(1)} %get-tuple-element.51.refs_1_.refs_2_), channel_id=1, source_target_pairs={{16,0},{0,16},{17,1},{1,17},{18,2},{2,18},{19,3},{3,19},{20,4},{4,... | collective-permute-start | bytes 786440 | tf_op jit(solution)/shard_map/ppermute | solution.py:751
  29.4 9.2 %collective-permute-start.7 = (bf16[128,1024]{1,0:T(8,128)(2,1)S(1)}, bf16[128,1024]{1,0:T(8,128)(2,1)S(1)}, u32[]{:S(2)}, u32[]{:S(2)}) collective-permute-start(bf16[128,1024]{1,0:T(8,128)(2,1)S(1)} %shard_map.97.refs_0_), channel_id=1, source_target_pairs={{16,0},{0,16},{17,1},{1,17},{18,2},{2,18},{19,3},{3,19},{20,4},{4,... | collective-permute-start | bytes 786440 | tf_op jit(solution)/shard_map/ppermute | solution.py:751
  31.2 13.7 %collective-permute-start.9 = (bf16[8,128,128]{2,1,0:T(8,128)(2,1)S(1)}, bf16[8,128,128]{2,1,0:T(8,128)(2,1)S(1)}, u32[]{:S(2)}, u32[]{:S(2)}) collective-permute-start(bf16[8,128,128]{2,1,0:T(8,128)(2,1)S(1)} %get-tuple-element.52.refs_2_.refs_4_), channel_id=1, source_target_pairs={{16,0},{0,16},{17,1},{1,17},{18,2},{2,18},{19,3},{3,19},{20,4},{4,... | collective-permute-start | bytes 786440 | tf_op jit(solution)/shard_map/ppermute | solution.py:751
  31.5 15.4 %collective-permute-start.6 = (bf16[4,128,128]{2,1,0:T(8,128)(2,1)S(1)}, bf16[4,128,128]{2,1,0:T(8,128)(2,1)S(1)}, u32[]{:S(2)}, u32[]{:S(2)}) collective-permute-start(bf16[4,128,128]{2,1,0:T(8,128)(2,1)S(1)} %get-tuple-element.47.refs_3_.refs_0_), channel_id=1, source_target_pairs={{16,0},{0,16},{17,1},{1,17},{18,2},{2,18},{19,3},{3,19},{20,4},{4,... | collective-permute-start | bytes 393224 | tf_op jit(solution)/shard_map/ppermute | solution.py:751

commit v4 on v3

--- a/solution.py
+++ b/solution.py
@@ -442,11 +442,9 @@
     target_ref[...] = jnp.broadcast_to(looked_up(value_ref), target_ref.shape)
 
 
-def merge_kernel(own_ref, a_ref, b_ref, *refs):
+def merge_kernel(one_ref, other_ref, *refs):
     out_ref = refs[-1]
-    out_ref[...] = (
-        own_ref[...].astype(F32) + (a_ref[...].astype(F32) + b_ref[...].astype(F32))
-    ).astype(BF16)
+    out_ref[...] = (one_ref[...].astype(F32) + other_ref[...].astype(F32)).astype(BF16)
 
 
 def doubled(high, low):
@@ -573,17 +571,24 @@
         out_ref[b] = (found[:members, :] + found[members : members + 1, :] + diagonal).astype(BF16)
 
 
-def updated(left, parts, width):
-    members = parts[0].shape[0]
-    parts = [part.astype(F32) for part in parts]
+def departures(pairs):
+    count = len(pairs[0])
+    ensemble = pairs[0][0].shape[0] * count
+    parts = [joined([pair[k].astype(F32) for pair in pairs]) for k in range(count)]
     total = sum(jnp.sum(part, axis=0, keepdims=True) for part in parts)
-    mean = total * (1.0 / (members * len(parts)))
-    found = dot(left, jnp.concatenate([(part - mean).astype(BF16) for part in parts], axis=0))
+    mean = total * (1.0 / ensemble)
+    return jnp.concatenate([(part - mean).astype(BF16) for part in parts], axis=0), mean
+
+
+def updated(left, moved, mean, width):
+    members = left.shape[0] * width // LANES
+    found = dot(left, moved)
     result = found[:members, :]
-    lane = iota(result.shape, 1)
+    lane = iota(result.shape, 1) % LANES
     for k in range(1, LANES // width):
         result = jnp.where(lane < k * width, result, found[k * members : (k + 1) * members, :])
-    return result + mean
+    result = result + mean
+    return [result[:, k : k + LANES] for k in range(0, result.shape[1], LANES)]
 
 
 def weights_of(weight_ref, group, columns):
@@ -591,56 +596,69 @@
     return jnp.concatenate([weight_ref[group * per + k] for k in range(per)], axis=0)
 
 
+def prepare_kernel(*refs, others):
+    count = others + 1
+    middles, firsts = [refs[k * count : (k + 1) * count] for k in range(2)]
+    moved_ref, mean_ref = refs[2 * count :]
+    slot = 0
+    for piece in (middles, firsts):
+        for k in range(0, piece[0].shape[0], 2):
+            moved, mean = departures([[ref[k + j] for ref in piece] for j in range(2)])
+            moved_ref[slot] = moved
+            mean_ref[slot] = jnp.broadcast_to(mean, mean_ref.shape[1:])
+            slot += 1
+
+
 def update_kernel(*refs, others):
-    count = others + 1
-    middles, firsts, afters = [refs[k * count : (k + 1) * count] for k in range(3)]
-    weight_ref, out_hbm, rest_ref, stage, done, sems = refs[3 * count :]
+    afters = refs[: others + 1]
+    moved_ref, mean_ref, weight_ref, out_hbm, rest_ref, stage, done, sems = refs[others + 1 :]
     members, levels, columns = out_hbm.shape
     width = columns // weight_ref.shape[0]
     part = levels // 2
     groups = columns // LANES
+
+    def rows(level):
+        return pl.ds(level, members, stride=levels)
+
     copies = []
+    slot = 0
     for group in (*range(1, groups - 1), 0):
         left = weights_of(weight_ref, group, columns)
-        for level in range(levels):
-            place = (group - 1) * levels + level
-            if group == groups - 2 and level >= part:
-                parts = [ref[level - part] for ref in firsts]
-            elif group:
-                parts = [ref[place] for ref in middles]
-            elif level < part:
-                parts = [ref[part + level] for ref in firsts]
+        for level in range(0, levels, 2):
+            if group or level < part:
+                moved, mean = moved_ref[slot], mean_ref[slot, 0:1, :]
+                slot += 1
             else:
-                parts = [ref[level - part] for ref in afters]
-            stage[group, pl.ds(level, members, stride=levels), :] = updated(left, parts, width)
+                moved, mean = departures([[ref[level - part + j] for ref in afters] for j in range(2)])
+            for j, value in enumerate(updated(left, moved, mean, width)):
+                stage[group, rows(level + j), :] = value
         done[group] = stage[group].reshape(members, levels, LANES).astype(BF16)
         lanes = slice(group * LANES, (group + 1) * LANES)
         copies.append(pltpu.make_async_copy(done.at[group], out_hbm.at[:, :, lanes], sems.at[group]))
         copies[-1].start()
     left = weights_of(weight_ref, groups - 1, columns)
-    for level in range(part):
-        rest_ref[pl.ds(level, members, stride=levels), :] = updated(
-            left, [ref[part + level] for ref in afters], width
-        )
+    for level in range(0, part, 2):
+        moved, mean = departures([[ref[part + level + j] for ref in afters] for j in range(2)])
+        for j, value in enumerate(updated(left, moved, mean, width)):
+            rest_ref[rows(level + j), :] = value
     for level in range(part, levels):
-        rest_ref[pl.ds(level, members, stride=levels), :] = jnp.zeros((members, LANES), F32)
+        rest_ref[rows(level), :] = jnp.zeros((members, LANES), F32)
     for copy in copies:
         copy.wait()
 
 
 def finish_kernel(*refs, others):
-    count = others + 1
-    lasts = refs[:count]
-    weight_ref, rest_ref, _, out_hbm, stage, done, sem = refs[count:]
+    lasts = refs[: others + 1]
+    weight_ref, rest_ref, _, out_hbm, stage, done, sem = refs[others + 1 :]
     members, levels, columns = out_hbm.shape
     width = columns // weight_ref.shape[0]
     part = levels // 2
     left = weights_of(weight_ref, columns // LANES - 1, columns)
     stage[...] = rest_ref[...]
-    for level in range(part):
-        stage[pl.ds(part + level, members, stride=levels), :] = updated(
-            left, [ref[level] for ref in lasts], width
-        )
+    for level in range(0, part, 2):
+        moved, mean = departures([[ref[level + j] for ref in lasts] for j in range(2)])
+        for j, value in enumerate(updated(left, moved, mean, width)):
+            stage[pl.ds(part + level + j, members, stride=levels), :] = value
     done[...] = stage[...].reshape(members, levels, LANES).astype(BF16)
     copy = pltpu.make_async_copy(done, out_hbm.at[:, :, columns - LANES : columns], sem)
     copy.start()
@@ -804,11 +822,12 @@
         cost=2,
     )
     unused = middles[1:]
+    (readings,) = call(merge_kernel, [reading], [own, back_a], cost=2)
     (readings,) = call(
         merge_kernel,
         [reading],
-        [own, back_a, back_b, *unused],
-        in_specs=[vmem()] * 3 + [pl.BlockSpec(memory_space=pl.ANY)] * len(unused),
+        [readings, back_b, *unused],
+        in_specs=[vmem()] * 2 + [pl.BlockSpec(memory_space=pl.ANY)] * len(unused),
         cost=0,
     )
     readings, sent, sent_last = lax.optimization_barrier((readings, after, last))
@@ -837,7 +856,17 @@
     )
     rows = members * levels
     result = jax.ShapeDtypeStruct((members, levels, columns), BF16)
-    inputs = [*middles, *firsts, *afters, weights]
+    pairs = (middle.shape[0] + first.shape[0]) // 2
+    moved, mean = call(
+        functools.partial(prepare_kernel, others=others),
+        [
+            jax.ShapeDtypeStruct((pairs, ensemble, 2 * LANES), BF16),
+            jax.ShapeDtypeStruct((pairs, 8, 2 * LANES), F32),
+        ],
+        [*middles, *firsts],
+        cost=2,
+    )
+    inputs = [*afters, moved, mean, weights]
     analysis, rest = call(
         functools.partial(update_kernel, others=others),
         [result, jax.ShapeDtypeStruct((rows, LANES), F32)],

time: 48.4 us -> 47.6 us (0.983)
  waiting for transfers between devices: 10.1 us -> 9.26 us
    ppermute x1, waiting for transfers between devices: 4.17 us -> 2.49 us  [shards(): back_a = lax.ppermute(to_a, 'tile', odd_pairs)]
    ppermute x5, waiting for transfers between devices: 5.44 us -> 6.29 us  [swapped(): return [value] + [lax.ppermute(sent, 'mem', turn) for turn in turns]]
    pallas_call x10 -> x12, Pallas kernels: 21.1 us -> 21.2 us  [call(): pl.pallas_call(kernel, grid=(1,), out_shape=outs, in_specs=in_specs or [v...]
  transfers between devices with their start and end apart: 10 -> 10, of which waited for: 3 -> 4; matrix products, arithmetic and copies ran while one was open for 0% -> 0% of each run, Pallas kernels for 37% -> 38%
where the time goes in v4:
time: 47.6 us; the launch traced here: 47.4 us
  Pallas kernels  21.2 us (45%)
  starting transfers between devices  14.2 us (30%)
  waiting for transfers between devices  9.26 us (19%)
  local copies, waits for them, and re-layouts  2.38 us (5%)
    pallas_call x12, Pallas kernels, call(): pl.pallas_call(kernel, grid=(1,), out_shape=outs, in_specs=in_specs or [v...  21.2 us
    ppermute x5, starting transfers between devices, swapped(): return [value] + [lax.ppermute(sent, 'mem', turn) for turn in turns]  6.32 us
    ppermute x5, waiting for transfers between devices, swapped(): return [value] + [lax.ppermute(sent, 'mem', turn) for turn in turns]  6.29 us
    ppermute x1, starting transfers between devices, shards(): from_a = lax.ppermute(a, 'tile', odd_pairs)  5.51 us
    ppermute x1, waiting for transfers between devices, shards(): back_a = lax.ppermute(to_a, 'tile', odd_pairs)  2.49 us
    unnamed x16, local copies, waits for them, and re-layouts  2.38 us
    ppermute x1, starting transfers between devices, shards(): passed = [lax.ppermute(passed, 'mem', turn) for turn in turns]  1.56 us
  transfers between devices with their start and end apart: 10, of which 4 were waited for; matrix products, arithmetic and copies ran while one was open for 0% of the time, Pallas kernels for 38%

profile of v4, /device:TPU:0, one launch (start us, length us, event | category | flops | bytes accessed | tf_op | source)
XLA Modules:
  0.0 47.4 jit_solution(8638725635176592636)
XLA Ops:
  0.0 2.2 %shard_map.91 = (bf16[592,128]{1,0:T(8,128)(2,1)}, bf16[592,128]{1,0:T(8,128)(2,1)}, bf16[48,128]{1,0:T(8,128)(2,1)}, f32[16,512]{1,0:T(8,128)}) custom-call(f32[1024,512]{1,0:T(8,128)} %bitcast.5, f32[6,512]{1,0:T(8,128)} %coef_hbm.1, s32[6,512]{1,0:T(8,128)} %nbr_hbm.1, s32[4,1,128]{2,1,0:T(1,128)} %index_hbm.1, s32[4,1,128]{2,1,0:T(1,128)} %weight_hbm.1), custom_call_target="tpu_custom_call" | custom-call | bytes 1024 | tf_op jit(solution)/shard_map/pallas_call | solution.py:677
  2.2 5.5 %collective-permute-start = (bf16[592,128]{1,0:T(8,128)(2,1)}, bf16[592,128]{1,0:T(8,128)(2,1)S(1)}, u32[]{:S(2)}, u32[]{:S(2)}) collective-permute-start(bf16[592,128]{1,0:T(8,128)(2,1)} %get-tuple-element.32), channel_id=1, source_target_pairs={{1,2},{2,1},{3,4},{4,3},{5,6},{6,5},{7,8},{8,7},{9,10},{10,9},{11,... | collective-permute-start | bytes 454664 | tf_op jit(solution)/shard_map/ppermute | solution.py:742
  7.7 0.0 collective-permute-start.1
  7.7 0.0 copy-start
  7.7 1.6 %copy-done = f32[128,8,512]{2,1,0:T(8,128)S(1)} copy-done((f32[128,8,512]{2,1,0:T(8,128)S(1)}, f32[128,8,512]{2,1,0:T(8,128)}, u32[]{:S(2)}) %copy-start) | copy-done | bytes 2097176
  9.3 0.0 copy-start.4
  9.3 0.8 %copy-done.4 = f32[16,512]{1,0:T(8,128)S(1)} copy-done((f32[16,512]{1,0:T(8,128)S(1)}, f32[16,512]{1,0:T(8,128)}, u32[]{:S(2)}) %copy-start.4) | copy-done | bytes 32792
  10.1 0.0 copy-start.1
  10.1 0.0 copy-start.5
  10.1 3.4 %shard_map.92 = (bf16[12,128,128]{2,1,0:T(8,128)(2,1)S(1)}, bf16[4,128,128]{2,1,0:T(8,128)(2,1)S(1)}, bf16[2,1024,256]{2,1,0:T(8,128)(2,1)S(1)}, bf16[2,1024,256...) custom-call(f32[1024,512]{1,0:T(8,128)S(1)} %bitcast.6, f32[1024,512]{1,0:T(8,128)S(1)} %bitcast.7, ...), custom_call_target="tpu_custom_call" | custom-call | flops 4294967296 | bytes 1024 | tf_op jit(solution)/shard_map/pallas_call | solution.py:677
  13.5 0.0 collective-permute-done.a_ref.refs_4_
  13.5 0.0 collective-permute-done.1.b_ref.refs_4_
  13.5 0.0 copy-done.1
  13.5 1.6 %collective-permute-start.2 = (bf16[112,128]{1,0:T(8,128)(2,1)S(1)}, bf16[112,128]{1,0:T(8,128)(2,1)S(1)}, u32[]{:S(2)}, u32[]{:S(2)}) collective-permute-start(bf16[112,128]{1,0:T(8,128)(2,1)S(1)} %pad_maximum_fusion), channel_id=1, source_target_pairs={{16,0},{0,16},{17,1},{1,17},{18,2},{2,18},{19,3},{3,19},{20,4},{4,... | collective-permute-start | bytes 86024 | tf_op jit(solution)/shard_map/ppermute | solution.py:773
  15.1 0.5 %collective-permute-start.5 = (bf16[12,128,128]{2,1,0:T(8,128)(2,1)S(1)}, bf16[12,128,128]{2,1,0:T(8,128)(2,1)S(1)}, u32[]{:S(2)}, u32[]{:S(2)}) collective-permute-start(bf16[12,128,128]{2,1,0:T(8,128)(2,1)S(1)} %get-tuple-element.48.refs_0_), channel_id=1, source_target_pairs={{16,0},{0,16},{17,1},{1,17},{18,2},{2,18},{19,3},{3,19},{20,4},{4,... | collective-permute-start | bytes 1179656 | tf_op jit(solution)/shard_map/ppermute | solution.py:769
  15.6 0.0 copy-done.5
  15.6 0.0 copy-start.6
  15.6 0.0 copy-start.7
  15.6 1.4 %shard_map.93 = (bf16[8,128,128]{2,1,0:T(8,128)(2,1)S(1)}, bf16[8,128,128]{2,1,0:T(8,128)(2,1)S(1)}, bf16[4,128,128]{2,1,0:T(8,128)(2,1)S(1)}) custom-call(bf16[592,128]{1,0:T(8,128)(2,1)S(1)} %collective-permute-done.a_ref.refs_4_, bf16[592,128]{1,0:T(8,128)(2,1)S(1)} %collective-permute-done.1.b_ref.refs_4_, f32[16,512]{1,0:T(8,128)S(1)} %copy-done.5, ...), custom_call_target="tpu_custom_call" | custom-call | flops 2147483648 | bytes 1024 | tf_op jit(solution)/shard_map/pallas_call | solution.py:677
  17.0 0.5 collective-permute-done.2.refs_5_
  17.5 0.0 copy-done.6
  17.5 0.0 copy-done.7
  17.5 1.5 %shard_map.95.refs_8_ = bf16[128,1024]{1,0:T(8,128)(2,1)S(1)} custom-call(bf16[12,128,128]{2,1,0:T(8,128)(2,1)S(1)} %get-tuple-element.48.refs_0_, bf16[8,128,128]{2,1,0:T(8,128)(2,1)S(1)} %get-tuple-element.53.refs_1_.refs_2_, bf16[8,128,128]{2,1,0:T(8,128)(2,1)S(1)} %get-tuple-element.54.refs_2_.refs_0_, ...), custom_call_target="tpu_custom_call" | custom-call | flops 2147483648 | bytes 1024 | tf_op jit(solution)/shard_map/pallas_call | solution.py:677
  19.0 0.0 copy-start.2
  19.0 0.0 copy-start.3
  19.0 0.8 %collective-permute-start.3 = (bf16[128,1024]{1,0:T(8,128)(2,1)S(1)}, bf16[128,1024]{1,0:T(8,128)(2,1)S(1)}, u32[]{:S(2)}, u32[]{:S(2)}) collective-permute-start(bf16[128,1024]{1,0:T(8,128)(2,1)S(1)} %shard_map.95.refs_8_), channel_id=1, source_target_pairs={{1,2},{2,1},{3,4},{4,3},{5,6},{6,5},{7,8},{8,7},{9,10},{10,9},{11,... | collective-permute-start | bytes 786440 | tf_op jit(solution)/shard_map/ppermute | solution.py:806
  19.8 1.5 %shard_map.97 = bf16[128,1024]{1,0:T(8,128)(2,1)S(1)} custom-call(bf16[12,128,128]{2,1,0:T(8,128)(2,1)S(1)} %get-tuple-element.48.refs_0_, bf16[8,128,128]{2,1,0:T(8,128)(2,1)S(1)} %get-tuple-element.53.refs_1_.refs_2_, bf16[8,128,128]{2,1,0:T(8,128)(2,1)S(1)} %get-tuple-element.54.refs_2_.refs_0_, ...), custom_call_target="tpu_custom_call" | custom-call | flops 2147483648 | bytes 1024 | tf_op jit(solution)/shard_map/pallas_call | solution.py:677
  21.3 2.0 %collective-permute-start.8 = (bf16[8,128,128]{2,1,0:T(8,128)(2,1)S(1)}, bf16[8,128,128]{2,1,0:T(8,128)(2,1)S(1)}, u32[]{:S(2)}, u32[]{:S(2)}) collective-permute-start(bf16[8,128,128]{2,1,0:T(8,128)(2,1)S(1)} %get-tuple-element.53.refs_1_.refs_2_), channel_id=1, source_target_pairs={{16,0},{0,16},{17,1},{1,17},{18,2},{2,18},{19,3},{3,19},{20,4},{4,... | collective-permute-start | bytes 786440 | tf_op jit(solution)/shard_map/ppermute | solution.py:769
  23.3 0.0 collective-permute-start.4
  23.3 0.0 copy-done.2
  23.3 0.0 copy-done.3
  23.3 1.8 %shard_map.94 = (bf16[128,1024]{1,0:T(8,128)(2,1)S(1)}, f32[8,1024]{1,0:T(8,128)S(1)}, f32[8,1024]{1,0:T(8,128)S(1)}) custom-call(bf16[12,128,128]{2,1,0:T(8,128)(2,1)S(1)} %get-tuple-element.48.refs_0_, bf16[8,128,128]{2,1,0:T(8,128)(2,1)S(1)} %get-tuple-element.53.refs_1_.refs_2_, bf16[8,128,128]{2,1,0:T(8,128)(2,1)S(1)} %get-tuple-element.54.refs_2_.refs_0_, ...), custom_call_target="tpu_custom_call" | custom-call | flops 2147483648 | bytes 1024 | tf_op jit(solution)/shard_map/pallas_call | solution.py:677
  25.1 2.5 %collective-permute-done.3.other_ref = bf16[128,1024]{1,0:T(8,128)(2,1)S(1)} collective-permute-done((bf16[128,1024]{1,0:T(8,128)(2,1)S(1)}, bf16[128,1024]{1,0:T(8,128)(2,1)S(1)}, u32[]{:S(2)}, u32[]{:S(2)}) %collective-permute-start.3) | collective-permute-done | bytes 262176 | tf_op jit(solution)/shard_map/ppermute | solution.py:806
  27.6 0.1 shard_map.96.one_ref
  27.6 0.0 collective-permute-done.4.other_ref
  27.7 0.0 collective-permute-done.5.refs_0_.refs_1_
  27.7 0.1 shard_map.98.refs_0_
  27.7 1.8 %collective-permute-start.7 = (bf16[128,1024]{1,0:T(8,128)(2,1)S(1)}, bf16[128,1024]{1,0:T(8,128)(2,1)S(1)}, u32[]{:S(2)}, u32[]{:S(2)}) collective-permute-start(bf16[128,1024]{1,0:T(8,128)(2,1)S(1)} %shard_map.98.refs_0_), channel_id=1, source_target_pairs={{16,0},{0,16},{17,1},{1,17},{18,2},{2,18},{19,3},{3,19},{20,4},{4,... | collective-permute-start | bytes 786440 | tf_op jit(solution)/shard_map/ppermute | solution.py:769
  29.5 0.3 collective-permute-start.9
  29.8 1.7 %collective-permute-start.6 = (bf16[4,128,128]{2,1,0:T(8,128)(2,1)S(1)}, bf16[4,128,128]{2,1,0:T(8,128)(2,1)S(1)}, u32[]{:S(2)}, u32[]{:S(2)}) collective-permute-start(bf16[4,128,128]{2,1,0:T(8,128)(2,1)S(1)} %get-tuple-element.49.refs_3_.refs_0_), channel_id=1, source_target_pairs={{16,0},{0,16},{17,1},{1,17},{18,2},{2,18},{19,3},{3,19},{20,4},{4,... | collective-permute-start | bytes 393224 | tf_op jit(solution)/shard_map/ppermute | solution.py:769
  31.5 1.1 %collective-permute-done.8.refs_4_.refs_3_ = bf16[8,128,128]{2,1,0:T(8,128)(2,1)S(1)} collective-permute-done((bf16[8,128,128]{2,1,0:T(8,128)(2,1)S(1)}, bf16[8,128,128]{2,1,0:T(8,128)(2,1)S(1)}, u32[]{:S(2)}, u32[]{:S(2)}) %collective-permute-start.8) | collective-permute-done | bytes 262176 | tf_op jit(solution)/shard_map/ppermute | solution.py:769
  32.7 0.4 shard_map.100
  33.1 5.2 %collective-permute-done.7.refs_1_ = bf16[128,1024]{1,0:T(8,128)(2,1)S(1)} collective-permute-done((bf16[128,1024]{1,0:T(8,128)(2,1)S(1)}, bf16[128,1024]{1,0:T(8,128)(2,1)S(1)}, u32[]{:S(2)}, u32[]{:S(2)}) %collective-permute-start.7) | collective-permute-done | bytes 262176 | tf_op jit(solution)/shard_map/ppermute | solution.py:769
  38.3 6.3 %shard_map.99.refs_4_.refs_2_ = bf16[8,128,256]{2,1,0:T(8,128)(2,1)S(1)} custom-call(bf16[128,1024]{1,0:T(8,128)(2,1)S(1)} %shard_map.98.refs_0_, bf16[128,1024]{1,0:T(8,128)(2,1)S(1)} %collective-permute-done.7.refs_1_, f32[8,1024]{1,0:T(8,128)S(1)} %get-tuple-element.51.refs_2_, f32[8,1024]{1,0:T(8,128)S(1)} %get-tuple-element.52.refs_3_, ...), custom_call_target="tpu_custom_call" | custom-call | flops 8589934592 | bytes 1024 | tf_op jit(solution)/shard_map/pallas_call | solution.py:677
  44.6 0.0 collective-permute-done.9.refs_1_
  44.6 1.6 %shard_map.101 = (bf16[128,8,512]{2,1,0:T(8,128)(2,1)}, f32[1024,128]{1,0:T(8,128)S(1)}) custom-call(bf16[8,128,128]{2,1,0:T(8,128)(2,1)S(1)} %get-tuple-element.54.refs_2_.refs_0_, bf16[8,128,128]{2,1,0:T(8,128)(2,1)S(1)} %collective-permute-done.9.refs_1_, bf16[10,256,256]{2,1,0:T(8,128)(2,1)S(1)} %get-tuple-element.55.refs_2_, ...), custom_call_target="tpu_custom_call" | custom-call | flops 2147483648 | bytes 1024 | tf_op jit(solution)/shard_map/pallas_call | solution.py:677
  46.2 0.0 collective-permute-done.6.refs_1_
  46.2 1.1 %shard_map.102 = bf16[128,8,512]{2,1,0:T(8,128)(2,1)} custom-call(bf16[4,128,128]{2,1,0:T(8,128)(2,1)S(1)} %get-tuple-element.49.refs_3_.refs_0_, bf16[4,128,128]{2,1,0:T(8,128)(2,1)S(1)} %collective-permute-done.6.refs_1_, bf16[8,128,256]{2,1,0:T(8,128)(2,1)S(1)} %shard_map.99.refs_4_.refs_2_, ...), custom_call_target="tpu_custom_call", output_to_operand_aliasing={{}: (4, {})} | custom-call | flops 1073741824 | bytes 1024 | tf_op jit(solution)/shard_map/pallas_call | solution.py:677
  (3 shorter events, 0.0 us)
Async XLA Ops:
  2.2 11.3 %collective-permute-start = (bf16[592,128]{1,0:T(8,128)(2,1)}, bf16[592,128]{1,0:T(8,128)(2,1)S(1)}, u32[]{:S(2)}, u32[]{:S(2)}) collective-permute-start(bf16[592,128]{1,0:T(8,128)(2,1)} %get-tuple-element.32), channel_id=1, source_target_pairs={{1,2},{2,1},{3,4},{4,3},{5,6},{6,5},{7,8},{8,7},{9,10},{10,9},{11,... | collective-permute-start | bytes 454664 | tf_op jit(solution)/shard_map/ppermute | solution.py:742
  7.7 5.8 %collective-permute-start.1 = (bf16[592,128]{1,0:T(8,128)(2,1)}, bf16[592,128]{1,0:T(8,128)(2,1)S(1)}, u32[]{:S(2)}, u32[]{:S(2)}) collective-permute-start(bf16[592,128]{1,0:T(8,128)(2,1)} %get-tuple-element.33), channel_id=1, source_target_pairs={{0,1},{1,0},{2,3},{3,2},{4,5},{5,4},{6,7},{7,6},{8,9},{9,8},{10,11... | collective-permute-start | bytes 454664 | tf_op jit(solution)/shard_map/ppermute | solution.py:741
  7.7 1.6 %copy-start = (f32[128,8,512]{2,1,0:T(8,128)S(1)}, f32[128,8,512]{2,1,0:T(8,128)}, u32[]{:S(2)}) copy-start(f32[128,8,512]{2,1,0:T(8,128)} %param.9) | copy-start | bytes 6291460
  9.3 0.8 %copy-start.4 = (f32[16,512]{1,0:T(8,128)S(1)}, f32[16,512]{1,0:T(8,128)}, u32[]{:S(2)}) copy-start(f32[16,512]{1,0:T(8,128)} %get-tuple-element.34.refs_4_.small_ref) | copy-start | bytes 98308
  10.1 3.4 %copy-start.1 = (bf16[48,128]{1,0:T(8,128)(2,1)S(1)}, bf16[48,128]{1,0:T(8,128)(2,1)}, u32[]{:S(2)}) copy-start(bf16[48,128]{1,0:T(8,128)(2,1)} %get-tuple-element.44.refs_4_) | copy-start | bytes 36868
  10.1 5.6 %copy-start.5 = (f32[16,512]{1,0:T(8,128)S(1)}, f32[16,512]{1,0:T(8,128)}, u32[]{:S(2)}) copy-start(f32[16,512]{1,0:T(8,128)} %get-tuple-element.34.refs_4_.small_ref) | copy-start | bytes 98308
  13.5 3.9 %collective-permute-start.2 = (bf16[112,128]{1,0:T(8,128)(2,1)S(1)}, bf16[112,128]{1,0:T(8,128)(2,1)S(1)}, u32[]{:S(2)}, u32[]{:S(2)}) collective-permute-start(bf16[112,128]{1,0:T(8,128)(2,1)S(1)} %pad_maximum_fusion), channel_id=1, source_target_pairs={{16,0},{0,16},{17,1},{1,17},{18,2},{2,18},{19,3},{3,19},{20,4},{4,... | collective-permute-start | bytes 86024 | tf_op jit(solution)/shard_map/ppermute | solution.py:773
  15.1 12.6 %collective-permute-start.5 = (bf16[12,128,128]{2,1,0:T(8,128)(2,1)S(1)}, bf16[12,128,128]{2,1,0:T(8,128)(2,1)S(1)}, u32[]{:S(2)}, u32[]{:S(2)}) collective-permute-start(bf16[12,128,128]{2,1,0:T(8,128)(2,1)S(1)} %get-tuple-element.48.refs_0_), channel_id=1, source_target_pairs={{16,0},{0,16},{17,1},{1,17},{18,2},{2,18},{19,3},{3,19},{20,4},{4,... | collective-permute-start | bytes 1179656 | tf_op jit(solution)/shard_map/ppermute | solution.py:769
  15.6 1.8 %copy-start.6 = (s32[2048]{0:T(1024)S(1)}, s32[2048]{0:T(1024)}, u32[]{:S(2)}) copy-start(s32[2048]{0:T(1024)} %param.12) | copy-start | bytes 24580
  15.6 1.8 %copy-start.7 = (s32[2048]{0:T(1024)S(1)}, s32[2048]{0:T(1024)}, u32[]{:S(2)}) copy-start(s32[2048]{0:T(1024)} %param.13) | copy-start | bytes 24580
  19.0 4.3 %copy-start.2 = (f32[32768]{0:T(1024)S(1)}, f32[32768]{0:T(1024)}, u32[]{:S(2)}) copy-start(f32[32768]{0:T(1024)} %param.14) | copy-start | bytes 393220
  19.0 4.3 %copy-start.3 = (f32[32768]{0:T(1024)S(1)}, f32[32768]{0:T(1024)}, u32[]{:S(2)}) copy-start(f32[32768]{0:T(1024)} %param.15) | copy-start | bytes 393220
  19.0 8.6 %collective-permute-start.3 = (bf16[128,1024]{1,0:T(8,128)(2,1)S(1)}, bf16[128,1024]{1,0:T(8,128)(2,1)S(1)}, u32[]{:S(2)}, u32[]{:S(2)}) collective-permute-start(bf16[128,1024]{1,0:T(8,128)(2,1)S(1)} %shard_map.95.refs_8_), channel_id=1, source_target_pairs={{1,2},{2,1},{3,4},{4,3},{5,6},{6,5},{7,8},{8,7},{9,10},{10,9},{11,... | collective-permute-start | bytes 786440 | tf_op jit(solution)/shard_map/ppermute | solution.py:806
  21.3 11.3 %collective-permute-start.8 = (bf16[8,128,128]{2,1,0:T(8,128)(2,1)S(1)}, bf16[8,128,128]{2,1,0:T(8,128)(2,1)S(1)}, u32[]{:S(2)}, u32[]{:S(2)}) collective-permute-start(bf16[8,128,128]{2,1,0:T(8,128)(2,1)S(1)} %get-tuple-element.53.refs_1_.refs_2_), channel_id=1, source_target_pairs={{16,0},{0,16},{17,1},{1,17},{18,2},{2,18},{19,3},{3,19},{20,4},{4,... | collective-permute-start | bytes 786440 | tf_op jit(solution)/shard_map/ppermute | solution.py:769
  23.3 4.3 %collective-permute-start.4 = (bf16[128,1024]{1,0:T(8,128)(2,1)S(1)}, bf16[128,1024]{1,0:T(8,128)(2,1)S(1)}, u32[]{:S(2)}, u32[]{:S(2)}) collective-permute-start(bf16[128,1024]{1,0:T(8,128)(2,1)S(1)} %shard_map.97), channel_id=1, source_target_pairs={{0,1},{1,0},{2,3},{3,2},{4,5},{5,4},{6,7},{7,6},{8,9},{9,8},{10,11... | collective-permute-start | bytes 786440 | tf_op jit(solution)/shard_map/ppermute | solution.py:807
  27.7 10.5 %collective-permute-start.7 = (bf16[128,1024]{1,0:T(8,128)(2,1)S(1)}, bf16[128,1024]{1,0:T(8,128)(2,1)S(1)}, u32[]{:S(2)}, u32[]{:S(2)}) collective-permute-start(bf16[128,1024]{1,0:T(8,128)(2,1)S(1)} %shard_map.98.refs_0_), channel_id=1, source_target_pairs={{16,0},{0,16},{17,1},{1,17},{18,2},{2,18},{19,3},{3,19},{20,4},{4,... | collective-permute-start | bytes 786440 | tf_op jit(solution)/shard_map/ppermute | solution.py:769
  29.5 15.0 %collective-permute-start.9 = (bf16[8,128,128]{2,1,0:T(8,128)(2,1)S(1)}, bf16[8,128,128]{2,1,0:T(8,128)(2,1)S(1)}, u32[]{:S(2)}, u32[]{:S(2)}) collective-permute-start(bf16[8,128,128]{2,1,0:T(8,128)(2,1)S(1)} %get-tuple-element.54.refs_2_.refs_0_), channel_id=1, source_target_pairs={{16,0},{0,16},{17,1},{1,17},{18,2},{2,18},{19,3},{3,19},{20,4},{4,... | collective-permute-start | bytes 786440 | tf_op jit(solution)/shard_map/ppermute | solution.py:769
  29.8 16.4 %collective-permute-start.6 = (bf16[4,128,128]{2,1,0:T(8,128)(2,1)S(1)}, bf16[4,128,128]{2,1,0:T(8,128)(2,1)S(1)}, u32[]{:S(2)}, u32[]{:S(2)}) collective-permute-start(bf16[4,128,128]{2,1,0:T(8,128)(2,1)S(1)} %get-tuple-element.49.refs_3_.refs_0_), channel_id=1, source_target_pairs={{16,0},{0,16},{17,1},{1,17},{18,2},{2,18},{19,3},{3,19},{20,4},{4,... | collective-permute-start | bytes 393224 | tf_op jit(solution)/shard_map/ppermute | solution.py:769

commit v5 on v4

--- a/solution.py
+++ b/solution.py
@@ -155,25 +155,11 @@
     return jnp.concatenate([value, jnp.zeros((count, value.shape[1]), value.dtype)], axis=0)
 
 
-def middle_kernel(*refs, groups):
-    field_refs = refs[:groups]
-    small_ref, middle_ref, kept_ref = refs[groups : groups + 3]
-    (
-        edge_high,
-        edge_low,
-        part_ref,
-        second_ref,
-        u_high,
-        u_low,
-        first_high,
-        first_low,
-        second_high,
-        second_low,
-    ) = refs[groups + 3 :]
-    late, members, _ = kept_ref.shape
-    levels = 2 * late
-    early = (groups - 2) * levels - late
-    columns = groups * LANES
+def operator_kernel(
+    small_ref, both_ref, part_ref, second_ref, first_high, first_low, second_high, second_low
+):
+    columns = small_ref.shape[1]
+    groups = columns // LANES
     coef = padded(small_ref[0:6, :], 2)
     reach = padded(small_ref[8:14, :], 2)
     moved_coef = pltpu.roll(coef, HALO, axis=1)
@@ -197,8 +183,8 @@
         row, lane = (g - 1) * LANES, (g - 1) * LANES
         second_high[row : row + LANES + 2 * HALO, lane : lane + LANES] = seconds[g][0]
         second_low[row : row + LANES + 2 * HALO, lane : lane + LANES] = seconds[g][1]
-    both = split2(
-        dot3((first_high[...], first_low[...]), (second_high[...], second_low[...]))
+    both_ref[...] = joined(
+        split2(dot3((first_high[...], first_low[...]), (second_high[...], second_low[...])))
     )
 
     for k, g in enumerate((0, groups - 1)):
@@ -211,25 +197,27 @@
         else:
             part_ref[k] = padded(dot3(firsts[g], [value[:128, :] for value in second]), 64)
 
+
+def middle_kernel(*refs, groups):
+    field_refs = refs[:groups]
+    both_ref, middle_ref, kept_ref, edge_ref, fields = refs[groups:]
+    early, members, _ = middle_ref.shape
+    levels = field_refs[0].shape[0] // members
     lane = iota((members, LANES), 1)
     for level in range(levels):
         spot = slice(level * members, (level + 1) * members)
-        for group, ref in enumerate(field_refs):
-            own = ref[pl.ds(level, members, stride=levels), :]
-            high, low = split2(own)
-            u_high[spot, group * LANES : (group + 1) * LANES] = high
-            u_low[spot, group * LANES : (group + 1) * LANES] = low
-        for pieces, ref in ((u_high, edge_high), (u_low, edge_low)):
-            turned = [
-                pltpu.roll(pieces[spot, g * LANES : (g + 1) * LANES].astype(F32), 64, axis=1)
-                for g in (0, 1, groups - 2, groups - 1)
-            ]
-            zero = jnp.zeros_like(turned[0])
-            ref[0, spot, 0:LANES] = jnp.where(lane < 64, zero, turned[0]).astype(BF16)
-            ref[0, spot, LANES:] = jnp.where(lane < 64, turned[0], turned[1]).astype(BF16)
-            ref[1, spot, 0:LANES] = jnp.where(lane < 64, turned[2], turned[3]).astype(BF16)
-            ref[1, spot, LANES:] = jnp.where(lane < 64, turned[3], zero).astype(BF16)
-    result = dot3((u_high[...], u_low[...]), both)
+        own = [ref[pl.ds(level, members, stride=levels), :] for ref in field_refs]
+        for group in range(groups):
+            fields[spot, group * LANES : (group + 1) * LANES] = own[group].astype(BF16)
+        turned = [pltpu.roll(own[g], 64, axis=1) for g in (0, 1, groups - 2, groups - 1)]
+        zero = jnp.zeros_like(turned[0])
+        edge_ref[0, spot, 0:LANES] = jnp.where(lane < 64, zero, turned[0]).astype(BF16)
+        edge_ref[0, spot, LANES:] = jnp.where(lane < 64, turned[0], turned[1]).astype(BF16)
+        edge_ref[1, spot, 0:LANES] = jnp.where(lane < 64, turned[2], turned[3]).astype(BF16)
+        edge_ref[1, spot, LANES:] = jnp.where(lane < 64, turned[3], zero).astype(BF16)
+    result = dot(fields[...], both_ref[...])
+    half = result.shape[1] // 2
+    result = result[:, :half] + result[:, half:]
     for k in range((groups - 2) * levels):
         level, lane = k % levels, (k // levels) * LANES
         value = result[level * members : (level + 1) * members, lane : lane + LANES].astype(BF16)
@@ -240,7 +228,7 @@
 
 
 def edge_kernel(
-    a_ref, b_ref, small_ref, edge_high, edge_low, part_ref, second_ref, kept_ref, first_ref, next_ref, last_ref, u_high
+    a_ref, b_ref, small_ref, edge_ref, part_ref, second_ref, kept_ref, first_ref, next_ref, last_ref, fields
 ):
     levels, members, _ = next_ref.shape
     columns = small_ref.shape[1]
@@ -294,21 +282,23 @@
             for j in range(2):
                 spot = slice(top + j * half, top + (j + 1) * half)
                 if k == 0:
-                    own = edge_high[k, spot, 0:LANES].astype(F32)
-                    u_high[k, spot, 0:LANES] = jnp.where(lane < 64, pair[j], own).astype(BF16)
-                    u_high[k, spot, LANES:] = edge_high[k, spot, LANES:]
+                    own = edge_ref[k, spot, 0:LANES].astype(F32)
+                    fields[k, spot, 0:LANES] = jnp.where(lane < 64, pair[j], own).astype(BF16)
+                    fields[k, spot, LANES:] = edge_ref[k, spot, LANES:]
                 else:
-                    own = edge_high[k, spot, LANES:].astype(F32)
-                    u_high[k, spot, LANES:] = jnp.where(lane < 64, own, pair[j]).astype(BF16)
-                    u_high[k, spot, 0:LANES] = edge_high[k, spot, 0:LANES]
-        result = dot3((u_high[k], edge_low[k]), operators[k])
+                    own = edge_ref[k, spot, LANES:].astype(F32)
+                    fields[k, spot, LANES:] = jnp.where(lane < 64, own, pair[j]).astype(BF16)
+                    fields[k, spot, 0:LANES] = edge_ref[k, spot, 0:LANES]
+        result = dot(fields[k], joined(operators[k]))
+        result = result[:, :LANES] + result[:, LANES:]
         part = levels // 2
+        kept = kept_ref.shape[0]
         if k == 0:
-            first_ref[:part] = kept_ref[...]
+            first_ref[:kept] = kept_ref[...]
         for level in range(levels):
             value = result[level * members : (level + 1) * members, :].astype(BF16)
             if k == 0 and level < part:
-                first_ref[part + level] = value
+                first_ref[kept + level] = value
             elif k == 0:
                 next_ref[level - part] = value
             elif level < part:
@@ -368,9 +358,10 @@
 
 def whole(middle_ref, first_ref, next_ref, last_ref):
     part, members, _ = last_ref.shape
-    middle = jnp.concatenate([middle_ref[...], first_ref[:part]], axis=0)
+    kept = first_ref.shape[0] - part
+    middle = jnp.concatenate([middle_ref[...], first_ref[:kept]], axis=0)
     groups = [
-        jnp.concatenate([first_ref[part:], next_ref[:part]], axis=0),
+        jnp.concatenate([first_ref[kept:], next_ref[:part]], axis=0),
         *(middle[k : k + 2 * part] for k in range(0, middle.shape[0], 2 * part)),
         jnp.concatenate([next_ref[part:], last_ref[...]], axis=0),
     ]
@@ -741,27 +732,34 @@
     from_b = lax.ppermute(b, "tile", even_pairs)
     from_a = lax.ppermute(a, "tile", odd_pairs)
     flat_rows = members * levels
-    middle, kept, edge_high, edge_low, part, second = call(
-        functools.partial(middle_kernel, groups=groups),
-        [
-            jax.ShapeDtypeStruct(((groups - 2) * levels - levels // 2, members, LANES), BF16),
-            jax.ShapeDtypeStruct((levels // 2, members, LANES), BF16),
-            jax.ShapeDtypeStruct((2, flat_rows, 2 * LANES), BF16),
-            jax.ShapeDtypeStruct((2, flat_rows, 2 * LANES), BF16),
+    kept_levels = levels // 4
+    both, part, second = call(
+        operator_kernel,
+        [
+            jax.ShapeDtypeStruct((columns, 2 * (columns - 2 * LANES)), BF16),
             jax.ShapeDtypeStruct((2, 2 * LANES, LANES), F32),
             jax.ShapeDtypeStruct((4, 2 * LANES, LANES), BF16),
         ],
-        [flat] * groups + [small],
-        [
-            pltpu.VMEM((flat_rows, columns), BF16),
-            pltpu.VMEM((flat_rows, columns), BF16),
+        [small],
+        [
             pltpu.VMEM((columns, columns - LANES), BF16),
             pltpu.VMEM((columns, columns - LANES), BF16),
             pltpu.VMEM((columns - LANES, columns - 2 * LANES), BF16),
             pltpu.VMEM((columns - LANES, columns - 2 * LANES), BF16),
         ],
+        cost=2,
+    )
+    middle, kept, border = call(
+        functools.partial(middle_kernel, groups=groups),
+        [
+            jax.ShapeDtypeStruct(((groups - 2) * levels - kept_levels, members, LANES), BF16),
+            jax.ShapeDtypeStruct((kept_levels, members, LANES), BF16),
+            jax.ShapeDtypeStruct((2, flat_rows, 2 * LANES), BF16),
+        ],
+        [flat] * groups + [both],
+        [pltpu.VMEM((flat_rows, columns), BF16)],
         in_specs=[group_spec(flat_rows, group) for group in range(groups)] + [vmem()],
-        cost=4,
+        cost=3,
     )
     passed = jnp.concatenate([from_a[half + 48 :], from_b[half + 48 :], lists], axis=0)
 
@@ -774,11 +772,11 @@
     first, after, last = call(
         edge_kernel,
         [
-            jax.ShapeDtypeStruct((levels, members, LANES), BF16),
+            jax.ShapeDtypeStruct((kept_levels + levels // 2, members, LANES), BF16),
             jax.ShapeDtypeStruct((levels, members, LANES), BF16),
             jax.ShapeDtypeStruct((levels // 2, members, LANES), BF16),
         ],
-        [from_a, from_b, small, edge_high, edge_low, part, second, kept],
+        [from_a, from_b, small, border, part, second, kept],
         [pltpu.VMEM((2, flat_rows, 2 * LANES), BF16)],
         cost=2,
     )

time: 47.6 us -> 45.4 us (0.954)
  Pallas kernels: 21.2 us -> 19.5 us
  starting transfers between devices: 14.2 us -> 15.8 us
  local copies, waits for them, and re-layouts: 2.38 us -> 1.23 us
  waiting for transfers between devices: 9.26 us -> 8.32 us
    ppermute x1, starting transfers between devices: 0.79 us -> 3.58 us  [shards(): back_a = lax.ppermute(to_a, 'tile', odd_pairs)]
    ppermute x1, waiting for transfers between devices: 2.49 us -> 0.15 us  [shards(): back_a = lax.ppermute(to_a, 'tile', odd_pairs)]
    pallas_call x12 -> x13, Pallas kernels: 21.2 us -> 19.5 us  [call(): pl.pallas_call(kernel, grid=(1,), out_shape=outs, in_specs=in_specs or [v...]
    ppermute x5, starting transfers between devices: 6.32 us -> 5.05 us  [swapped(): return [value] + [lax.ppermute(sent, 'mem', turn) for turn in turns]]
    unnamed x16 -> x14, local copies, waits for them, and re-layouts: 2.38 us -> 1.22 us
    ppermute x5, waiting for transfers between devices: 6.29 us -> 7.18 us  [swapped(): return [value] + [lax.ppermute(sent, 'mem', turn) for turn in turns]]
    ppermute x1, waiting for transfers between devices: 0.47 us -> 0.99 us  [shards(): passed = [lax.ppermute(passed, 'mem', turn) for turn in turns]]
  transfers between devices with their start and end apart: 10 -> 10, of which waited for: 4 -> 5; matrix products, arithmetic and copies ran while one was open for 0% -> 0% of each run, Pallas kernels for 38% -> 36%
where the time goes in v5:
time: 45.4 us; the launch traced here: 45.1 us
  Pallas kernels  19.5 us (43%)
  starting transfers between devices  15.8 us (35%)
  waiting for transfers between devices  8.32 us (18%)
  local copies, waits for them, and re-layouts  1.23 us (3%)
    pallas_call x13, Pallas kernels, call(): pl.pallas_call(kernel, grid=(1,), out_shape=outs, in_specs=in_specs or [v...  19.5 us
    ppermute x5, waiting for transfers between devices, swapped(): return [value] + [lax.ppermute(sent, 'mem', turn) for turn in turns]  7.18 us
    ppermute x1, starting transfers between devices, shards(): from_a = lax.ppermute(a, 'tile', odd_pairs)  5.51 us
    ppermute x5, starting transfers between devices, swapped(): return [value] + [lax.ppermute(sent, 'mem', turn) for turn in turns]  5.05 us
    ppermute x1, starting transfers between devices, shards(): back_a = lax.ppermute(to_a, 'tile', odd_pairs)  3.58 us
    ppermute x1, starting transfers between devices, shards(): passed = [lax.ppermute(passed, 'mem', turn) for turn in turns]  1.62 us
    unnamed x14, local copies, waits for them, and re-layouts  1.22 us
    ppermute x1, waiting for transfers between devices, shards(): passed = [lax.ppermute(passed, 'mem', turn) for turn in turns]  0.99 us
  transfers between devices with their start and end apart: 10, of which 5 were waited for; matrix products, arithmetic and copies ran while one was open for 0% of the time, Pallas kernels for 36%

profile of v5, /device:TPU:0, one launch (start us, length us, event | category | flops | bytes accessed | tf_op | source)
XLA Modules:
  0.0 45.1 jit_solution(6419579654459348127)
XLA Ops:
  0.0 2.2 %shard_map.91 = (bf16[592,128]{1,0:T(8,128)(2,1)}, bf16[592,128]{1,0:T(8,128)(2,1)}, bf16[48,128]{1,0:T(8,128)(2,1)}, f32[16,512]{1,0:T(8,128)}) custom-call(f32[1024,512]{1,0:T(8,128)} %bitcast.5, f32[6,512]{1,0:T(8,128)} %coef_hbm.1, s32[6,512]{1,0:T(8,128)} %nbr_hbm.1, s32[4,1,128]{2,1,0:T(1,128)} %index_hbm.1, s32[4,1,128]{2,1,0:T(1,128)} %weight_hbm.1), custom_call_target="tpu_custom_call" | custom-call | bytes 1024 | tf_op jit(solution)/shard_map/pallas_call | solution.py:668
  2.2 5.5 %collective-permute-start = (bf16[592,128]{1,0:T(8,128)(2,1)}, bf16[592,128]{1,0:T(8,128)(2,1)S(1)}, u32[]{:S(2)}, u32[]{:S(2)}) collective-permute-start(bf16[592,128]{1,0:T(8,128)(2,1)} %get-tuple-element.32), channel_id=1, source_target_pairs={{1,2},{2,1},{3,4},{4,3},{5,6},{6,5},{7,8},{8,7},{9,10},{10,9},{11,... | collective-permute-start | bytes 454664 | tf_op jit(solution)/shard_map/ppermute | solution.py:733
  7.7 0.0 collective-permute-start.1
  7.7 0.0 copy-start.4
  7.7 0.8 %copy-done.4 = f32[16,512]{1,0:T(8,128)S(1)} copy-done((f32[16,512]{1,0:T(8,128)S(1)}, f32[16,512]{1,0:T(8,128)}, u32[]{:S(2)}) %copy-start.4) | copy-done | bytes 32792
  8.5 0.0 copy-start
  8.5 1.1 %shard_map.92 = (bf16[512,512]{1,0:T(8,128)(2,1)S(1)}, f32[2,256,128]{2,1,0:T(8,128)S(1)}, bf16[4,256,128]{2,1,0:T(8,128)(2,1)S(1)}) custom-call(f32[16,512]{1,0:T(8,128)S(1)} %copy-done.4), custom_call_target="tpu_custom_call" | custom-call | flops 2147483648 | bytes 1024 | tf_op jit(solution)/shard_map/pallas_call | solution.py:668
  9.6 0.4 copy-done
  10.1 0.0 copy-start.1
  10.1 1.1 %shard_map.93 = (bf16[14,128,128]{2,1,0:T(8,128)(2,1)S(1)}, bf16[2,128,128]{2,1,0:T(8,128)(2,1)S(1)}, bf16[2,1024,256]{2,1,0:T(8,128)(2,1)S(1)}) custom-call(f32[1024,512]{1,0:T(8,128)S(1)} %bitcast.6, f32[1024,512]{1,0:T(8,128)S(1)} %bitcast.7, f32[1024,512]{1,0:T(8,128)S(1)} %bitcast.8, f32[1024,512]{1,0:T(8,128)S(1)} %bitcast.9, ...), custom_call_target="tpu_custom_call" | custom-call | flops 3221225472 | bytes 1024 | tf_op jit(solution)/shard_map/pallas_call | solution.py:668
  11.1 0.0 collective-permute-done.a_ref.refs_4_
  11.2 0.0 collective-permute-done.1.b_ref.refs_4_
  11.2 0.0 copy-done.1
  11.2 1.6 %collective-permute-start.2 = (bf16[112,128]{1,0:T(8,128)(2,1)S(1)}, bf16[112,128]{1,0:T(8,128)(2,1)S(1)}, u32[]{:S(2)}, u32[]{:S(2)}) collective-permute-start(bf16[112,128]{1,0:T(8,128)(2,1)S(1)} %pad_maximum_fusion), channel_id=1, source_target_pairs={{16,0},{0,16},{17,1},{1,17},{18,2},{2,18},{19,3},{3,19},{20,4},{4,... | collective-permute-start | bytes 86024 | tf_op jit(solution)/shard_map/ppermute | solution.py:771
  12.8 0.5 %collective-permute-start.5 = (bf16[14,128,128]{2,1,0:T(8,128)(2,1)S(1)}, bf16[14,128,128]{2,1,0:T(8,128)(2,1)S(1)}, u32[]{:S(2)}, u32[]{:S(2)}) collective-permute-start(bf16[14,128,128]{2,1,0:T(8,128)(2,1)S(1)} %get-tuple-element.48.refs_0_), channel_id=1, source_target_pairs={{16,0},{0,16},{17,1},{1,17},{18,2},{2,18},{19,3},{3,19},{20,4},{4,... | collective-permute-start | bytes 1376264 | tf_op jit(solution)/shard_map/ppermute | solution.py:767
  13.3 0.0 copy-start.5
  13.3 0.0 copy-start.6
  13.3 0.8 %shard_map.94 = (bf16[6,128,128]{2,1,0:T(8,128)(2,1)S(1)}, bf16[8,128,128]{2,1,0:T(8,128)(2,1)S(1)}, bf16[4,128,128]{2,1,0:T(8,128)(2,1)S(1)}) custom-call(bf16[592,128]{1,0:T(8,128)(2,1)S(1)} %collective-permute-done.a_ref.refs_4_, bf16[592,128]{1,0:T(8,128)(2,1)S(1)} %collective-permute-done.1.b_ref.refs_4_, f32[16,512]{1,0:T(8,128)S(1)} %copy-done.4, ...), custom_call_target="tpu_custom_call" | custom-call | flops 2147483648 | bytes 1024 | tf_op jit(solution)/shard_map/pallas_call | solution.py:668
  14.1 1.0 %collective-permute-done.2.refs_5_ = bf16[112,128]{1,0:T(8,128)(2,1)S(1)} collective-permute-done((bf16[112,128]{1,0:T(8,128)(2,1)S(1)}, bf16[112,128]{1,0:T(8,128)(2,1)S(1)}, u32[]{:S(2)}, u32[]{:S(2)}) %collective-permute-start.2) | collective-permute-done | bytes 28704 | tf_op jit(solution)/shard_map/ppermute | solution.py:771
  15.1 0.0 copy-done.5
  15.1 0.0 copy-done.6
  15.1 1.5 %shard_map.96.refs_8_ = bf16[128,1024]{1,0:T(8,128)(2,1)S(1)} custom-call(bf16[14,128,128]{2,1,0:T(8,128)(2,1)S(1)} %get-tuple-element.48.refs_0_, bf16[6,128,128]{2,1,0:T(8,128)(2,1)S(1)} %get-tuple-element.53.refs_1_.refs_2_, bf16[8,128,128]{2,1,0:T(8,128)(2,1)S(1)} %get-tuple-element.54.refs_2_.refs_0_, ...), custom_call_target="tpu_custom_call" | custom-call | flops 2147483648 | bytes 1024 | tf_op jit(solution)/shard_map/pallas_call | solution.py:668
  16.7 0.0 copy-start.2
  16.7 0.0 copy-start.3
  16.7 3.6 %collective-permute-start.3 = (bf16[128,1024]{1,0:T(8,128)(2,1)S(1)}, bf16[128,1024]{1,0:T(8,128)(2,1)S(1)}, u32[]{:S(2)}, u32[]{:S(2)}) collective-permute-start(bf16[128,1024]{1,0:T(8,128)(2,1)S(1)} %shard_map.96.refs_8_), channel_id=1, source_target_pairs={{1,2},{2,1},{3,4},{4,3},{5,6},{6,5},{7,8},{8,7},{9,10},{10,9},{11,... | collective-permute-start | bytes 786440 | tf_op jit(solution)/shard_map/ppermute | solution.py:804
  20.3 1.5 %shard_map.98 = bf16[128,1024]{1,0:T(8,128)(2,1)S(1)} custom-call(bf16[14,128,128]{2,1,0:T(8,128)(2,1)S(1)} %get-tuple-element.48.refs_0_, bf16[6,128,128]{2,1,0:T(8,128)(2,1)S(1)} %get-tuple-element.53.refs_1_.refs_2_, bf16[8,128,128]{2,1,0:T(8,128)(2,1)S(1)} %get-tuple-element.54.refs_2_.refs_0_, ...), custom_call_target="tpu_custom_call" | custom-call | flops 2147483648 | bytes 1024 | tf_op jit(solution)/shard_map/pallas_call | solution.py:668
  21.8 1.6 %collective-permute-start.8 = (bf16[6,128,128]{2,1,0:T(8,128)(2,1)S(1)}, bf16[6,128,128]{2,1,0:T(8,128)(2,1)S(1)}, u32[]{:S(2)}, u32[]{:S(2)}) collective-permute-start(bf16[6,128,128]{2,1,0:T(8,128)(2,1)S(1)} %get-tuple-element.53.refs_1_.refs_2_), channel_id=1, source_target_pairs={{16,0},{0,16},{17,1},{1,17},{18,2},{2,18},{19,3},{3,19},{20,4},{4,... | collective-permute-start | bytes 589832 | tf_op jit(solution)/shard_map/ppermute | solution.py:767
  23.3 0.0 collective-permute-start.4
  23.3 0.0 copy-done.2
  23.3 0.0 copy-done.3
  23.3 1.8 %shard_map.95 = (bf16[128,1024]{1,0:T(8,128)(2,1)S(1)}, f32[8,1024]{1,0:T(8,128)S(1)}, f32[8,1024]{1,0:T(8,128)S(1)}) custom-call(bf16[14,128,128]{2,1,0:T(8,128)(2,1)S(1)} %get-tuple-element.48.refs_0_, bf16[6,128,128]{2,1,0:T(8,128)(2,1)S(1)} %get-tuple-element.53.refs_1_.refs_2_, bf16[8,128,128]{2,1,0:T(8,128)(2,1)S(1)} %get-tuple-element.54.refs_2_.refs_0_, ...), custom_call_target="tpu_custom_call" | custom-call | flops 2147483648 | bytes 1024 | tf_op jit(solution)/shard_map/pallas_call | solution.py:668
  25.1 0.1 collective-permute-done.3.other_ref
  25.2 0.1 shard_map.97.one_ref
  25.3 0.0 collective-permute-done.4.other_ref
  25.3 0.9 %collective-permute-done.5.refs_0_.refs_1_ = bf16[14,128,128]{2,1,0:T(8,128)(2,1)S(1)} collective-permute-done((bf16[14,128,128]{2,1,0:T(8,128)(2,1)S(1)}, bf16[14,128,128]{2,1,0:T(8,128)(2,1)S(1)}, u32[]{:S(2)}, u32[]{:S(2)}) %collective-permute-start.5) | collective-permute-done | bytes 458784 | tf_op jit(solution)/shard_map/ppermute | solution.py:767
  26.2 0.1 shard_map.99.refs_0_
  26.3 1.0 %collective-permute-start.7 = (bf16[128,1024]{1,0:T(8,128)(2,1)S(1)}, bf16[128,1024]{1,0:T(8,128)(2,1)S(1)}, u32[]{:S(2)}, u32[]{:S(2)}) collective-permute-start(bf16[128,1024]{1,0:T(8,128)(2,1)S(1)} %shard_map.99.refs_0_), channel_id=1, source_target_pairs={{16,0},{0,16},{17,1},{1,17},{18,2},{2,18},{19,3},{3,19},{20,4},{4,... | collective-permute-start | bytes 786440 | tf_op jit(solution)/shard_map/ppermute | solution.py:767
  27.3 1.1 %collective-permute-start.9 = (bf16[8,128,128]{2,1,0:T(8,128)(2,1)S(1)}, bf16[8,128,128]{2,1,0:T(8,128)(2,1)S(1)}, u32[]{:S(2)}, u32[]{:S(2)}) collective-permute-start(bf16[8,128,128]{2,1,0:T(8,128)(2,1)S(1)} %get-tuple-element.54.refs_2_.refs_0_), channel_id=1, source_target_pairs={{16,0},{0,16},{17,1},{1,17},{18,2},{2,18},{19,3},{3,19},{20,4},{4,... | collective-permute-start | bytes 786440 | tf_op jit(solution)/shard_map/ppermute | solution.py:767
  28.4 0.9 %collective-permute-start.6 = (bf16[4,128,128]{2,1,0:T(8,128)(2,1)S(1)}, bf16[4,128,128]{2,1,0:T(8,128)(2,1)S(1)}, u32[]{:S(2)}, u32[]{:S(2)}) collective-permute-start(bf16[4,128,128]{2,1,0:T(8,128)(2,1)S(1)} %get-tuple-element.49.refs_3_.refs_0_), channel_id=1, source_target_pairs={{16,0},{0,16},{17,1},{1,17},{18,2},{2,18},{19,3},{3,19},{20,4},{4,... | collective-permute-start | bytes 393224 | tf_op jit(solution)/shard_map/ppermute | solution.py:767
  29.3 1.1 %collective-permute-done.8.refs_4_.refs_3_ = bf16[6,128,128]{2,1,0:T(8,128)(2,1)S(1)} collective-permute-done((bf16[6,128,128]{2,1,0:T(8,128)(2,1)S(1)}, bf16[6,128,128]{2,1,0:T(8,128)(2,1)S(1)}, u32[]{:S(2)}, u32[]{:S(2)}) %collective-permute-start.8) | collective-permute-done | bytes 196640 | tf_op jit(solution)/shard_map/ppermute | solution.py:767
  30.4 0.4 shard_map.101
  30.9 5.2 %collective-permute-done.7.refs_1_ = bf16[128,1024]{1,0:T(8,128)(2,1)S(1)} collective-permute-done((bf16[128,1024]{1,0:T(8,128)(2,1)S(1)}, bf16[128,1024]{1,0:T(8,128)(2,1)S(1)}, u32[]{:S(2)}, u32[]{:S(2)}) %collective-permute-start.7) | collective-permute-done | bytes 262176 | tf_op jit(solution)/shard_map/ppermute | solution.py:767
  36.0 6.3 %shard_map.100.refs_4_.refs_2_ = bf16[8,128,256]{2,1,0:T(8,128)(2,1)S(1)} custom-call(bf16[128,1024]{1,0:T(8,128)(2,1)S(1)} %shard_map.99.refs_0_, bf16[128,1024]{1,0:T(8,128)(2,1)S(1)} %collective-permute-done.7.refs_1_, f32[8,1024]{1,0:T(8,128)S(1)} %get-tuple-element.51.refs_2_, f32[8,1024]{1,0:T(8,128)S(1)} %get-tuple-element.52.refs_3_, ...), custom_call_target="tpu_custom_call" | custom-call | flops 8589934592 | bytes 1024 | tf_op jit(solution)/shard_map/pallas_call | solution.py:668
  42.3 0.0 collective-permute-done.9.refs_1_
  42.3 1.6 %shard_map.102 = (bf16[128,8,512]{2,1,0:T(8,128)(2,1)}, f32[1024,128]{1,0:T(8,128)S(1)}) custom-call(bf16[8,128,128]{2,1,0:T(8,128)(2,1)S(1)} %get-tuple-element.54.refs_2_.refs_0_, bf16[8,128,128]{2,1,0:T(8,128)(2,1)S(1)} %collective-permute-done.9.refs_1_, bf16[10,256,256]{2,1,0:T(8,128)(2,1)S(1)} %get-tuple-element.55.refs_2_, ...), custom_call_target="tpu_custom_call" | custom-call | flops 2147483648 | bytes 1024 | tf_op jit(solution)/shard_map/pallas_call | solution.py:668
  43.9 0.0 collective-permute-done.6.refs_1_
  43.9 1.1 %shard_map.103 = bf16[128,8,512]{2,1,0:T(8,128)(2,1)} custom-call(bf16[4,128,128]{2,1,0:T(8,128)(2,1)S(1)} %get-tuple-element.49.refs_3_.refs_0_, bf16[4,128,128]{2,1,0:T(8,128)(2,1)S(1)} %collective-permute-done.6.refs_1_, bf16[8,128,256]{2,1,0:T(8,128)(2,1)S(1)} %shard_map.100.refs_4_.refs_2_, ...), custom_call_target="tpu_custom_call", output_to_operand_aliasing={{}: (4, {})} | custom-call | flops 1073741824 | bytes 1024 | tf_op jit(solution)/shard_map/pallas_call | solution.py:668
  (3 shorter events, 0.0 us)
Async XLA Ops:
  2.2 8.9 %collective-permute-start = (bf16[592,128]{1,0:T(8,128)(2,1)}, bf16[592,128]{1,0:T(8,128)(2,1)S(1)}, u32[]{:S(2)}, u32[]{:S(2)}) collective-permute-start(bf16[592,128]{1,0:T(8,128)(2,1)} %get-tuple-element.32), channel_id=1, source_target_pairs={{1,2},{2,1},{3,4},{4,3},{5,6},{6,5},{7,8},{8,7},{9,10},{10,9},{11,... | collective-permute-start | bytes 454664 | tf_op jit(solution)/shard_map/ppermute | solution.py:733
  7.7 3.4 %collective-permute-start.1 = (bf16[592,128]{1,0:T(8,128)(2,1)}, bf16[592,128]{1,0:T(8,128)(2,1)S(1)}, u32[]{:S(2)}, u32[]{:S(2)}) collective-permute-start(bf16[592,128]{1,0:T(8,128)(2,1)} %get-tuple-element.33), channel_id=1, source_target_pairs={{0,1},{1,0},{2,3},{3,2},{4,5},{5,4},{6,7},{7,6},{8,9},{9,8},{10,11... | collective-permute-start | bytes 454664 | tf_op jit(solution)/shard_map/ppermute | solution.py:732
  7.7 0.8 %copy-start.4 = (f32[16,512]{1,0:T(8,128)S(1)}, f32[16,512]{1,0:T(8,128)}, u32[]{:S(2)}) copy-start(f32[16,512]{1,0:T(8,128)} %get-tuple-element.34.small_ref) | copy-start | bytes 98308
  8.5 1.6 %copy-start = (f32[128,8,512]{2,1,0:T(8,128)S(1)}, f32[128,8,512]{2,1,0:T(8,128)}, u32[]{:S(2)}) copy-start(f32[128,8,512]{2,1,0:T(8,128)} %param.9) | copy-start | bytes 6291460
  10.1 1.1 %copy-start.1 = (bf16[48,128]{1,0:T(8,128)(2,1)S(1)}, bf16[48,128]{1,0:T(8,128)(2,1)}, u32[]{:S(2)}) copy-start(bf16[48,128]{1,0:T(8,128)(2,1)} %get-tuple-element.44.refs_4_) | copy-start | bytes 36868
  11.2 3.9 %collective-permute-start.2 = (bf16[112,128]{1,0:T(8,128)(2,1)S(1)}, bf16[112,128]{1,0:T(8,128)(2,1)S(1)}, u32[]{:S(2)}, u32[]{:S(2)}) collective-permute-start(bf16[112,128]{1,0:T(8,128)(2,1)S(1)} %pad_maximum_fusion), channel_id=1, source_target_pairs={{16,0},{0,16},{17,1},{1,17},{18,2},{2,18},{19,3},{3,19},{20,4},{4,... | collective-permute-start | bytes 86024 | tf_op jit(solution)/shard_map/ppermute | solution.py:771
  12.8 13.4 %collective-permute-start.5 = (bf16[14,128,128]{2,1,0:T(8,128)(2,1)S(1)}, bf16[14,128,128]{2,1,0:T(8,128)(2,1)S(1)}, u32[]{:S(2)}, u32[]{:S(2)}) collective-permute-start(bf16[14,128,128]{2,1,0:T(8,128)(2,1)S(1)} %get-tuple-element.48.refs_0_), channel_id=1, source_target_pairs={{16,0},{0,16},{17,1},{1,17},{18,2},{2,18},{19,3},{3,19},{20,4},{4,... | collective-permute-start | bytes 1376264 | tf_op jit(solution)/shard_map/ppermute | solution.py:767
  13.3 1.8 %copy-start.5 = (s32[2048]{0:T(1024)S(1)}, s32[2048]{0:T(1024)}, u32[]{:S(2)}) copy-start(s32[2048]{0:T(1024)} %param.12) | copy-start | bytes 24580
  13.3 1.8 %copy-start.6 = (s32[2048]{0:T(1024)S(1)}, s32[2048]{0:T(1024)}, u32[]{:S(2)}) copy-start(s32[2048]{0:T(1024)} %param.13) | copy-start | bytes 24580
  16.7 6.7 %copy-start.2 = (f32[32768]{0:T(1024)S(1)}, f32[32768]{0:T(1024)}, u32[]{:S(2)}) copy-start(f32[32768]{0:T(1024)} %param.14) | copy-start | bytes 393220
  16.7 6.7 %copy-start.3 = (f32[32768]{0:T(1024)S(1)}, f32[32768]{0:T(1024)}, u32[]{:S(2)}) copy-start(f32[32768]{0:T(1024)} %param.15) | copy-start | bytes 393220
  16.7 8.6 %collective-permute-start.3 = (bf16[128,1024]{1,0:T(8,128)(2,1)S(1)}, bf16[128,1024]{1,0:T(8,128)(2,1)S(1)}, u32[]{:S(2)}, u32[]{:S(2)}) collective-permute-start(bf16[128,1024]{1,0:T(8,128)(2,1)S(1)} %shard_map.96.refs_8_), channel_id=1, source_target_pairs={{1,2},{2,1},{3,4},{4,3},{5,6},{6,5},{7,8},{8,7},{9,10},{10,9},{11,... | collective-permute-start | bytes 786440 | tf_op jit(solution)/shard_map/ppermute | solution.py:804
  21.8 8.6 %collective-permute-start.8 = (bf16[6,128,128]{2,1,0:T(8,128)(2,1)S(1)}, bf16[6,128,128]{2,1,0:T(8,128)(2,1)S(1)}, u32[]{:S(2)}, u32[]{:S(2)}) collective-permute-start(bf16[6,128,128]{2,1,0:T(8,128)(2,1)S(1)} %get-tuple-element.53.refs_1_.refs_2_), channel_id=1, source_target_pairs={{16,0},{0,16},{17,1},{1,17},{18,2},{2,18},{19,3},{3,19},{20,4},{4,... | collective-permute-start | bytes 589832 | tf_op jit(solution)/shard_map/ppermute | solution.py:767
  23.3 2.0 %collective-permute-start.4 = (bf16[128,1024]{1,0:T(8,128)(2,1)S(1)}, bf16[128,1024]{1,0:T(8,128)(2,1)S(1)}, u32[]{:S(2)}, u32[]{:S(2)}) collective-permute-start(bf16[128,1024]{1,0:T(8,128)(2,1)S(1)} %shard_map.98), channel_id=1, source_target_pairs={{0,1},{1,0},{2,3},{3,2},{4,5},{5,4},{6,7},{7,6},{8,9},{9,8},{10,11... | collective-permute-start | bytes 786440 | tf_op jit(solution)/shard_map/ppermute | solution.py:805
  26.3 9.8 %collective-permute-start.7 = (bf16[128,1024]{1,0:T(8,128)(2,1)S(1)}, bf16[128,1024]{1,0:T(8,128)(2,1)S(1)}, u32[]{:S(2)}, u32[]{:S(2)}) collective-permute-start(bf16[128,1024]{1,0:T(8,128)(2,1)S(1)} %shard_map.99.refs_0_), channel_id=1, source_target_pairs={{16,0},{0,16},{17,1},{1,17},{18,2},{2,18},{19,3},{3,19},{20,4},{4,... | collective-permute-start | bytes 786440 | tf_op jit(solution)/shard_map/ppermute | solution.py:767
  27.3 15.0 %collective-permute-start.9 = (bf16[8,128,128]{2,1,0:T(8,128)(2,1)S(1)}, bf16[8,128,128]{2,1,0:T(8,128)(2,1)S(1)}, u32[]{:S(2)}, u32[]{:S(2)}) collective-permute-start(bf16[8,128,128]{2,1,0:T(8,128)(2,1)S(1)} %get-tuple-element.54.refs_2_.refs_0_), channel_id=1, source_target_pairs={{16,0},{0,16},{17,1},{1,17},{18,2},{2,18},{19,3},{3,19},{20,4},{4,... | collective-permute-start | bytes 786440 | tf_op jit(solution)/shard_map/ppermute | solution.py:767
  28.4 15.6 %collective-permute-start.6 = (bf16[4,128,128]{2,1,0:T(8,128)(2,1)S(1)}, bf16[4,128,128]{2,1,0:T(8,128)(2,1)S(1)}, u32[]{:S(2)}, u32[]{:S(2)}) collective-permute-start(bf16[4,128,128]{2,1,0:T(8,128)(2,1)S(1)} %get-tuple-element.49.refs_3_.refs_0_), channel_id=1, source_target_pairs={{16,0},{0,16},{17,1},{1,17},{18,2},{2,18},{19,3},{3,19},{20,4},{4,... | collective-permute-start | bytes 393224 | tf_op jit(solution)/shard_map/ppermute | solution.py:767

commit v6 on v5

--- a/solution.py
+++ b/solution.py
@@ -44,8 +44,10 @@
 
 
 def message_rows(field_rows):
-    names = ("coef_high", "coef_low", "offset", "list_high", "list_low")
-    return {name: field_rows + 16 * place for place, name in enumerate(names)}
+    return {name: field_rows + 16 * place for place, name in enumerate(("coef", "offset", "list"))}
+
+
+MESSAGE_EXTRA = 48
 
 
 def pack_kernel(
@@ -100,27 +102,23 @@
     small_ref[...] = jnp.zeros_like(small_ref)
     small_ref[0:6, :] = coef_ref[...]
     small_ref[8:14, :] = offset
-    coef_high, coef_low = split2(coef_ref[...])
-    for name, value in (
-        ("coef_high", coef_high.astype(F32)),
-        ("coef_low", coef_low.astype(F32)),
-        ("offset", offset),
-    ):
-        first = padded(value[:, :LANES], 10)
-        last = padded(value[:, columns - LANES :], 10)
+    pieces = [padded(value.astype(F32), 2) for value in split2(coef_ref[...])]
+    reach = padded(offset, 10)
+    for name, value in (("coef", jnp.concatenate(pieces, axis=0)), ("offset", reach)):
+        first = value[:, :LANES]
+        last = value[:, columns - LANES :]
         start = rows[name]
         a_ref[start : start + 16, :] = jnp.where(odd, last, first).astype(BF16)
         b_ref[start : start + 16, :] = jnp.where(odd, first, last).astype(BF16)
     blocks = index_ref.shape[0]
-    index = padded(index_ref[:, 0, :].astype(F32), 16 - blocks)
-    high = jnp.floor(index * (1.0 / 64.0))
-    for k, value in enumerate((high, index - 64.0 * high)):
-        value = value.astype(BF16)
-        start = rows["list_high"] + 16 * k
-        a_ref[start : start + 16, :] = value
-        b_ref[start : start + 16, :] = value
-        lists_ref[16 * k : 16 * k + 16, :] = value
-    lists_ref[32:48, :] = padded(weight_ref[:, 0, :].astype(F32), 16 - blocks).astype(BF16)
+    index = index_ref[:, 0, :]
+    quotient = padded(((index // LANES) * 4 + weight_ref[:, 0, :]).astype(F32), 8 - blocks)
+    entries = padded((index % LANES).astype(F32), 8 - blocks)
+    entries = jnp.concatenate([quotient, entries], axis=0).astype(BF16)
+    start = rows["list"]
+    a_ref[start : start + 16, :] = entries
+    b_ref[start : start + 16, :] = entries
+    lists_ref[...] = entries
 
     for copy in copies[4:]:
         copy.wait()
@@ -152,55 +150,51 @@
 
 
 def padded(value, count):
+    if not count:
+        return value
     return jnp.concatenate([value, jnp.zeros((count, value.shape[1]), value.dtype)], axis=0)
 
 
-def operator_kernel(
-    small_ref, both_ref, part_ref, second_ref, first_high, first_low, second_high, second_low
-):
+def operator_kernel(small_ref, both_ref, part_ref, second_ref):
     columns = small_ref.shape[1]
     groups = columns // LANES
     coef = padded(small_ref[0:6, :], 2)
     reach = padded(small_ref[8:14, :], 2)
-    moved_coef = pltpu.roll(coef, HALO, axis=1)
-    moved_reach = pltpu.roll(reach, HALO, axis=1)
-
-    def lanes(value, group):
-        return value[:, group * LANES : (group + 1) * LANES]
-
-    firsts = {
-        g: split2(band(lanes(moved_coef, g), lanes(moved_reach, g))) for g in range(1, groups)
-    }
-    seconds = [split2(band(lanes(coef, g), lanes(reach, g))) for g in range(groups)]
-    for ref in (first_high, first_low, second_high, second_low):
-        ref[...] = jnp.zeros_like(ref)
-    for g in range(1, groups):
+    moved = pltpu.roll(coef, HALO, axis=1), pltpu.roll(reach, HALO, axis=1)
+
+    def operator(values, group):
+        lanes = slice(group * LANES, (group + 1) * LANES)
+        return split2(band(*(value[:, lanes] for value in values)))
+
+    firsts = {g: operator(moved, g) for g in range(1, groups)}
+    seconds = [[padded(v, 64) for v in operator((coef, reach), g)] for g in range(groups)]
+
+    def upper(g):
+        return padded(dot3(firsts[g], [value[:LANES, :] for value in seconds[g]]), 64)
+
+    def lower(g):
+        result = dot3(
+            [value[:LANES, :] for value in firsts[g + 1]],
+            [value[LANES:, :] for value in seconds[g]],
+        )
+        return jnp.concatenate([jnp.zeros_like(result), result], axis=0)
+
+    both_ref[...] = jnp.zeros_like(both_ref)
+    half = both_ref.shape[1] // 2
+    for g in range(1, groups - 1):
         row, lane = g * LANES - 64, (g - 1) * LANES
-        count = min(LANES + 2 * HALO, columns - row)
-        first_high[row : row + count, lane : lane + LANES] = firsts[g][0][:count, :]
-        first_low[row : row + count, lane : lane + LANES] = firsts[g][1][:count, :]
-    for g in range(1, groups - 1):
-        row, lane = (g - 1) * LANES, (g - 1) * LANES
-        second_high[row : row + LANES + 2 * HALO, lane : lane + LANES] = seconds[g][0]
-        second_low[row : row + LANES + 2 * HALO, lane : lane + LANES] = seconds[g][1]
-    both_ref[...] = joined(
-        split2(dot3((first_high[...], first_low[...]), (second_high[...], second_low[...])))
-    )
-
+        for k, value in enumerate(split2(upper(g) + lower(g))):
+            both_ref[row : row + 2 * LANES, k * half + lane : k * half + lane + LANES] = value
+    part_ref[0] = lower(0)
+    part_ref[1] = upper(groups - 1)
     for k, g in enumerate((0, groups - 1)):
-        second = [padded(value, 64) for value in seconds[g]]
         for j in range(2):
-            second_ref[2 * k + j] = second[j]
-        if k == 0:
-            part = dot3([value[:128, :] for value in firsts[1]], [value[128:, :] for value in second])
-            part_ref[k] = jnp.concatenate([jnp.zeros_like(part), part], axis=0)
-        else:
-            part_ref[k] = padded(dot3(firsts[g], [value[:128, :] for value in second]), 64)
+            second_ref[2 * k + j] = seconds[g][j]
 
 
 def middle_kernel(*refs, groups):
     field_refs = refs[:groups]
-    both_ref, middle_ref, kept_ref, edge_ref, fields = refs[groups:]
+    both_ref, middle_ref, kept_ref, edge_ref, edge_low_ref, fields, fields_low = refs[groups:]
     early, members, _ = middle_ref.shape
     levels = field_refs[0].shape[0] // members
     lane = iota((members, LANES), 1)
@@ -208,16 +202,21 @@
         spot = slice(level * members, (level + 1) * members)
         own = [ref[pl.ds(level, members, stride=levels), :] for ref in field_refs]
         for group in range(groups):
-            fields[spot, group * LANES : (group + 1) * LANES] = own[group].astype(BF16)
-        turned = [pltpu.roll(own[g], 64, axis=1) for g in (0, 1, groups - 2, groups - 1)]
-        zero = jnp.zeros_like(turned[0])
-        edge_ref[0, spot, 0:LANES] = jnp.where(lane < 64, zero, turned[0]).astype(BF16)
-        edge_ref[0, spot, LANES:] = jnp.where(lane < 64, turned[0], turned[1]).astype(BF16)
-        edge_ref[1, spot, 0:LANES] = jnp.where(lane < 64, turned[2], turned[3]).astype(BF16)
-        edge_ref[1, spot, LANES:] = jnp.where(lane < 64, turned[3], zero).astype(BF16)
+            lanes = slice(group * LANES, (group + 1) * LANES)
+            fields[spot, lanes], fields_low[spot, lanes] = split2(own[group])
+        pieces = [
+            split2(pltpu.roll(own[g], 64, axis=1)) for g in (0, 1, groups - 2, groups - 1)
+        ]
+        for part, ref in enumerate((edge_ref, edge_low_ref)):
+            turned = [piece[part].astype(F32) for piece in pieces]
+            zero = jnp.zeros_like(turned[0])
+            ref[0, spot, 0:LANES] = jnp.where(lane < 64, zero, turned[0]).astype(BF16)
+            ref[0, spot, LANES:] = jnp.where(lane < 64, turned[0], turned[1]).astype(BF16)
+            ref[1, spot, 0:LANES] = jnp.where(lane < 64, turned[2], turned[3]).astype(BF16)
+            ref[1, spot, LANES:] = jnp.where(lane < 64, turned[3], zero).astype(BF16)
     result = dot(fields[...], both_ref[...])
     half = result.shape[1] // 2
-    result = result[:, :half] + result[:, half:]
+    result = result[:, :half] + (result[:, half:] + dot(fields_low[...], both_ref[:, :half]))
     for k in range((groups - 2) * levels):
         level, lane = k % levels, (k // levels) * LANES
         value = result[level * members : (level + 1) * members, lane : lane + LANES].astype(BF16)
@@ -228,9 +227,10 @@
 
 
 def edge_kernel(
-    a_ref, b_ref, small_ref, edge_ref, part_ref, second_ref, kept_ref, first_ref, next_ref, last_ref, fields
+    a_ref, b_ref, small_ref, edge_ref, edge_low_ref, part_ref, second_ref, kept_ref, first_ref, next_ref, last_ref, fields
 ):
-    levels, members, _ = next_ref.shape
+    _, members, _ = next_ref.shape
+    levels = fields.shape[1] // members
     columns = small_ref.shape[1]
     half = members // 2
     rows = message_rows(levels * half)
@@ -247,7 +247,8 @@
     lane = iota((half, LANES), 1)
     operators = []
     for k in range(2):
-        near = side(k, rows["coef_high"], 16)[:8] + side(k, rows["coef_low"], 16)[:8]
+        near = side(k, rows["coef"], 16)
+        near = near[:8] + near[8:]
         reach = side(k, rows["offset"], 16)[:8]
         if k == 0:
             own = (own_coef[:, :LANES], own_reach[:, :LANES])
@@ -290,37 +291,39 @@
                     fields[k, spot, LANES:] = jnp.where(lane < 64, own, pair[j]).astype(BF16)
                     fields[k, spot, 0:LANES] = edge_ref[k, spot, 0:LANES]
         result = dot(fields[k], joined(operators[k]))
-        result = result[:, :LANES] + result[:, LANES:]
-        part = levels // 2
+        result = result[:, :LANES] + (
+            result[:, LANES:] + dot(edge_low_ref[k], operators[k][0])
+        )
         kept = kept_ref.shape[0]
         if k == 0:
             first_ref[:kept] = kept_ref[...]
+        places = [
+            (ref, place)
+            for ref, start in ((first_ref, kept), (next_ref, 0), (last_ref, 0))
+            for place in range(start, ref.shape[0])
+        ]
         for level in range(levels):
-            value = result[level * members : (level + 1) * members, :].astype(BF16)
-            if k == 0 and level < part:
-                first_ref[kept + level] = value
-            elif k == 0:
-                next_ref[level - part] = value
-            elif level < part:
-                next_ref[part + level] = value
-            else:
-                last_ref[level - part] = value
-
-
-def gather_lists(parts, blocks):
+            ref, place = places[k * levels + level]
+            ref[place] = result[level * members : (level + 1) * members, :].astype(BF16)
+
+
+def in_order(parts):
     count = len(parts)
     me = lax.axis_index("mem")
-    rows = [
-        jnp.concatenate([part[b : b + 1, :].astype(F32) for b in range(blocks)], axis=1)
-        for part in parts
-    ]
     placed = []
     for place in range(count):
-        value = rows[0]
+        value = parts[0]
         for shift in range(1, count):
-            value = jnp.where((me + shift) % count == place, rows[shift], value)
+            value = jnp.where((me + shift) % count == place, parts[shift], value)
         placed.append(value)
-    return jnp.concatenate(placed, axis=1)
+    return joined(placed)
+
+
+def entries_of(part, blocks):
+    part = part.astype(F32)
+    quotient = joined([part[b : b + 1, :] for b in range(blocks)]).astype(jnp.int32)
+    rest = joined([part[8 + b : 9 + b, :] for b in range(blocks)]).astype(jnp.int32)
+    return (quotient // 4) * LANES + rest, quotient % 4
 
 
 def read_places(table_ref, slot):
@@ -345,55 +348,60 @@
     table[32:48, :] = (cell % 16).astype(F32).astype(BF16)
 
 
-def read_forecast(field, level, column, out_ref, lane):
-    members = out_ref.shape[0]
+def read_some(field, levels, level, column):
+    members = field.shape[0] // levels
     wide = level.shape[1]
     one = jnp.where(iota((field.shape[1], wide), 0) == column, 1.0, 0.0).astype(BF16)
     found = dot(field, one)
     total = jnp.zeros((members, wide), F32)
-    for l in range(field.shape[0] // members):
+    for l in range(levels):
         total = total + jnp.where(level == l, found[l * members : (l + 1) * members, :], 0.0)
-    out_ref[:, lane : lane + wide] = total.astype(BF16)
-
-
-def whole(middle_ref, first_ref, next_ref, last_ref):
-    part, members, _ = last_ref.shape
-    kept = first_ref.shape[0] - part
-    middle = jnp.concatenate([middle_ref[...], first_ref[:kept]], axis=0)
-    groups = [
-        jnp.concatenate([first_ref[kept:], next_ref[:part]], axis=0),
-        *(middle[k : k + 2 * part] for k in range(0, middle.shape[0], 2 * part)),
-        jnp.concatenate([next_ref[part:], last_ref[...]], axis=0),
-    ]
-    return joined([group.reshape(-1, LANES) for group in groups])
-
-
-def neighbour_kernel(*refs, others, blocks, turn):
-    message_ref = refs[4]
-    other_refs = refs[5 : 5 + others]
-    cell_ref, level_ref = refs[5 + others : 7 + others]
+    return total
+
+
+def read_forecast(field, levels, level, column):
+    step = min(256, level.shape[1])
+    return joined(
+        [
+            read_some(field, levels, level[:, k : k + step], column[:, k : k + step])
+            for k in range(0, level.shape[1], step)
+        ]
+    )
+
+
+def whole(middle_ref, first_ref, next_ref, last_ref, levels):
+    runs = jnp.concatenate([ref[...] for ref in (middle_ref, first_ref, next_ref, last_ref)], axis=0)
+    groups = [runs[k : k + levels].reshape(-1, LANES) for k in range(0, runs.shape[0], levels)]
+    return joined([groups[-2], *groups[:-2], groups[-1]])
+
+
+def neighbour_kernel(*refs, others, blocks, levels, turn, given):
+    message_ref, cell_ref, level_ref = refs[4:7]
+    passed_refs = refs[7 : 7 + others]
     out_ref, table = refs[-2:]
-    half = message_ref.shape[0] - 80
+    half = message_ref.shape[0] - MESSAGE_EXTRA
     rows = message_rows(half)
     odd = is_odd_tile()
     obs = 16 * LANES
     make_table(cell_ref, level_ref, table)
-    field = whole(*refs[:4])
-    base = 32 * turn
-    parts = [message_ref[rows["list_high"] : rows["list_high"] + 32, :]]
-    parts += [r[base : base + 32, :] for r in other_refs]
-    high = gather_lists([part[:16, :] for part in parts], blocks)
-    low = gather_lists([part[16:, :] for part in parts], blocks)
-    index = (high * 64.0 + low).astype(jnp.int32)
+    field = whole(*refs[:4], levels)
     skip = jnp.where(odd, 0, 2 * obs) if turn == 0 else jnp.where(odd, 2 * obs, 0)
+    parts = [ref[16 * turn : 16 * turn + 16, :] for ref in passed_refs]
+    if not given:
+        parts = [message_ref[rows["list"] : rows["list"] + 16, :], *parts]
+    index = joined([entries_of(part, blocks)[0] for part in parts])
     level, column = read_places(table, index - skip)
-    for lane in range(0, index.shape[1], 256):
-        read_forecast(
-            field, level[:, lane : lane + 256], column[:, lane : lane + 256], out_ref, lane
-        )
-
-
-def own_kernel(*refs, others, blocks, tiles):
+    found = read_forecast(field, levels, level, column)
+    if others:
+        mine = blocks * LANES
+        found = [found[:, k : k + mine] for k in range(0, found.shape[1], mine)]
+        if given:
+            found = [refs[7 + others][...].astype(F32), *found]
+        found = in_order(found)
+    out_ref[...] = found.astype(BF16)
+
+
+def own_kernel(*refs, others, blocks, levels, tiles):
     lists_ref = refs[4]
     other_refs = refs[5 : 5 + others]
     (
@@ -408,16 +416,14 @@
     ) = refs[5 + others :]
     obs = 16 * LANES
     make_table(cell_ref, level_ref, table)
-    field = whole(*refs[:4])
-
-    parts = [lists_ref[...]] + [r[64:112, :] for r in other_refs]
-    passed = [gather_lists([part[16 * k : 16 * k + 16, :] for part in parts], blocks) for k in range(3)]
-    index = (passed[0] * 64.0 + passed[1]).astype(jnp.int32)
-    weight = passed[2]
+    field = whole(*refs[:4], levels)
+    parts = [lists_ref[...]] + [r[32:48, :] for r in other_refs]
+    parts = [entries_of(part, blocks) for part in parts]
+    index = in_order([index for index, _ in parts])
+    weight = in_order([weight for _, weight in parts]).astype(F32)
     wide = index.shape[1]
     level, column = read_places(table, index - obs)
-    for lane in range(0, wide, 256):
-        read_forecast(field, level[:, lane : lane + 256], column[:, lane : lane + 256], r_ref, lane)
+    r_ref[...] = read_forecast(field, levels, level, column).astype(BF16)
 
     tile = lax.axis_index("tile")
     starts = [((tile + tiles + shift) % tiles) * 16 for shift in (-1, 0, 1)]
@@ -605,8 +611,9 @@
     moved_ref, mean_ref, weight_ref, out_hbm, rest_ref, stage, done, sems = refs[others + 1 :]
     members, levels, columns = out_hbm.shape
     width = columns // weight_ref.shape[0]
-    part = levels // 2
     groups = columns // LANES
+    soon = 2 * moved_ref.shape[0] - (groups - 2) * levels
+    part = afters[0].shape[0] - (levels - soon)
 
     def rows(level):
         return pl.ds(level, members, stride=levels)
@@ -616,11 +623,11 @@
     for group in (*range(1, groups - 1), 0):
         left = weights_of(weight_ref, group, columns)
         for level in range(0, levels, 2):
-            if group or level < part:
+            if group or level < soon:
                 moved, mean = moved_ref[slot], mean_ref[slot, 0:1, :]
                 slot += 1
             else:
-                moved, mean = departures([[ref[level - part + j] for ref in afters] for j in range(2)])
+                moved, mean = departures([[ref[level - soon + j] for ref in afters] for j in range(2)])
             for j, value in enumerate(updated(left, moved, mean, width)):
                 stage[group, rows(level + j), :] = value
         done[group] = stage[group].reshape(members, levels, LANES).astype(BF16)
@@ -629,7 +636,9 @@
         copies[-1].start()
     left = weights_of(weight_ref, groups - 1, columns)
     for level in range(0, part, 2):
-        moved, mean = departures([[ref[part + level + j] for ref in afters] for j in range(2)])
+        moved, mean = departures(
+            [[ref[levels - soon + level + j] for ref in afters] for j in range(2)]
+        )
         for j, value in enumerate(updated(left, moved, mean, width)):
             rest_ref[rows(level + j), :] = value
     for level in range(part, levels):
@@ -643,10 +652,11 @@
     weight_ref, rest_ref, _, out_hbm, stage, done, sem = refs[others + 1 :]
     members, levels, columns = out_hbm.shape
     width = columns // weight_ref.shape[0]
-    part = levels // 2
+    count = lasts[0].shape[0]
+    part = levels - count
     left = weights_of(weight_ref, columns // LANES - 1, columns)
     stage[...] = rest_ref[...]
-    for level in range(0, part, 2):
+    for level in range(0, count, 2):
         moved, mean = departures([[ref[level + j] for ref in lasts] for j in range(2)])
         for j, value in enumerate(updated(left, moved, mean, width)):
             stage[pl.ds(part + level + j, members, stride=levels), :] = value
@@ -696,7 +706,7 @@
     blocks = obs_index.shape[0]
     entries = blocks * sharers * LANES
     half = members * levels // 2
-    message = jax.ShapeDtypeStruct((half + 80, LANES), BF16)
+    message = jax.ShapeDtypeStruct((half + MESSAGE_EXTRA, LANES), BF16)
     even_pairs = []
     odd_pairs = []
     for i in range(0, tiles, 2):
@@ -713,7 +723,7 @@
         [
             message,
             message,
-            jax.ShapeDtypeStruct((48, LANES), BF16),
+            jax.ShapeDtypeStruct((16, LANES), BF16),
             jax.ShapeDtypeStruct((16, columns), F32),
         ],
         [flat, coefficients, neighbours, obs_index, obs_weight],
@@ -732,7 +742,9 @@
     from_b = lax.ppermute(b, "tile", even_pairs)
     from_a = lax.ppermute(a, "tile", odd_pairs)
     flat_rows = members * levels
-    kept_levels = levels // 4
+    kept_levels = levels // 2
+    soon_levels = levels // 4
+    last_levels = levels // 2
     both, part, second = call(
         operator_kernel,
         [
@@ -741,27 +753,22 @@
             jax.ShapeDtypeStruct((4, 2 * LANES, LANES), BF16),
         ],
         [small],
-        [
-            pltpu.VMEM((columns, columns - LANES), BF16),
-            pltpu.VMEM((columns, columns - LANES), BF16),
-            pltpu.VMEM((columns - LANES, columns - 2 * LANES), BF16),
-            pltpu.VMEM((columns - LANES, columns - 2 * LANES), BF16),
-        ],
-        cost=2,
-    )
-    middle, kept, border = call(
+        cost=1,
+    )
+    middle, kept, border, border_low = call(
         functools.partial(middle_kernel, groups=groups),
         [
             jax.ShapeDtypeStruct(((groups - 2) * levels - kept_levels, members, LANES), BF16),
             jax.ShapeDtypeStruct((kept_levels, members, LANES), BF16),
             jax.ShapeDtypeStruct((2, flat_rows, 2 * LANES), BF16),
+            jax.ShapeDtypeStruct((2, flat_rows, 2 * LANES), BF16),
         ],
         [flat] * groups + [both],
-        [pltpu.VMEM((flat_rows, columns), BF16)],
+        [pltpu.VMEM((flat_rows, columns), BF16)] * 2,
         in_specs=[group_spec(flat_rows, group) for group in range(groups)] + [vmem()],
         cost=3,
     )
-    passed = jnp.concatenate([from_a[half + 48 :], from_b[half + 48 :], lists], axis=0)
+    passed = jnp.concatenate([from_a[half + 32 :], from_b[half + 32 :], lists], axis=0)
 
     def swapped(value, sent):
         return [value] + [lax.ppermute(sent, "mem", turn) for turn in turns]
@@ -772,11 +779,16 @@
     first, after, last = call(
         edge_kernel,
         [
-            jax.ShapeDtypeStruct((kept_levels + levels // 2, members, LANES), BF16),
-            jax.ShapeDtypeStruct((levels, members, LANES), BF16),
-            jax.ShapeDtypeStruct((levels // 2, members, LANES), BF16),
+            *(
+                jax.ShapeDtypeStruct((count, members, LANES), BF16)
+                for count in (
+                    kept_levels + soon_levels,
+                    2 * levels - soon_levels - last_levels,
+                    last_levels,
+                )
+            ),
         ],
-        [from_a, from_b, small, border, part, second, kept],
+        [from_a, from_b, small, border, border_low, part, second, kept],
         [pltpu.VMEM((2, flat_rows, 2 * LANES), BF16)],
         cost=2,
     )
@@ -785,27 +797,38 @@
     level = obs_level.reshape(16, LANES)
     reading = jax.ShapeDtypeStruct((members, entries), BF16)
     table = pltpu.VMEM((48, LANES), BF16)
-    to_neighbour = []
-    for turn, received in enumerate((from_a, from_b)):
-        inputs = [*pieces, received, *passed, cell, level]
-        to_neighbour += call(
+    def read_for(turn, received, passed, shape, held=(), unused=(), cost=2):
+        inputs = [*pieces, received, cell, level, *passed, *held]
+        (result,) = call(
             functools.partial(
-                neighbour_kernel, others=others, blocks=blocks, turn=turn
+                neighbour_kernel,
+                others=len(passed),
+                blocks=blocks,
+                levels=levels,
+                turn=turn,
+                given=len(held),
             ),
-            [reading],
-            [*inputs, *to_neighbour],
+            [shape],
+            [*inputs, *unused],
             [table],
-            in_specs=[vmem()] * len(inputs) + [pl.BlockSpec(memory_space=pl.ANY)] * turn,
-            cost=2,
+            in_specs=[vmem()] * len(inputs) + [pl.BlockSpec(memory_space=pl.ANY)] * len(unused),
+            cost=cost,
         )
-    to_a, to_b = to_neighbour
+        return result
+
+    mine = jax.ShapeDtypeStruct((members, blocks * LANES), BF16)
+    mine = read_for(0, from_a, [], mine, cost=1)
+    to_a = read_for(0, from_a, passed, reading, held=[mine], cost=1)
+    to_b = read_for(1, from_b, passed, reading, unused=[to_a])
     to_b, sent = lax.optimization_barrier((to_b, first))
     firsts = swapped(first, sent)
     back_a = lax.ppermute(to_a, "tile", odd_pairs)
     back_b = lax.ppermute(to_b, "tile", even_pairs)
     vector = jax.ShapeDtypeStruct((8, entries), F32)
     own, weight, target = call(
-        functools.partial(own_kernel, others=others, blocks=blocks, tiles=tiles),
+        functools.partial(
+            own_kernel, others=others, blocks=blocks, levels=levels, tiles=tiles
+        ),
         [reading, vector, vector],
         [
             *pieces,

time: 45.4 us -> 45.1 us (level)
  waiting for transfers between devices: 8.32 us -> 6.94 us
  Pallas kernels: 19.5 us -> 20.5 us
    pallas_call x13 -> x14, Pallas kernels: 19.5 us -> 20.5 us  [call(): pl.pallas_call(kernel, grid=(1,), out_shape=outs, in_specs=in_specs or [v...]
    ppermute x1, waiting for transfers between devices: 0.99 us -> 0.01 us  [shards(): passed = [lax.ppermute(passed, 'mem', turn) for turn in turns]]
    ppermute x5, starting transfers between devices: 5.05 us -> 5.67 us  [swapped(): return [value] + [lax.ppermute(sent, 'mem', turn) for turn in turns]]
    ppermute x5, waiting for transfers between devices: 7.18 us -> 6.59 us  [swapped(): return [value] + [lax.ppermute(sent, 'mem', turn) for turn in turns]]
  transfers between devices with their start and end apart: 10 -> 10, of which waited for: 5 -> 4; matrix products, arithmetic and copies ran while one was open for 0% -> 0% of each run, Pallas kernels for 36% -> 39%
where the time goes in v6:
time: 45.1 us; the launch traced here: 44.9 us
  Pallas kernels  20.5 us (45%)
  starting transfers between devices  16.2 us (36%)
  waiting for transfers between devices  6.94 us (15%)
  local copies, waits for them, and re-layouts  0.79 us (2%)
    pallas_call x14, Pallas kernels, call(): pl.pallas_call(kernel, grid=(1,), out_shape=outs, in_specs=in_specs or [v...  20.5 us
    ppermute x5, waiting for transfers between devices, swapped(): return [value] + [lax.ppermute(sent, 'mem', turn) for turn in turns]  6.59 us
    ppermute x5, starting transfers between devices, swapped(): return [value] + [lax.ppermute(sent, 'mem', turn) for turn in turns]  5.67 us
    ppermute x1, starting transfers between devices, shards(): from_a = lax.ppermute(a, 'tile', odd_pairs)  5.51 us
    ppermute x1, starting transfers between devices, shards(): back_a = lax.ppermute(to_a, 'tile', odd_pairs)  3.49 us
    ppermute x1, starting transfers between devices, shards(): passed = [lax.ppermute(passed, 'mem', turn) for turn in turns]  1.56 us
  transfers between devices with their start and end apart: 10, of which 4 were waited for; matrix products, arithmetic and copies ran while one was open for 0% of the time, Pallas kernels for 39%

profile of v6, /device:TPU:0, one launch (start us, length us, event | category | flops | bytes accessed | tf_op | source)
XLA Modules:
  0.0 44.9 jit_solution(13384282100409504802)
XLA Ops:
  0.0 2.2 %shard_map.91 = (bf16[560,128]{1,0:T(8,128)(2,1)}, bf16[560,128]{1,0:T(8,128)(2,1)}, bf16[16,128]{1,0:T(8,128)(2,1)}, f32[16,512]{1,0:T(8,128)}) custom-call(f32[1024,512]{1,0:T(8,128)} %bitcast.5, f32[6,512]{1,0:T(8,128)} %coef_hbm.1, s32[6,512]{1,0:T(8,128)} %nbr_hbm.1, s32[4,1,128]{2,1,0:T(1,128)} %index_hbm.1, s32[4,1,128]{2,1,0:T(1,128)} %weight_hbm.1), custom_call_target="tpu_custom_call" | custom-call | bytes 1024 | tf_op jit(solution)/shard_map/pallas_call | solution.py:678
  2.2 0.0 copy-start
  2.2 5.5 %collective-permute-start = (bf16[560,128]{1,0:T(8,128)(2,1)}, bf16[560,128]{1,0:T(8,128)(2,1)S(1)}, u32[]{:S(2)}, u32[]{:S(2)}) collective-permute-start(bf16[560,128]{1,0:T(8,128)(2,1)} %get-tuple-element.33), channel_id=1, source_target_pairs={{1,2},{2,1},{3,4},{4,3},{5,6},{6,5},{7,8},{8,7},{9,10},{10,9},{11,... | collective-permute-start | bytes 430088 | tf_op jit(solution)/shard_map/ppermute | solution.py:743
  7.7 0.0 collective-permute-start.1
  7.7 0.0 copy-start.4
  7.7 0.8 %copy-done.4 = f32[16,512]{1,0:T(8,128)S(1)} copy-done((f32[16,512]{1,0:T(8,128)S(1)}, f32[16,512]{1,0:T(8,128)}, u32[]{:S(2)}) %copy-start.4) | copy-done | bytes 32792
  8.5 0.9 %shard_map.92 = (bf16[512,512]{1,0:T(8,128)(2,1)S(1)}, f32[2,256,128]{2,1,0:T(8,128)S(1)}, bf16[4,256,128]{2,1,0:T(8,128)(2,1)S(1)}) custom-call(f32[16,512]{1,0:T(8,128)S(1)} %copy-done.4), custom_call_target="tpu_custom_call" | custom-call | flops 1073741824 | bytes 1024 | tf_op jit(solution)/shard_map/pallas_call | solution.py:678
  9.4 0.0 copy-done
  9.4 0.0 copy-start.1
  9.4 1.8 %shard_map.93 = (bf16[12,128,128]{2,1,0:T(8,128)(2,1)S(1)}, bf16[4,128,128]{2,1,0:T(8,128)(2,1)S(1)}, bf16[2,1024,256]{2,1,0:T(8,128)(2,1)S(1)}, bf16[2,1024,256]{2,1,0:T(8,128)(2,1)S(1)}) custom-call(f32[1024,512]{1,0:T(8,128)S(1)} %bitcast.6, f32[1024,512]{1,0:T(8,128)S(1)} %bitcast.7, f32[1024,512]{1,0:T(8,128)S(1)} %bitcast.8, f32[1024,512]{1,0:T(8,128)S(1)} %bitcast.9, ...), custom_call_target="tpu_custom_call" | custom-call | flops 3221225472 | bytes 1024 | tf_op jit(solution)/shard_map/pallas_call | solution.py:678
  11.1 0.0 collective-permute-done.a_ref.refs_4_
  11.2 0.0 collective-permute-done.1.b_ref.refs_4_
  11.2 0.0 copy-done.1
  11.2 1.6 %collective-permute-start.2 = (bf16[48,128]{1,0:T(8,128)(2,1)S(1)}, bf16[48,128]{1,0:T(8,128)(2,1)S(1)}, u32[]{:S(2)}, u32[]{:S(2)}) collective-permute-start(bf16[48,128]{1,0:T(8,128)(2,1)S(1)} %pad_maximum_fusion), channel_id=1, source_target_pairs={{16,0},{0,16},{17,1},{1,17},{18,2},{2,18},{19,3},{3,19},{20,4},{4,... | collective-permute-start | bytes 36872 | tf_op jit(solution)/shard_map/ppermute | solution.py:778
  12.8 0.5 %collective-permute-start.5 = (bf16[12,128,128]{2,1,0:T(8,128)(2,1)S(1)}, bf16[12,128,128]{2,1,0:T(8,128)(2,1)S(1)}, u32[]{:S(2)}, u32[]{:S(2)}) collective-permute-start(bf16[12,128,128]{2,1,0:T(8,128)(2,1)S(1)} %get-tuple-element.50.refs_0_), channel_id=1, source_target_pairs={{16,0},{0,16},{17,1},{1,17},{18,2},{2,18},{19,3},{3,19},{20,4},{4,... | collective-permute-start | bytes 1179656 | tf_op jit(solution)/shard_map/ppermute | solution.py:774
  13.3 0.0 copy-start.5
  13.3 0.0 copy-start.6
  13.3 1.1 %shard_map.94 = (bf16[6,128,128]{2,1,0:T(8,128)(2,1)S(1)}, bf16[10,128,128]{2,1,0:T(8,128)(2,1)S(1)}, bf16[4,128,128]{2,1,0:T(8,128)(2,1)S(1)}) custom-call(bf16[560,128]{1,0:T(8,128)(2,1)S(1)} %collective-permute-done.a_ref.refs_4_, bf16[560,128]{1,0:T(8,128)(2,1)S(1)} %collective-permute-done.1.b_ref.refs_4_, f32[16,512]{1,0:T(8,128)S(1)} %copy-done.4, ...), custom_call_target="tpu_custom_call" | custom-call | flops 2147483648 | bytes 1024 | tf_op jit(solution)/shard_map/pallas_call | solution.py:678
  14.3 0.0 copy-done.5
  14.4 0.0 copy-done.6
  14.4 0.9 %shard_map.96.refs_8_ = bf16[128,512]{1,0:T(8,128)(2,1)S(1)} custom-call(bf16[12,128,128]{2,1,0:T(8,128)(2,1)S(1)} %get-tuple-element.50.refs_0_, bf16[6,128,128]{2,1,0:T(8,128)(2,1)S(1)} %get-tuple-element.55.refs_1_.refs_2_, bf16[10,128,128]{2,1,0:T(8,128)(2,1)S(1)} %get-tuple-element.56.refs_2_.refs_0_, ...), custom_call_target="tpu_custom_call" | custom-call | flops 1073741824 | bytes 1024 | tf_op jit(solution)/shard_map/pallas_call | solution.py:678
  15.3 0.0 collective-permute-done.2.refs_5_.refs_7_
  15.3 1.0 %shard_map.97.refs_8_ = bf16[128,1024]{1,0:T(8,128)(2,1)S(1)} custom-call(bf16[12,128,128]{2,1,0:T(8,128)(2,1)S(1)} %get-tuple-element.50.refs_0_, bf16[6,128,128]{2,1,0:T(8,128)(2,1)S(1)} %get-tuple-element.55.refs_1_.refs_2_, bf16[10,128,128]{2,1,0:T(8,128)(2,1)S(1)} %get-tuple-element.56.refs_2_.refs_0_, ...), custom_call_target="tpu_custom_call" | custom-call | flops 1073741824 | bytes 1024 | tf_op jit(solution)/shard_map/pallas_call | solution.py:678
  16.3 0.0 copy-start.2
  16.3 0.0 copy-start.3
  16.3 3.5 %collective-permute-start.3 = (bf16[128,1024]{1,0:T(8,128)(2,1)S(1)}, bf16[128,1024]{1,0:T(8,128)(2,1)S(1)}, u32[]{:S(2)}, u32[]{:S(2)}) collective-permute-start(bf16[128,1024]{1,0:T(8,128)(2,1)S(1)} %shard_map.97.refs_8_), channel_id=1, source_target_pairs={{1,2},{2,1},{3,4},{4,3},{5,6},{6,5},{7,8},{8,7},{9,10},{10,9},{11,... | collective-permute-start | bytes 786440 | tf_op jit(solution)/shard_map/ppermute | solution.py:825
  19.8 1.5 %shard_map.99 = bf16[128,1024]{1,0:T(8,128)(2,1)S(1)} custom-call(bf16[12,128,128]{2,1,0:T(8,128)(2,1)S(1)} %get-tuple-element.50.refs_0_, bf16[6,128,128]{2,1,0:T(8,128)(2,1)S(1)} %get-tuple-element.55.refs_1_.refs_2_, bf16[10,128,128]{2,1,0:T(8,128)(2,1)S(1)} %get-tuple-element.56.refs_2_.refs_0_, ...), custom_call_target="tpu_custom_call" | custom-call | flops 2147483648 | bytes 1024 | tf_op jit(solution)/shard_map/pallas_call | solution.py:678
  21.4 1.6 %collective-permute-start.8 = (bf16[6,128,128]{2,1,0:T(8,128)(2,1)S(1)}, bf16[6,128,128]{2,1,0:T(8,128)(2,1)S(1)}, u32[]{:S(2)}, u32[]{:S(2)}) collective-permute-start(bf16[6,128,128]{2,1,0:T(8,128)(2,1)S(1)} %get-tuple-element.55.refs_1_.refs_2_), channel_id=1, source_target_pairs={{16,0},{0,16},{17,1},{1,17},{18,2},{2,18},{19,3},{3,19},{20,4},{4,... | collective-permute-start | bytes 589832 | tf_op jit(solution)/shard_map/ppermute | solution.py:774
  22.9 0.0 collective-permute-start.4
  22.9 0.0 copy-done.2
  22.9 0.0 copy-done.3
  22.9 1.7 %shard_map.95 = (bf16[128,1024]{1,0:T(8,128)(2,1)S(1)}, f32[8,1024]{1,0:T(8,128)S(1)}, f32[8,1024]{1,0:T(8,128)S(1)}) custom-call(bf16[12,128,128]{2,1,0:T(8,128)(2,1)S(1)} %get-tuple-element.50.refs_0_, bf16[6,128,128]{2,1,0:T(8,128)(2,1)S(1)} %get-tuple-element.55.refs_1_.refs_2_, bf16[10,128,128]{2,1,0:T(8,128)(2,1)S(1)} %get-tuple-element.56.refs_2_.refs_0_, ...), custom_call_target="tpu_custom_call" | custom-call | flops 2147483648 | bytes 1024 | tf_op jit(solution)/shard_map/pallas_call | solution.py:678
  24.7 0.3 collective-permute-done.3.other_ref
  25.0 0.1 shard_map.98.one_ref
  25.1 0.0 collective-permute-done.4.other_ref
  25.1 0.0 collective-permute-done.5.refs_0_.refs_1_
  25.1 0.1 shard_map.100.refs_0_
  25.1 1.6 %collective-permute-start.7 = (bf16[128,1024]{1,0:T(8,128)(2,1)S(1)}, bf16[128,1024]{1,0:T(8,128)(2,1)S(1)}, u32[]{:S(2)}, u32[]{:S(2)}) collective-permute-start(bf16[128,1024]{1,0:T(8,128)(2,1)S(1)} %shard_map.100.refs_0_), channel_id=1, source_target_pairs={{16,0},{0,16},{17,1},{1,17},{18,2},{2,18},{19,3},{3,19},{20,4},{4,... | collective-permute-start | bytes 786440 | tf_op jit(solution)/shard_map/ppermute | solution.py:774
  26.7 0.5 %collective-permute-start.9 = (bf16[10,128,128]{2,1,0:T(8,128)(2,1)S(1)}, bf16[10,128,128]{2,1,0:T(8,128)(2,1)S(1)}, u32[]{:S(2)}, u32[]{:S(2)}) collective-permute-start(bf16[10,128,128]{2,1,0:T(8,128)(2,1)S(1)} %get-tuple-element.56.refs_2_.refs_0_), channel_id=1, source_target_pairs={{16,0},{0,16},{17,1},{1,17},{18,2},{2,18},{19,3},{3,19},{20,4},{4,... | collective-permute-start | bytes 983048 | tf_op jit(solution)/shard_map/ppermute | solution.py:774
  27.2 1.5 %collective-permute-start.6 = (bf16[4,128,128]{2,1,0:T(8,128)(2,1)S(1)}, bf16[4,128,128]{2,1,0:T(8,128)(2,1)S(1)}, u32[]{:S(2)}, u32[]{:S(2)}) collective-permute-start(bf16[4,128,128]{2,1,0:T(8,128)(2,1)S(1)} %get-tuple-element.51.refs_3_.refs_0_), channel_id=1, source_target_pairs={{16,0},{0,16},{17,1},{1,17},{18,2},{2,18},{19,3},{3,19},{20,4},{4,... | collective-permute-start | bytes 393224 | tf_op jit(solution)/shard_map/ppermute | solution.py:774
  28.7 0.0 collective-permute-done.8.refs_4_.refs_3_
  28.7 0.4 shard_map.102
  29.1 5.2 %collective-permute-done.7.refs_1_ = bf16[128,1024]{1,0:T(8,128)(2,1)S(1)} collective-permute-done((bf16[128,1024]{1,0:T(8,128)(2,1)S(1)}, bf16[128,1024]{1,0:T(8,128)(2,1)S(1)}, u32[]{:S(2)}, u32[]{:S(2)}) %collective-permute-start.7) | collective-permute-done | bytes 262176 | tf_op jit(solution)/shard_map/ppermute | solution.py:774
  34.4 6.3 %shard_map.101.refs_4_.refs_2_ = bf16[8,128,256]{2,1,0:T(8,128)(2,1)S(1)} custom-call(bf16[128,1024]{1,0:T(8,128)(2,1)S(1)} %shard_map.100.refs_0_, bf16[128,1024]{1,0:T(8,128)(2,1)S(1)} %collective-permute-done.7.refs_1_, f32[8,1024]{1,0:T(8,128)S(1)} %get-tuple-element.53.refs_2_, f32[8,1024]{1,0:T(8,128)S(1)} %get-tuple-element.54.refs_3_, ...), custom_call_target="tpu_custom_call" | custom-call | flops 8589934592 | bytes 1024 | tf_op jit(solution)/shard_map/pallas_call | solution.py:678
  40.6 0.7 %collective-permute-done.9.refs_1_ = bf16[10,128,128]{2,1,0:T(8,128)(2,1)S(1)} collective-permute-done((bf16[10,128,128]{2,1,0:T(8,128)(2,1)S(1)}, bf16[10,128,128]{2,1,0:T(8,128)(2,1)S(1)}, u32[]{:S(2)}, u32[]{:S(2)}) %collective-permute-start.9) | collective-permute-done | bytes 327712 | tf_op jit(solution)/shard_map/ppermute | solution.py:774
  41.4 1.6 %shard_map.103 = (bf16[128,8,512]{2,1,0:T(8,128)(2,1)}, f32[1024,128]{1,0:T(8,128)S(1)}) custom-call(bf16[10,128,128]{2,1,0:T(8,128)(2,1)S(1)} %get-tuple-element.56.refs_2_.refs_0_, bf16[10,128,128]{2,1,0:T(8,128)(2,1)S(1)} %collective-permute-done.9.refs_1_, bf16[9,256,256]{2,1,0:T(8,128)(2,1)S(1)} %get-tuple-element.57.refs_2_, ...), custom_call_target="tpu_custom_call" | custom-call | flops 2147483648 | bytes 1024 | tf_op jit(solution)/shard_map/pallas_call | solution.py:678
  43.0 0.6 %collective-permute-done.6.refs_1_ = bf16[4,128,128]{2,1,0:T(8,128)(2,1)S(1)} collective-permute-done((bf16[4,128,128]{2,1,0:T(8,128)(2,1)S(1)}, bf16[4,128,128]{2,1,0:T(8,128)(2,1)S(1)}, u32[]{:S(2)}, u32[]{:S(2)}) %collective-permute-start.6) | collective-permute-done | bytes 131104 | tf_op jit(solution)/shard_map/ppermute | solution.py:774
  43.7 1.0 %shard_map.104 = bf16[128,8,512]{2,1,0:T(8,128)(2,1)} custom-call(bf16[4,128,128]{2,1,0:T(8,128)(2,1)S(1)} %get-tuple-element.51.refs_3_.refs_0_, bf16[4,128,128]{2,1,0:T(8,128)(2,1)S(1)} %collective-permute-done.6.refs_1_, bf16[8,128,256]{2,1,0:T(8,128)(2,1)S(1)} %shard_map.101.refs_4_.refs_2_, ...), custom_call_target="tpu_custom_call", output_to_operand_aliasing={{}: (4, {})} | custom-call | flops 1073741824 | bytes 1024 | tf_op jit(solution)/shard_map/pallas_call | solution.py:678
  (3 shorter events, 0.0 us)
Async XLA Ops:
  2.2 7.2 %copy-start = (f32[128,8,512]{2,1,0:T(8,128)S(1)}, f32[128,8,512]{2,1,0:T(8,128)}, u32[]{:S(2)}) copy-start(f32[128,8,512]{2,1,0:T(8,128)} %param.9) | copy-start | bytes 6291460
  2.2 8.9 %collective-permute-start = (bf16[560,128]{1,0:T(8,128)(2,1)}, bf16[560,128]{1,0:T(8,128)(2,1)S(1)}, u32[]{:S(2)}, u32[]{:S(2)}) collective-permute-start(bf16[560,128]{1,0:T(8,128)(2,1)} %get-tuple-element.33), channel_id=1, source_target_pairs={{1,2},{2,1},{3,4},{4,3},{5,6},{6,5},{7,8},{8,7},{9,10},{10,9},{11,... | collective-permute-start | bytes 430088 | tf_op jit(solution)/shard_map/ppermute | solution.py:743
  7.7 3.4 %collective-permute-start.1 = (bf16[560,128]{1,0:T(8,128)(2,1)}, bf16[560,128]{1,0:T(8,128)(2,1)S(1)}, u32[]{:S(2)}, u32[]{:S(2)}) collective-permute-start(bf16[560,128]{1,0:T(8,128)(2,1)} %get-tuple-element.34), channel_id=1, source_target_pairs={{0,1},{1,0},{2,3},{3,2},{4,5},{5,4},{6,7},{7,6},{8,9},{9,8},{10,11... | collective-permute-start | bytes 430088 | tf_op jit(solution)/shard_map/ppermute | solution.py:742
  7.7 0.8 %copy-start.4 = (f32[16,512]{1,0:T(8,128)S(1)}, f32[16,512]{1,0:T(8,128)}, u32[]{:S(2)}) copy-start(f32[16,512]{1,0:T(8,128)} %get-tuple-element.35.small_ref) | copy-start | bytes 98308
  9.4 1.8 %copy-start.1 = (bf16[16,128]{1,0:T(8,128)(2,1)S(1)}, bf16[16,128]{1,0:T(8,128)(2,1)}, u32[]{:S(2)}) copy-start(bf16[16,128]{1,0:T(8,128)(2,1)} %get-tuple-element.46.refs_4_) | copy-start | bytes 12292
  11.2 4.1 %collective-permute-start.2 = (bf16[48,128]{1,0:T(8,128)(2,1)S(1)}, bf16[48,128]{1,0:T(8,128)(2,1)S(1)}, u32[]{:S(2)}, u32[]{:S(2)}) collective-permute-start(bf16[48,128]{1,0:T(8,128)(2,1)S(1)} %pad_maximum_fusion), channel_id=1, source_target_pairs={{16,0},{0,16},{17,1},{1,17},{18,2},{2,18},{19,3},{3,19},{20,4},{4,... | collective-permute-start | bytes 36872 | tf_op jit(solution)/shard_map/ppermute | solution.py:778
  12.8 12.3 %collective-permute-start.5 = (bf16[12,128,128]{2,1,0:T(8,128)(2,1)S(1)}, bf16[12,128,128]{2,1,0:T(8,128)(2,1)S(1)}, u32[]{:S(2)}, u32[]{:S(2)}) collective-permute-start(bf16[12,128,128]{2,1,0:T(8,128)(2,1)S(1)} %get-tuple-element.50.refs_0_), channel_id=1, source_target_pairs={{16,0},{0,16},{17,1},{1,17},{18,2},{2,18},{19,3},{3,19},{20,4},{4,... | collective-permute-start | bytes 1179656 | tf_op jit(solution)/shard_map/ppermute | solution.py:774
  13.3 1.1 %copy-start.5 = (s32[2048]{0:T(1024)S(1)}, s32[2048]{0:T(1024)}, u32[]{:S(2)}) copy-start(s32[2048]{0:T(1024)} %param.12) | copy-start | bytes 24580
  13.3 1.1 %copy-start.6 = (s32[2048]{0:T(1024)S(1)}, s32[2048]{0:T(1024)}, u32[]{:S(2)}) copy-start(s32[2048]{0:T(1024)} %param.13) | copy-start | bytes 24580
  16.3 6.6 %copy-start.2 = (f32[32768]{0:T(1024)S(1)}, f32[32768]{0:T(1024)}, u32[]{:S(2)}) copy-start(f32[32768]{0:T(1024)} %param.14) | copy-start | bytes 393220
  16.3 6.6 %copy-start.3 = (f32[32768]{0:T(1024)S(1)}, f32[32768]{0:T(1024)}, u32[]{:S(2)}) copy-start(f32[32768]{0:T(1024)} %param.15) | copy-start | bytes 393220
  16.3 8.7 %collective-permute-start.3 = (bf16[128,1024]{1,0:T(8,128)(2,1)S(1)}, bf16[128,1024]{1,0:T(8,128)(2,1)S(1)}, u32[]{:S(2)}, u32[]{:S(2)}) collective-permute-start(bf16[128,1024]{1,0:T(8,128)(2,1)S(1)} %shard_map.97.refs_8_), channel_id=1, source_target_pairs={{1,2},{2,1},{3,4},{4,3},{5,6},{6,5},{7,8},{8,7},{9,10},{10,9},{11,... | collective-permute-start | bytes 786440 | tf_op jit(solution)/shard_map/ppermute | solution.py:825
  21.4 7.4 %collective-permute-start.8 = (bf16[6,128,128]{2,1,0:T(8,128)(2,1)S(1)}, bf16[6,128,128]{2,1,0:T(8,128)(2,1)S(1)}, u32[]{:S(2)}, u32[]{:S(2)}) collective-permute-start(bf16[6,128,128]{2,1,0:T(8,128)(2,1)S(1)} %get-tuple-element.55.refs_1_.refs_2_), channel_id=1, source_target_pairs={{16,0},{0,16},{17,1},{1,17},{18,2},{2,18},{19,3},{3,19},{20,4},{4,... | collective-permute-start | bytes 589832 | tf_op jit(solution)/shard_map/ppermute | solution.py:774
  22.9 2.2 %collective-permute-start.4 = (bf16[128,1024]{1,0:T(8,128)(2,1)S(1)}, bf16[128,1024]{1,0:T(8,128)(2,1)S(1)}, u32[]{:S(2)}, u32[]{:S(2)}) collective-permute-start(bf16[128,1024]{1,0:T(8,128)(2,1)S(1)} %shard_map.99), channel_id=1, source_target_pairs={{0,1},{1,0},{2,3},{3,2},{4,5},{5,4},{6,7},{7,6},{8,9},{9,8},{10,11... | collective-permute-start | bytes 786440 | tf_op jit(solution)/shard_map/ppermute | solution.py:826
  25.1 9.2 %collective-permute-start.7 = (bf16[128,1024]{1,0:T(8,128)(2,1)S(1)}, bf16[128,1024]{1,0:T(8,128)(2,1)S(1)}, u32[]{:S(2)}, u32[]{:S(2)}) collective-permute-start(bf16[128,1024]{1,0:T(8,128)(2,1)S(1)} %shard_map.100.refs_0_), channel_id=1, source_target_pairs={{16,0},{0,16},{17,1},{1,17},{18,2},{2,18},{19,3},{3,19},{20,4},{4,... | collective-permute-start | bytes 786440 | tf_op jit(solution)/shard_map/ppermute | solution.py:774
  26.7 14.7 %collective-permute-start.9 = (bf16[10,128,128]{2,1,0:T(8,128)(2,1)S(1)}, bf16[10,128,128]{2,1,0:T(8,128)(2,1)S(1)}, u32[]{:S(2)}, u32[]{:S(2)}) collective-permute-start(bf16[10,128,128]{2,1,0:T(8,128)(2,1)S(1)} %get-tuple-element.56.refs_2_.refs_0_), channel_id=1, source_target_pairs={{16,0},{0,16},{17,1},{1,17},{18,2},{2,18},{19,3},{3,19},{20,4},{4,... | collective-permute-start | bytes 983048 | tf_op jit(solution)/shard_map/ppermute | solution.py:774
  27.2 16.4 %collective-permute-start.6 = (bf16[4,128,128]{2,1,0:T(8,128)(2,1)S(1)}, bf16[4,128,128]{2,1,0:T(8,128)(2,1)S(1)}, u32[]{:S(2)}, u32[]{:S(2)}) collective-permute-start(bf16[4,128,128]{2,1,0:T(8,128)(2,1)S(1)} %get-tuple-element.51.refs_3_.refs_0_), channel_id=1, source_target_pairs={{16,0},{0,16},{17,1},{1,17},{18,2},{2,18},{19,3},{3,19},{20,4},{4,... | collective-permute-start | bytes 393224 | tf_op jit(solution)/shard_map/ppermute | solution.py:774

commit v7 on v6

--- a/solution.py
+++ b/solution.py
@@ -48,6 +48,7 @@
 
 
 MESSAGE_EXTRA = 48
+LISTS = 48
 
 
 def pack_kernel(
@@ -194,8 +195,9 @@
 
 def middle_kernel(*refs, groups):
     field_refs = refs[:groups]
-    both_ref, middle_ref, kept_ref, edge_ref, edge_low_ref, fields, fields_low = refs[groups:]
-    early, members, _ = middle_ref.shape
+    both_ref, soon_ref, middle_ref, kept_ref, edge_ref, edge_low_ref, fields, fields_low = refs[groups:]
+    members = middle_ref.shape[1]
+    soon = (soon_ref.shape[0] - LISTS) // members
     levels = field_refs[0].shape[0] // members
     lane = iota((members, LANES), 1)
     for level in range(levels):
@@ -217,13 +219,16 @@
     result = dot(fields[...], both_ref[...])
     half = result.shape[1] // 2
     result = result[:, :half] + (result[:, half:] + dot(fields_low[...], both_ref[:, :half]))
+    soon_ref[soon * members :, :] = jnp.zeros((LISTS, LANES), BF16)
     for k in range((groups - 2) * levels):
         level, lane = k % levels, (k // levels) * LANES
         value = result[level * members : (level + 1) * members, lane : lane + LANES].astype(BF16)
-        if k < early:
-            middle_ref[k] = value
+        if k < soon:
+            soon_ref[k * members : (k + 1) * members, :] = value
+        elif k < soon + middle_ref.shape[0]:
+            middle_ref[k - soon] = value
         else:
-            kept_ref[k - early] = value
+            kept_ref[k - soon - middle_ref.shape[0]] = value
 
 
 def edge_kernel(
@@ -369,24 +374,27 @@
     )
 
 
-def whole(middle_ref, first_ref, next_ref, last_ref, levels):
-    runs = jnp.concatenate([ref[...] for ref in (middle_ref, first_ref, next_ref, last_ref)], axis=0)
+def whole(soon_ref, middle_ref, first_ref, next_ref, last_ref, levels):
+    soon = soon_ref[: soon_ref.shape[0] - LISTS, :].reshape(-1, *middle_ref.shape[1:])
+    rest = [ref[...] for ref in (middle_ref, first_ref, next_ref, last_ref)]
+    runs = jnp.concatenate([soon, *rest], axis=0)
     groups = [runs[k : k + levels].reshape(-1, LANES) for k in range(0, runs.shape[0], levels)]
     return joined([groups[-2], *groups[:-2], groups[-1]])
 
 
 def neighbour_kernel(*refs, others, blocks, levels, turn, given):
-    message_ref, cell_ref, level_ref = refs[4:7]
-    passed_refs = refs[7 : 7 + others]
+    message_ref, cell_ref, level_ref = refs[5:8]
+    passed_refs = refs[8 : 8 + others]
     out_ref, table = refs[-2:]
     half = message_ref.shape[0] - MESSAGE_EXTRA
     rows = message_rows(half)
     odd = is_odd_tile()
     obs = 16 * LANES
     make_table(cell_ref, level_ref, table)
-    field = whole(*refs[:4], levels)
+    field = whole(*refs[:5], levels)
     skip = jnp.where(odd, 0, 2 * obs) if turn == 0 else jnp.where(odd, 2 * obs, 0)
-    parts = [ref[16 * turn : 16 * turn + 16, :] for ref in passed_refs]
+    base = refs[0].shape[0] - LISTS + 16 * turn
+    parts = [ref[base : base + 16, :] for ref in passed_refs]
     if not given:
         parts = [message_ref[rows["list"] : rows["list"] + 16, :], *parts]
     index = joined([entries_of(part, blocks)[0] for part in parts])
@@ -396,14 +404,14 @@
         mine = blocks * LANES
         found = [found[:, k : k + mine] for k in range(0, found.shape[1], mine)]
         if given:
-            found = [refs[7 + others][...].astype(F32), *found]
+            found = [refs[8 + others][...].astype(F32), *found]
         found = in_order(found)
     out_ref[...] = found.astype(BF16)
 
 
 def own_kernel(*refs, others, blocks, levels, tiles):
-    lists_ref = refs[4]
-    other_refs = refs[5 : 5 + others]
+    lists_ref = refs[5]
+    other_refs = refs[6 : 6 + others]
     (
         cell_ref,
         level_ref,
@@ -413,11 +421,12 @@
         weight_ref,
         target_ref,
         table,
-    ) = refs[5 + others :]
+    ) = refs[6 + others :]
     obs = 16 * LANES
     make_table(cell_ref, level_ref, table)
-    field = whole(*refs[:4], levels)
-    parts = [lists_ref[...]] + [r[32:48, :] for r in other_refs]
+    field = whole(*refs[:5], levels)
+    base = refs[0].shape[0] - LISTS + 32
+    parts = [lists_ref[...]] + [r[base : base + 16, :] for r in other_refs]
     parts = [entries_of(part, blocks) for part in parts]
     index = in_order([index for index, _ in parts])
     weight = in_order([weight for _, weight in parts]).astype(F32)
@@ -595,15 +604,17 @@
 
 def prepare_kernel(*refs, others):
     count = others + 1
-    middles, firsts = [refs[k * count : (k + 1) * count] for k in range(2)]
-    moved_ref, mean_ref = refs[2 * count :]
-    slot = 0
+    soons, middles, firsts = [refs[k * count : (k + 1) * count] for k in range(3)]
+    moved_ref, mean_ref = refs[3 * count :]
+    members = middles[0].shape[1]
+    soon = (soons[0].shape[0] - LISTS) // members
+    runs = [[ref[k * members : (k + 1) * members, :] for ref in soons] for k in range(soon)]
     for piece in (middles, firsts):
-        for k in range(0, piece[0].shape[0], 2):
-            moved, mean = departures([[ref[k + j] for ref in piece] for j in range(2)])
-            moved_ref[slot] = moved
-            mean_ref[slot] = jnp.broadcast_to(mean, mean_ref.shape[1:])
-            slot += 1
+        runs += [[ref[k] for ref in piece] for k in range(piece[0].shape[0])]
+    for slot in range(len(runs) // 2):
+        moved, mean = departures(runs[2 * slot : 2 * slot + 2])
+        moved_ref[slot] = moved
+        mean_ref[slot] = jnp.broadcast_to(mean, mean_ref.shape[1:])
 
 
 def update_kernel(*refs, others):
@@ -742,8 +753,9 @@
     from_b = lax.ppermute(b, "tile", even_pairs)
     from_a = lax.ppermute(a, "tile", odd_pairs)
     flat_rows = members * levels
-    kept_levels = levels // 2
-    soon_levels = levels // 4
+    kept_levels = levels // 4
+    soon_sent = levels // 8
+    soon_levels = levels // 2
     last_levels = levels // 2
     both, part, second = call(
         operator_kernel,
@@ -755,10 +767,13 @@
         [small],
         cost=1,
     )
-    middle, kept, border, border_low = call(
+    soon, middle, kept, border, border_low = call(
         functools.partial(middle_kernel, groups=groups),
         [
-            jax.ShapeDtypeStruct(((groups - 2) * levels - kept_levels, members, LANES), BF16),
+            jax.ShapeDtypeStruct((soon_sent * members + LISTS, LANES), BF16),
+            jax.ShapeDtypeStruct(
+                ((groups - 2) * levels - soon_sent - kept_levels, members, LANES), BF16
+            ),
             jax.ShapeDtypeStruct((kept_levels, members, LANES), BF16),
             jax.ShapeDtypeStruct((2, flat_rows, 2 * LANES), BF16),
             jax.ShapeDtypeStruct((2, flat_rows, 2 * LANES), BF16),
@@ -768,14 +783,16 @@
         in_specs=[group_spec(flat_rows, group) for group in range(groups)] + [vmem()],
         cost=3,
     )
-    passed = jnp.concatenate([from_a[half + 32 :], from_b[half + 32 :], lists], axis=0)
 
     def swapped(value, sent):
         return [value] + [lax.ppermute(sent, "mem", turn) for turn in turns]
 
-    passed, sent = lax.optimization_barrier((passed, middle))
+    passed = jnp.concatenate([from_a[half + 32 :], from_b[half + 32 :], lists], axis=0)
+    soon = lax.dynamic_update_slice(soon, passed, (soon_sent * members, 0))
+    soon, sent = lax.optimization_barrier((soon, middle))
     middles = swapped(middle, sent)
-    passed = [lax.ppermute(passed, "mem", turn) for turn in turns]
+    soons = swapped(soon, soon)
+    passed = soons[1:]
     first, after, last = call(
         edge_kernel,
         [
@@ -792,7 +809,7 @@
         [pltpu.VMEM((2, flat_rows, 2 * LANES), BF16)],
         cost=2,
     )
-    pieces = [middle, first, after, last]
+    pieces = [soon, middle, first, after, last]
     cell = obs_cell.reshape(16, LANES)
     level = obs_level.reshape(16, LANES)
     reading = jax.ShapeDtypeStruct((members, entries), BF16)
@@ -842,7 +859,7 @@
         [table],
         cost=2,
     )
-    unused = middles[1:]
+    unused = []
     (readings,) = call(merge_kernel, [reading], [own, back_a], cost=2)
     (readings,) = call(
         merge_kernel,
@@ -855,7 +872,7 @@
     readings = swapped(readings, readings)
     afters = swapped(after, sent)
     lasts = swapped(last, sent_last)
-    unused = firsts[1:]
+    unused = [*middles[1:], *firsts[1:]]
     ensemble = members * sharers
     total = blocks * sharers
     square = pltpu.VMEM((total, LANES, LANES), F32)
@@ -877,14 +894,14 @@
     )
     rows = members * levels
     result = jax.ShapeDtypeStruct((members, levels, columns), BF16)
-    pairs = (middle.shape[0] + first.shape[0]) // 2
+    pairs = (soon_sent + middle.shape[0] + first.shape[0]) // 2
     moved, mean = call(
         functools.partial(prepare_kernel, others=others),
         [
             jax.ShapeDtypeStruct((pairs, ensemble, 2 * LANES), BF16),
             jax.ShapeDtypeStruct((pairs, 8, 2 * LANES), F32),
         ],
-        [*middles, *firsts],
+        [*soons, *middles, *firsts],
         cost=2,
     )
     inputs = [*afters, moved, mean, weights]

time: 45.1 us -> 44.7 us (level)
  waiting for transfers between devices: 6.94 us -> 5.97 us
    ppermute x5 -> x6, starting transfers between devices: 5.67 us -> 7.49 us  [swapped(): return [value] + [lax.ppermute(sent, 'mem', turn) for turn in turns]]
    ppermute x1 -> x0, starting transfers between devices: 1.56 us -> none  [shards(): passed = [lax.ppermute(passed, 'mem', turn) for turn in turns]]
    ppermute x5 -> x6, waiting for transfers between devices: 6.59 us -> 5.78 us  [swapped(): return [value] + [lax.ppermute(sent, 'mem', turn) for turn in turns]]
  transfers between devices with their start and end apart: 10 -> 10, of which waited for: 4 -> 3; matrix products, arithmetic and copies ran while one was open for 0% -> 0% of each run, Pallas kernels for 39% -> 39%
where the time goes in v7:
time: 44.7 us; the launch traced here: 44.4 us
  Pallas kernels  20.6 us (46%)
  starting transfers between devices  16.6 us (37%)
  waiting for transfers between devices  5.97 us (13%)
  local copies, waits for them, and re-layouts  0.79 us (2%)
    pallas_call x14, Pallas kernels, call(): pl.pallas_call(kernel, grid=(1,), out_shape=outs, in_specs=in_specs or [v...  20.6 us
    ppermute x6, starting transfers between devices, swapped(): return [value] + [lax.ppermute(sent, 'mem', turn) for turn in turns]  7.49 us
    ppermute x6, waiting for transfers between devices, swapped(): return [value] + [lax.ppermute(sent, 'mem', turn) for turn in turns]  5.78 us
    ppermute x1, starting transfers between devices, shards(): from_a = lax.ppermute(a, 'tile', odd_pairs)  5.51 us
    ppermute x1, starting transfers between devices, shards(): back_a = lax.ppermute(to_a, 'tile', odd_pairs)  3.63 us
  transfers between devices with their start and end apart: 10, of which 3 were waited for; matrix products, arithmetic and copies ran while one was open for 0% of the time, Pallas kernels for 39%

profile of v7, /device:TPU:0, one launch (start us, length us, event | category | flops | bytes accessed | tf_op | source)
XLA Modules:
  0.0 44.4 jit_solution(14755324015032991511)
XLA Ops:
  0.0 2.2 %shard_map.91 = (bf16[560,128]{1,0:T(8,128)(2,1)}, bf16[560,128]{1,0:T(8,128)(2,1)}, bf16[16,128]{1,0:T(8,128)(2,1)}, f32[16,512]{1,0:T(8,128)}) custom-call(f32[1024,512]{1,0:T(8,128)} %bitcast.5, f32[6,512]{1,0:T(8,128)} %coef_hbm.1, s32[6,512]{1,0:T(8,128)} %nbr_hbm.1, s32[4,1,128]{2,1,0:T(1,128)} %index_hbm.1, s32[4,1,128]{2,1,0:T(1,128)} %weight_hbm.1), custom_call_target="tpu_custom_call" | custom-call | bytes 1024 | tf_op jit(solution)/shard_map/pallas_call | solution.py:689
  2.2 0.0 copy-start
  2.2 5.5 %collective-permute-start = (bf16[560,128]{1,0:T(8,128)(2,1)}, bf16[560,128]{1,0:T(8,128)(2,1)S(1)}, u32[]{:S(2)}, u32[]{:S(2)}) collective-permute-start(bf16[560,128]{1,0:T(8,128)(2,1)} %get-tuple-element.34), channel_id=1, source_target_pairs={{1,2},{2,1},{3,4},{4,3},{5,6},{6,5},{7,8},{8,7},{9,10},{10,9},{11,... | collective-permute-start | bytes 430088 | tf_op jit(solution)/shard_map/ppermute | solution.py:754
  7.7 0.0 collective-permute-start.1
  7.7 0.0 copy-start.4
  7.7 0.8 %copy-done.4 = f32[16,512]{1,0:T(8,128)S(1)} copy-done((f32[16,512]{1,0:T(8,128)S(1)}, f32[16,512]{1,0:T(8,128)}, u32[]{:S(2)}) %copy-start.4) | copy-done | bytes 32792
  8.5 0.9 %shard_map.92 = (bf16[512,512]{1,0:T(8,128)(2,1)S(1)}, f32[2,256,128]{2,1,0:T(8,128)S(1)}, bf16[4,256,128]{2,1,0:T(8,128)(2,1)S(1)}) custom-call(f32[16,512]{1,0:T(8,128)S(1)} %copy-done.4), custom_call_target="tpu_custom_call" | custom-call | flops 1073741824 | bytes 1024 | tf_op jit(solution)/shard_map/pallas_call | solution.py:689
  9.4 0.0 copy-done
  9.4 0.0 copy-start.1
  9.4 1.8 %shard_map.93 = (bf16[176,128]{1,0:T(8,128)(2,1)S(1)}, bf16[13,128,128]{2,1,0:T(8,128)(2,1)S(1)}, bf16[2,128,128]{2,1,0:T(8,128)(2,1)S(1)}, bf16[2,1024,256]{2,1,0:T(8,128)(2,1)S(1)}, bf16[2,1024,256]{2,1,0:T(8,128)(2,1)S(1)}) custom-call(f32[1024,512]{1,0:T(8,128)S(1)} %bitcast.6, f32[1024,512]{1,0:T(8,128)S(1)} %bitcast.7, f32[1024,512]{1,0:T(8,128)S(1)} %bitcast.8, ...), custom_call_target="tpu_custom_call" | custom-call | flops 3221225472 | bytes 1024 | tf_op jit(solution)/shard_map/pallas_call | solution.py:689
  11.1 0.0 collective-permute-done.a_ref.refs_5_
  11.2 0.0 collective-permute-done.1.b_ref.refs_5_
  11.2 0.0 copy-done.1
  11.2 1.6 %collective-permute-start.2 = (bf16[176,128]{1,0:T(8,128)(2,1)S(1)}, bf16[176,128]{1,0:T(8,128)(2,1)S(1)}, u32[]{:S(2)}, u32[]{:S(2)}) collective-permute-start(bf16[176,128]{1,0:T(8,128)(2,1)S(1)} %maximum_dynamic-update-slice_fusion.refs_0_), channel_id=1, source_target_pairs={{16,0},{0,16},{17,1},{1,17},{18,2},{2,18},{19,3},{3,19},{20,4},{4,... | collective-permute-start | bytes 135176 | tf_op jit(solution)/shard_map/ppermute | solution.py:788
  12.8 0.5 %collective-permute-start.7 = (bf16[13,128,128]{2,1,0:T(8,128)(2,1)S(1)}, bf16[13,128,128]{2,1,0:T(8,128)(2,1)S(1)}, u32[]{:S(2)}, u32[]{:S(2)}) collective-permute-start(bf16[13,128,128]{2,1,0:T(8,128)(2,1)S(1)} %get-tuple-element.56.refs_1_.refs_2_), channel_id=1, source_target_pairs={{16,0},{0,16},{17,1},{1,17},{18,2},{2,18},{19,3},{3,19},{20,4},{4,... | collective-permute-start | bytes 1277960 | tf_op jit(solution)/shard_map/ppermute | solution.py:788
  13.3 0.0 copy-start.5
  13.3 0.0 copy-start.6
  13.3 1.1 %shard_map.94 = (bf16[6,128,128]{2,1,0:T(8,128)(2,1)S(1)}, bf16[8,128,128]{2,1,0:T(8,128)(2,1)S(1)}, bf16[4,128,128]{2,1,0:T(8,128)(2,1)S(1)}) custom-call(bf16[560,128]{1,0:T(8,128)(2,1)S(1)} %collective-permute-done.a_ref.refs_5_, bf16[560,128]{1,0:T(8,128)(2,1)S(1)} %collective-permute-done.1.b_ref.refs_5_, f32[16,512]{1,0:T(8,128)S(1)} %copy-done.4, ...), custom_call_target="tpu_custom_call" | custom-call | flops 2147483648 | bytes 1024 | tf_op jit(solution)/shard_map/pallas_call | solution.py:689
  14.4 0.0 copy-done.5
  14.4 0.0 copy-done.6
  14.4 0.9 %shard_map.96.refs_9_ = bf16[128,512]{1,0:T(8,128)(2,1)S(1)} custom-call(bf16[176,128]{1,0:T(8,128)(2,1)S(1)} %maximum_dynamic-update-slice_fusion.refs_0_, bf16[13,128,128]{2,1,0:T(8,128)(2,1)S(1)} %get-tuple-element.56.refs_1_.refs_2_, bf16[6,128,128]{2,1,0:T(8,128)(2,1)S(1)} %get-tuple-element.57.refs_2_.refs_4_, ...), custom_call_target="tpu_custom_call" | custom-call | flops 1073741824 | bytes 1024 | tf_op jit(solution)/shard_map/pallas_call | solution.py:689
  15.3 0.0 collective-permute-done.2.refs_6_.refs_8_.refs_1_
  15.4 1.0 %shard_map.97.refs_9_ = bf16[128,1024]{1,0:T(8,128)(2,1)S(1)} custom-call(bf16[176,128]{1,0:T(8,128)(2,1)S(1)} %maximum_dynamic-update-slice_fusion.refs_0_, bf16[13,128,128]{2,1,0:T(8,128)(2,1)S(1)} %get-tuple-element.56.refs_1_.refs_2_, bf16[6,128,128]{2,1,0:T(8,128)(2,1)S(1)} %get-tuple-element.57.refs_2_.refs_4_, ...), custom_call_target="tpu_custom_call" | custom-call | flops 1073741824 | bytes 1024 | tf_op jit(solution)/shard_map/pallas_call | solution.py:689
  16.3 0.0 copy-start.2
  16.3 0.0 copy-start.3
  16.4 3.6 %collective-permute-start.3 = (bf16[128,1024]{1,0:T(8,128)(2,1)S(1)}, bf16[128,1024]{1,0:T(8,128)(2,1)S(1)}, u32[]{:S(2)}, u32[]{:S(2)}) collective-permute-start(bf16[128,1024]{1,0:T(8,128)(2,1)S(1)} %shard_map.97.refs_9_), channel_id=1, source_target_pairs={{1,2},{2,1},{3,4},{4,3},{5,6},{6,5},{7,8},{8,7},{9,10},{10,9},{11,... | collective-permute-start | bytes 786440 | tf_op jit(solution)/shard_map/ppermute | solution.py:842
  20.0 1.5 %shard_map.99 = bf16[128,1024]{1,0:T(8,128)(2,1)S(1)} custom-call(bf16[176,128]{1,0:T(8,128)(2,1)S(1)} %maximum_dynamic-update-slice_fusion.refs_0_, bf16[13,128,128]{2,1,0:T(8,128)(2,1)S(1)} %get-tuple-element.56.refs_1_.refs_2_, bf16[6,128,128]{2,1,0:T(8,128)(2,1)S(1)} %get-tuple-element.57.refs_2_.refs_4_, ...), custom_call_target="tpu_custom_call" | custom-call | flops 2147483648 | bytes 1024 | tf_op jit(solution)/shard_map/pallas_call | solution.py:689
  21.5 1.6 %collective-permute-start.8 = (bf16[6,128,128]{2,1,0:T(8,128)(2,1)S(1)}, bf16[6,128,128]{2,1,0:T(8,128)(2,1)S(1)}, u32[]{:S(2)}, u32[]{:S(2)}) collective-permute-start(bf16[6,128,128]{2,1,0:T(8,128)(2,1)S(1)} %get-tuple-element.57.refs_2_.refs_4_), channel_id=1, source_target_pairs={{16,0},{0,16},{17,1},{1,17},{18,2},{2,18},{19,3},{3,19},{20,4},{4,... | collective-permute-start | bytes 589832 | tf_op jit(solution)/shard_map/ppermute | solution.py:788
  23.1 0.0 collective-permute-start.4
  23.1 0.0 copy-done.2
  23.1 0.0 copy-done.3
  23.1 1.7 %shard_map.95 = (bf16[128,1024]{1,0:T(8,128)(2,1)S(1)}, f32[8,1024]{1,0:T(8,128)S(1)}, f32[8,1024]{1,0:T(8,128)S(1)}) custom-call(bf16[176,128]{1,0:T(8,128)(2,1)S(1)} %maximum_dynamic-update-slice_fusion.refs_0_, bf16[13,128,128]{2,1,0:T(8,128)(2,1)S(1)} %get-tuple-element.56.refs_1_.refs_2_, bf16[6,128,128]{2,1,0:T(8,128)(2,1)S(1)} %get-tuple-element.57.refs_2_.refs_4_, ...), custom_call_target="tpu_custom_call" | custom-call | flops 2147483648 | bytes 1024 | tf_op jit(solution)/shard_map/pallas_call | solution.py:689
  24.8 0.2 collective-permute-done.3.other_ref
  25.0 0.1 shard_map.98.one_ref
  25.1 0.0 collective-permute-done.4.other_ref
  25.1 0.1 shard_map.100.refs_0_
  25.2 1.8 %collective-permute-start.6 = (bf16[128,1024]{1,0:T(8,128)(2,1)S(1)}, bf16[128,1024]{1,0:T(8,128)(2,1)S(1)}, u32[]{:S(2)}, u32[]{:S(2)}) collective-permute-start(bf16[128,1024]{1,0:T(8,128)(2,1)S(1)} %shard_map.100.refs_0_), channel_id=1, source_target_pairs={{16,0},{0,16},{17,1},{1,17},{18,2},{2,18},{19,3},{3,19},{20,4},{4,... | collective-permute-start | bytes 786440 | tf_op jit(solution)/shard_map/ppermute | solution.py:788
  27.0 0.3 collective-permute-start.9
  27.3 1.7 %collective-permute-start.5 = (bf16[4,128,128]{2,1,0:T(8,128)(2,1)S(1)}, bf16[4,128,128]{2,1,0:T(8,128)(2,1)S(1)}, u32[]{:S(2)}, u32[]{:S(2)}) collective-permute-start(bf16[4,128,128]{2,1,0:T(8,128)(2,1)S(1)} %get-tuple-element.52.refs_4_.refs_0_), channel_id=1, source_target_pairs={{16,0},{0,16},{17,1},{1,17},{18,2},{2,18},{19,3},{3,19},{20,4},{4,... | collective-permute-start | bytes 393224 | tf_op jit(solution)/shard_map/ppermute | solution.py:788
  29.0 0.6 %collective-permute-done.8.refs_5_ = bf16[6,128,128]{2,1,0:T(8,128)(2,1)S(1)} collective-permute-done((bf16[6,128,128]{2,1,0:T(8,128)(2,1)S(1)}, bf16[6,128,128]{2,1,0:T(8,128)(2,1)S(1)}, u32[]{:S(2)}, u32[]{:S(2)}) %collective-permute-start.8) | collective-permute-done | bytes 196640 | tf_op jit(solution)/shard_map/ppermute | solution.py:788
  29.6 0.0 collective-permute-done.7.refs_4_.refs_3_
  29.6 0.5 %shard_map.102 = (bf16[10,256,256]{2,1,0:T(8,128)(2,1)S(1)}, f32[10,8,256]{2,1,0:T(8,128)S(1)}) custom-call(bf16[176,128]{1,0:T(8,128)(2,1)S(1)} %maximum_dynamic-update-slice_fusion.refs_0_, bf16[176,128]{1,0:T(8,128)(2,1)S(1)} %collective-permute-done.2.refs_6_.refs_8_.refs_1_, bf16[13,128,128]{2,1,0:T(8,128)(2,1)S(1)} %get-tuple-element.56.refs_1_.refs_2_, ...), custom_call_target="tpu_custom_call" | custom-call | flops 2147483648 | bytes 1024 | tf_op jit(solution)/shard_map/pallas_call | solution.py:689
  30.1 5.2 %collective-permute-done.6.refs_1_ = bf16[128,1024]{1,0:T(8,128)(2,1)S(1)} collective-permute-done((bf16[128,1024]{1,0:T(8,128)(2,1)S(1)}, bf16[128,1024]{1,0:T(8,128)(2,1)S(1)}, u32[]{:S(2)}, u32[]{:S(2)}) %collective-permute-start.6) | collective-permute-done | bytes 262176 | tf_op jit(solution)/shard_map/ppermute | solution.py:788
  35.2 6.3 %shard_map.101.refs_4_.refs_2_ = bf16[8,128,256]{2,1,0:T(8,128)(2,1)S(1)} custom-call(bf16[128,1024]{1,0:T(8,128)(2,1)S(1)} %shard_map.100.refs_0_, bf16[128,1024]{1,0:T(8,128)(2,1)S(1)} %collective-permute-done.6.refs_1_, f32[8,1024]{1,0:T(8,128)S(1)} %get-tuple-element.54.refs_2_, f32[8,1024]{1,0:T(8,128)S(1)} %get-tuple-element.55.refs_3_, ...), custom_call_target="tpu_custom_call" | custom-call | flops 8589934592 | bytes 1024 | tf_op jit(solution)/shard_map/pallas_call | solution.py:689
  41.5 0.0 collective-permute-done.9.refs_1_
  41.5 1.6 %shard_map.103 = (bf16[128,8,512]{2,1,0:T(8,128)(2,1)}, f32[1024,128]{1,0:T(8,128)S(1)}) custom-call(bf16[8,128,128]{2,1,0:T(8,128)(2,1)S(1)} %get-tuple-element.58.refs_3_.refs_0_, bf16[8,128,128]{2,1,0:T(8,128)(2,1)S(1)} %collective-permute-done.9.refs_1_, bf16[10,256,256]{2,1,0:T(8,128)(2,1)S(1)} %get-tuple-element.59.refs_2_, ...), custom_call_target="tpu_custom_call" | custom-call | flops 2147483648 | bytes 1024 | tf_op jit(solution)/shard_map/pallas_call | solution.py:689
  43.2 0.0 collective-permute-done.5.refs_1_
  43.2 1.1 %shard_map.104 = bf16[128,8,512]{2,1,0:T(8,128)(2,1)} custom-call(bf16[4,128,128]{2,1,0:T(8,128)(2,1)S(1)} %get-tuple-element.52.refs_4_.refs_0_, bf16[4,128,128]{2,1,0:T(8,128)(2,1)S(1)} %collective-permute-done.5.refs_1_, bf16[8,128,256]{2,1,0:T(8,128)(2,1)S(1)} %shard_map.101.refs_4_.refs_2_, ...), custom_call_target="tpu_custom_call", output_to_operand_aliasing={{}: (4, {})} | custom-call | flops 1073741824 | bytes 1024 | tf_op jit(solution)/shard_map/pallas_call | solution.py:689
  (3 shorter events, 0.0 us)
Async XLA Ops:
  2.2 7.2 %copy-start = (f32[128,8,512]{2,1,0:T(8,128)S(1)}, f32[128,8,512]{2,1,0:T(8,128)}, u32[]{:S(2)}) copy-start(f32[128,8,512]{2,1,0:T(8,128)} %param.9) | copy-start | bytes 6291460
  2.2 8.9 %collective-permute-start = (bf16[560,128]{1,0:T(8,128)(2,1)}, bf16[560,128]{1,0:T(8,128)(2,1)S(1)}, u32[]{:S(2)}, u32[]{:S(2)}) collective-permute-start(bf16[560,128]{1,0:T(8,128)(2,1)} %get-tuple-element.34), channel_id=1, source_target_pairs={{1,2},{2,1},{3,4},{4,3},{5,6},{6,5},{7,8},{8,7},{9,10},{10,9},{11,... | collective-permute-start | bytes 430088 | tf_op jit(solution)/shard_map/ppermute | solution.py:754
  7.7 3.4 %collective-permute-start.1 = (bf16[560,128]{1,0:T(8,128)(2,1)}, bf16[560,128]{1,0:T(8,128)(2,1)S(1)}, u32[]{:S(2)}, u32[]{:S(2)}) collective-permute-start(bf16[560,128]{1,0:T(8,128)(2,1)} %get-tuple-element.35), channel_id=1, source_target_pairs={{0,1},{1,0},{2,3},{3,2},{4,5},{5,4},{6,7},{7,6},{8,9},{9,8},{10,11... | collective-permute-start | bytes 430088 | tf_op jit(solution)/shard_map/ppermute | solution.py:753
  7.7 0.8 %copy-start.4 = (f32[16,512]{1,0:T(8,128)S(1)}, f32[16,512]{1,0:T(8,128)}, u32[]{:S(2)}) copy-start(f32[16,512]{1,0:T(8,128)} %get-tuple-element.36.small_ref) | copy-start | bytes 98308
  9.4 1.8 %copy-start.1 = (bf16[16,128]{1,0:T(8,128)(2,1)S(1)}, bf16[16,128]{1,0:T(8,128)(2,1)}, u32[]{:S(2)}) copy-start(bf16[16,128]{1,0:T(8,128)(2,1)} %get-tuple-element.45.refs_5_) | copy-start | bytes 12292
  11.2 4.1 %collective-permute-start.2 = (bf16[176,128]{1,0:T(8,128)(2,1)S(1)}, bf16[176,128]{1,0:T(8,128)(2,1)S(1)}, u32[]{:S(2)}, u32[]{:S(2)}) collective-permute-start(bf16[176,128]{1,0:T(8,128)(2,1)S(1)} %maximum_dynamic-update-slice_fusion.refs_0_), channel_id=1, source_target_pairs={{16,0},{0,16},{17,1},{1,17},{18,2},{2,18},{19,3},{3,19},{20,4},{4,... | collective-permute-start | bytes 135176 | tf_op jit(solution)/shard_map/ppermute | solution.py:788
  12.8 16.9 %collective-permute-start.7 = (bf16[13,128,128]{2,1,0:T(8,128)(2,1)S(1)}, bf16[13,128,128]{2,1,0:T(8,128)(2,1)S(1)}, u32[]{:S(2)}, u32[]{:S(2)}) collective-permute-start(bf16[13,128,128]{2,1,0:T(8,128)(2,1)S(1)} %get-tuple-element.56.refs_1_.refs_2_), channel_id=1, source_target_pairs={{16,0},{0,16},{17,1},{1,17},{18,2},{2,18},{19,3},{3,19},{20,4},{4,... | collective-permute-start | bytes 1277960 | tf_op jit(solution)/shard_map/ppermute | solution.py:788
  13.3 1.1 %copy-start.5 = (s32[2048]{0:T(1024)S(1)}, s32[2048]{0:T(1024)}, u32[]{:S(2)}) copy-start(s32[2048]{0:T(1024)} %param.12) | copy-start | bytes 24580
  13.3 1.1 %copy-start.6 = (s32[2048]{0:T(1024)S(1)}, s32[2048]{0:T(1024)}, u32[]{:S(2)}) copy-start(s32[2048]{0:T(1024)} %param.13) | copy-start | bytes 24580
  16.3 6.8 %copy-start.2 = (f32[32768]{0:T(1024)S(1)}, f32[32768]{0:T(1024)}, u32[]{:S(2)}) copy-start(f32[32768]{0:T(1024)} %param.14) | copy-start | bytes 393220
  16.3 6.8 %copy-start.3 = (f32[32768]{0:T(1024)S(1)}, f32[32768]{0:T(1024)}, u32[]{:S(2)}) copy-start(f32[32768]{0:T(1024)} %param.15) | copy-start | bytes 393220
  16.4 8.7 %collective-permute-start.3 = (bf16[128,1024]{1,0:T(8,128)(2,1)S(1)}, bf16[128,1024]{1,0:T(8,128)(2,1)S(1)}, u32[]{:S(2)}, u32[]{:S(2)}) collective-permute-start(bf16[128,1024]{1,0:T(8,128)(2,1)S(1)} %shard_map.97.refs_9_), channel_id=1, source_target_pairs={{1,2},{2,1},{3,4},{4,3},{5,6},{6,5},{7,8},{8,7},{9,10},{10,9},{11,... | collective-permute-start | bytes 786440 | tf_op jit(solution)/shard_map/ppermute | solution.py:842
  21.5 8.1 %collective-permute-start.8 = (bf16[6,128,128]{2,1,0:T(8,128)(2,1)S(1)}, bf16[6,128,128]{2,1,0:T(8,128)(2,1)S(1)}, u32[]{:S(2)}, u32[]{:S(2)}) collective-permute-start(bf16[6,128,128]{2,1,0:T(8,128)(2,1)S(1)} %get-tuple-element.57.refs_2_.refs_4_), channel_id=1, source_target_pairs={{16,0},{0,16},{17,1},{1,17},{18,2},{2,18},{19,3},{3,19},{20,4},{4,... | collective-permute-start | bytes 589832 | tf_op jit(solution)/shard_map/ppermute | solution.py:788
  23.1 2.0 %collective-permute-start.4 = (bf16[128,1024]{1,0:T(8,128)(2,1)S(1)}, bf16[128,1024]{1,0:T(8,128)(2,1)S(1)}, u32[]{:S(2)}, u32[]{:S(2)}) collective-permute-start(bf16[128,1024]{1,0:T(8,128)(2,1)S(1)} %shard_map.99), channel_id=1, source_target_pairs={{0,1},{1,0},{2,3},{3,2},{4,5},{5,4},{6,7},{7,6},{8,9},{9,8},{10,11... | collective-permute-start | bytes 786440 | tf_op jit(solution)/shard_map/ppermute | solution.py:843
  25.2 10.1 %collective-permute-start.6 = (bf16[128,1024]{1,0:T(8,128)(2,1)S(1)}, bf16[128,1024]{1,0:T(8,128)(2,1)S(1)}, u32[]{:S(2)}, u32[]{:S(2)}) collective-permute-start(bf16[128,1024]{1,0:T(8,128)(2,1)S(1)} %shard_map.100.refs_0_), channel_id=1, source_target_pairs={{16,0},{0,16},{17,1},{1,17},{18,2},{2,18},{19,3},{3,19},{20,4},{4,... | collective-permute-start | bytes 786440 | tf_op jit(solution)/shard_map/ppermute | solution.py:788
  27.0 14.6 %collective-permute-start.9 = (bf16[8,128,128]{2,1,0:T(8,128)(2,1)S(1)}, bf16[8,128,128]{2,1,0:T(8,128)(2,1)S(1)}, u32[]{:S(2)}, u32[]{:S(2)}) collective-permute-start(bf16[8,128,128]{2,1,0:T(8,128)(2,1)S(1)} %get-tuple-element.58.refs_3_.refs_0_), channel_id=1, source_target_pairs={{16,0},{0,16},{17,1},{1,17},{18,2},{2,18},{19,3},{3,19},{20,4},{4,... | collective-permute-start | bytes 786440 | tf_op jit(solution)/shard_map/ppermute | solution.py:788
  27.3 15.9 %collective-permute-start.5 = (bf16[4,128,128]{2,1,0:T(8,128)(2,1)S(1)}, bf16[4,128,128]{2,1,0:T(8,128)(2,1)S(1)}, u32[]{:S(2)}, u32[]{:S(2)}) collective-permute-start(bf16[4,128,128]{2,1,0:T(8,128)(2,1)S(1)} %get-tuple-element.52.refs_4_.refs_0_), channel_id=1, source_target_pairs={{16,0},{0,16},{17,1},{1,17},{18,2},{2,18},{19,3},{3,19},{20,4},{4,... | collective-permute-start | bytes 393224 | tf_op jit(solution)/shard_map/ppermute | solution.py:788
